TPU v7x, 256 devices: a whole 4x4x8 slice. The times are simulated.
256 devices in a mesh: row: 16 (over y, z_hi, core), col: 16 (over x, z_lo).
Axes of the slice: x: 4, y: 4, z: 8 (z_hi: 2, z_lo: 4; z = z_hi * 4 + z_lo), core: 2. Of those that a mesh axis runs over, the one named last changes fastest.
Arguments:
- features: bfloat16 [32768, 1536], P(('row', 'col')), may hold values from -8 to 8
- targets: float32 [32768], P(('row', 'col')), may hold values from -6 to 6
- tile_pairs: int32 [16, 16, 32, 2], P('row', 'col'), may hold values from 0 to 15, as said below
- tile_count: int32 [16, 16], P('row', 'col'), may hold values from 1 to 32, as said below
Outputs:
- solution: float32 [32768], P(('row', 'col'))
- residual: float32 [32768], P(('row', 'col'))
Inputs may be any that keep to these rules, and one draw needn't show every extreme that they name: `tile_pairs`: for each device the first tile_count slots name distinct local block pairs whose row block i is at most its column block j; over all devices each such pair is listed at most once; the first entry is below the number of devices along col, the second below the number along row; later slots hold any such numbers and are not used. `tile_count`: the device at row index 0 and the last col index always lists 32 tiles.
All inputs are finite; a program needn't handle non-finite values.
Results may differ from a plain program's by a relative error of at most 0.0003.
Values may be sent and summed in bfloat16 or wider, within the bound.
No kernel may reach another device: no remote copies, remote signals or barrier semaphores. Data moves between devices by JAX's collectives and lax.ppermute only.
A program may use at most 64 MiB of HBM per device.

v0:
```python
import jax
import jax.numpy as jnp
from jax import lax
from jax.sharding import PartitionSpec as P

ITERS = 2


RIDGE = 1.0
GROUP = 4


def block_norms(gathered, count):
    blocks = gathered.reshape(count, -1, gathered.shape[-1])
    norms = jnp.einsum("cid,cid->ci", blocks, blocks, preferred_element_type=jnp.float32)
    return (blocks, norms)


def sweep(fetched, row_dirs, col_dirs, row_pick, col_pick, live, other, want_degree, width):
    row_blocks, col_blocks, row_norms, col_norms = fetched
    block = row_blocks.shape[1]
    row_span = row_blocks.shape[0]
    col_span = col_blocks.shape[0]
    turns = row_pick.shape[0] // GROUP

    def advance(counter, carry):
        start = counter * GROUP
        take_row = lax.dynamic_slice_in_dim(row_pick, start, GROUP)
        take_col = lax.dynamic_slice_in_dim(col_pick, start, GROUP)
        live_now = lax.dynamic_slice_in_dim(live, start, GROUP)
        other_now = lax.dynamic_slice_in_dim(other, start, GROUP)
        inner = jnp.einsum(
            "gid,gjd->gij",
            row_blocks[take_row],
            col_blocks[take_col],
            preferred_element_type=jnp.float32,
        )
        distance = row_norms[take_row][:, :, None] + col_norms[take_col][:, None, :] - 2.0 * inner
        kernel = jnp.exp(-jnp.maximum(distance, 0.0) / width)
        row_term = (
            jnp.einsum("gij,gj->gi", kernel, col_dirs[take_col], precision=lax.Precision.HIGHEST)
            * live_now[:, None]
        )
        col_term = (
            jnp.einsum("gij,gi->gj", kernel, row_dirs[take_row], precision=lax.Precision.HIGHEST)
            * other_now[:, None]
        )
        row_onehot = (take_row[:, None] == jnp.arange(row_span, dtype=jnp.int32)[None, :]).astype(
            jnp.float32
        )
        col_onehot = (take_col[:, None] == jnp.arange(col_span, dtype=jnp.int32)[None, :]).astype(
            jnp.float32
        )
        row_acc = carry[0] + jnp.einsum(
            "gc,gi->ci", row_onehot, row_term, precision=lax.Precision.HIGHEST
        )
        col_acc = carry[1] + jnp.einsum(
            "gc,gi->ci", col_onehot, col_term, precision=lax.Precision.HIGHEST
        )
        if want_degree:
            row_deg = carry[2] + jnp.einsum(
                "gc,gi->ci",
                row_onehot,
                jnp.sum(kernel, axis=2) * live_now[:, None],
                precision=lax.Precision.HIGHEST,
            )
            col_deg = carry[3] + jnp.einsum(
                "gc,gi->ci",
                col_onehot,
                jnp.sum(kernel, axis=1) * other_now[:, None],
                precision=lax.Precision.HIGHEST,
            )
            return (row_acc, col_acc, row_deg, col_deg)
        return (row_acc, col_acc)

    row_zero = jnp.zeros((row_span, block), jnp.float32)
    col_zero = jnp.zeros((col_span, block), jnp.float32)
    if want_degree:
        start_carry = (row_zero, col_zero, row_zero, col_zero)
    else:
        start_carry = (row_zero, col_zero)
    return lax.fori_loop(0, turns, advance, start_carry)


def body(features, targets, tile_pairs, tile_count):
    row_count = lax.axis_size("row")
    col_count = lax.axis_size("col")
    row_index = lax.axis_index("row")
    col_index = lax.axis_index("col")
    pairs = tile_pairs[0, 0]
    listed = tile_count[0, 0]
    slots = pairs.shape[0]
    block = features.shape[0]
    width = features.shape[1]
    row_pick = pairs[:, 0]
    col_pick = pairs[:, 1]
    live = (jnp.arange(slots, dtype=jnp.int32) < listed).astype(jnp.float32)
    same_block = row_index * col_count + row_pick == col_pick * col_count + col_index
    other = live * (1.0 - same_block.astype(jnp.float32))
    kept_rows = block_norms(lax.all_gather(features, "col", axis=0, tiled=True), col_count)
    kept_cols = block_norms(lax.all_gather(features, "row", axis=0, tiled=True), row_count)
    whole = (kept_rows[0], kept_cols[0], kept_rows[1], kept_cols[1])

    def apply_kernel(vector, fetched, want_degree):
        row_dirs = lax.all_gather(vector, "col", axis=0, tiled=True).reshape(col_count, block)
        col_dirs = lax.all_gather(vector, "row", axis=0, tiled=True).reshape(row_count, block)
        return sweep(
            fetched, row_dirs, col_dirs, row_pick, col_pick, live, other, want_degree, width
        )

    def squares(vector):
        return lax.psum(jnp.sum(vector * vector), ("row", "col"))

    solution = jnp.zeros_like(targets)
    residual = targets
    direction = targets
    norm_now = squares(residual)
    degree = jnp.zeros_like(targets)
    for counter in range(ITERS):
        if counter == 0:
            first_row_acc, first_col_acc, row_deg, col_deg = apply_kernel(direction, whole, True)
            first_row_sum = lax.psum_scatter(
                first_row_acc.reshape(-1), "col", scatter_dimension=0, tiled=True
            )
            row_degree = lax.psum_scatter(
                row_deg.reshape(-1), "col", scatter_dimension=0, tiled=True
            )
            first_col_sum = lax.psum_scatter(
                first_col_acc.reshape(-1), "row", scatter_dimension=0, tiled=True
            )
            col_degree = lax.psum_scatter(
                col_deg.reshape(-1), "row", scatter_dimension=0, tiled=True
            )
            first_degree = row_degree + col_degree
            image = (
                RIDGE * direction
                + (first_degree * direction + first_row_sum + first_col_sum) / block
            )
            degree = first_degree
        else:
            row_acc, col_acc = apply_kernel(direction, whole, False)
            row_sum = lax.psum_scatter(row_acc.reshape(-1), "col", scatter_dimension=0, tiled=True)
            col_sum = lax.psum_scatter(col_acc.reshape(-1), "row", scatter_dimension=0, tiled=True)
            image = RIDGE * direction + (degree * direction + row_sum + col_sum) / block
        alpha = norm_now / lax.psum(jnp.sum(direction * image), ("row", "col"))
        solution = solution + alpha * direction
        residual = residual - alpha * image
        norm_next = squares(residual)
        direction = residual + norm_next / norm_now * direction
        norm_now = norm_next
    return (solution, residual)


def solution(mesh):
    return jax.shard_map(
        body,
        mesh=mesh,
        in_specs=(
            P(("row", "col"), None),
            P(("row", "col")),
            P("row", "col", None, None),
            P("row", "col"),
        ),
        out_specs=(P(("row", "col")), P(("row", "col"))),
        check_vma=False,
    )
```

profile of v0, /device:TPU:1, one launch (start us, length us, event | category | flops | bytes accessed | tf_op | source)
XLA Modules:
  0.0 979.6 jit_solution(4322291067065258880)
XLA Ops:
  13.3 34.9 %all-gather = f32[16,1,128]{2,1,0:T(1,128)S(1)} all-gather(f32[1,1,128]{2,1,0:T(1,128)} %bitcast.116), channel_id=1, replica_groups=mesh['row'=16,'col'=16] {'row'}, dimensions={0}, use_global_device_ids=true | all-gather | bytes 8704 | tf_op jit(solution)/shard_map/all_gather | solution.py:106
  48.2 38.5 %all-gather.1 = f32[16,1,128]{2,1,0:T(1,128)S(1)} all-gather(f32[1,1,128]{2,1,0:T(1,128)} %bitcast.117), channel_id=1, replica_groups=mesh['row'=16,'col'=16] {'col'}, dimensions={0}, use_global_device_ids=true | all-gather | bytes 8704 | tf_op jit(solution)/shard_map/all_gather | solution.py:105
  88.2 19.9 %all-gather.9.cloned.1.call-done = bf16[2048,1536]{1,0:T(8,128)(2,1)} async-done(((bf16[128,1536]{1,0:T(8,128)(2,1)}), bf16[2048,1536]{1,0:T(8,128)(2,1)}) %all-gather.9.cloned.1.call-update) | async-done | bytes 6291472 | tf_op jit(solution)/shard_map/all_gather | solution.py:101
  108.1 4.1 fusion.28
  112.2 136.0 %all-gather.7.cloned.1.call-done = bf16[2048,1536]{1,0:T(8,128)(2,1)} async-done(((bf16[128,1536]{1,0:T(8,128)(2,1)}), bf16[2048,1536]{1,0:T(8,128)(2,1)}) %all-gather.7.cloned.1.call-update) | async-done | bytes 6291472 | tf_op jit(solution)/shard_map/all_gather | solution.py:100
  248.1 4.1 fusion.29
  252.2 95.7 %while.36 = (s32[]{:T(128)}, f32[16,128]{1,0:T(8,128)S(1)}, f32[16,128]{1,0:T(8,128)S(1)}, f32[16,128]{1,0:T(8,128)S(1)}, f32[16,128]{1,0:T(8,128)S(1)}, /*index...) while((s32[]{:T(128)}, f32[16,128]{1,0:T(8,128)S(1)}, ...), condition=%wide.region_5.0_spmd.clone, body=%wide.region_2.0_spmd.clone.sunk | while | flops 203836704 | bytes 10338964 | solution.py:82
  252.3 3.4 gather_fusion
  264.3 3.4 gather_fusion
  276.2 3.4 gather_fusion
  288.2 3.4 gather_fusion
  300.2 3.4 gather_fusion
  312.1 3.4 gather_fusion
  324.1 3.4 gather_fusion
  336.1 3.4 gather_fusion
  347.9 61.2 %all-reduce.7 = (f32[2048]{0:T(1024)S(1)}, f32[2048]{0:T(1024)S(1)}) all-reduce(f32[2048]{0:T(1024)S(1)} %bitcast.122, f32[2048]{0:T(1024)S(1)} %bitcast.124), channel_id=4, replica_groups=mesh['row'=16,'col'=16] {'col'}, use_global_device_ids=true, to_apply=%region_8.0.clone | all-reduce | flops 4096 | bytes 32768
  409.1 91.4 %all-reduce.8 = (f32[2048]{0:T(1024)S(1)}, f32[2048]{0:T(1024)S(1)}) all-reduce(f32[2048]{0:T(1024)S(1)} %bitcast.123, f32[2048]{0:T(1024)S(1)} %bitcast.125), channel_id=5, replica_groups=mesh['row'=16,'col'=16] {'row'}, use_global_device_ids=true, to_apply=%region_9.0.clone | all-reduce | flops 4096 | bytes 32768
  501.1 78.8 %all-reduce.6 = (f32[]{:T(128)}, f32[]{:T(128)}) all-reduce(f32[]{:T(128)} %get-tuple-element.563, f32[]{:T(128)} %get-tuple-element.562), channel_id=1, replica_groups=mesh['row'=16,'col'=16] {'row','col'}, use_global_device_ids=true, to_apply=%region_1.0 | all-reduce | flops 2 | bytes 16 | tf_op jit(solution)/shard_map/psum | solution.py:112
  581.9 74.5 %psum.30 = f32[]{:T(128)} all-reduce(f32[]{:T(128)} %get-tuple-element.636), channel_id=1, replica_groups=mesh['row'=16,'col'=16] {'row','col'}, use_global_device_ids=true, to_apply=%region_13.0 | all-reduce | flops 1 | bytes 8 | tf_op jit(solution)/shard_map/psum | solution.py:112
  657.7 28.5 %all-gather.2 = f32[16,1,128]{2,1,0:T(1,128)S(1)} all-gather(f32[1,1,128]{2,1,0:T(1,128)S(1)} %bitcast.118), channel_id=1, replica_groups=mesh['row'=16,'col'=16] {'row'}, dimensions={0}, use_global_device_ids=true | all-gather | bytes 8704 | tf_op jit(solution)/shard_map/all_gather | solution.py:106
  686.1 31.3 %all-gather.3 = f32[16,1,128]{2,1,0:T(1,128)S(1)} all-gather(f32[1,1,128]{2,1,0:T(1,128)S(1)} %bitcast.119), channel_id=1, replica_groups=mesh['row'=16,'col'=16] {'col'}, dimensions={0}, use_global_device_ids=true | all-gather | bytes 8704 | tf_op jit(solution)/shard_map/all_gather | solution.py:105
  717.5 90.8 %while.37 = (s32[]{:T(128)}, f32[16,128]{1,0:T(8,128)S(1)}, f32[16,128]{1,0:T(8,128)S(1)}, s32[32]{0:T(128)S(1)}, f32[16,128]{1,0:T(8,128)S(1)}, /*index=5*/s32[...) while((s32[]{:T(128)}, f32[16,128]{1,0:T(8,128)S(1)}, ...), condition=%wide.region_15.0_spmd.clone, body=%wide.region_14.0_spmd.clone.sunk | while | flops 203500704 | bytes 10297922 | solution.py:82
  728.9 3.4 gather_fusion.6
  740.3 3.4 gather_fusion.6
  751.6 3.4 gather_fusion.6
  763.0 3.4 gather_fusion.6
  774.3 3.4 gather_fusion.6
  785.7 3.4 gather_fusion.6
  797.0 3.4 gather_fusion.6
  808.3 32.1 %all-reduce.4 = f32[2048]{0:T(1024)S(1)} all-reduce(f32[2048]{0:T(1024)S(1)} %bitcast.120), channel_id=6, replica_groups=mesh['row'=16,'col'=16] {'col'}, use_global_device_ids=true, to_apply=%region_16.0.clone | all-reduce | flops 2048 | bytes 16384
  840.4 56.7 %all-reduce.5 = f32[2048]{0:T(1024)S(1)} all-reduce(f32[2048]{0:T(1024)S(1)} %bitcast.121), channel_id=7, replica_groups=mesh['row'=16,'col'=16] {'row'}, use_global_device_ids=true, to_apply=%region_17.0.clone | all-reduce | flops 2048 | bytes 16384
  897.8 73.1 %psum.31 = f32[]{:T(128)} all-reduce(f32[]{:T(128)} %get-tuple-element.634), channel_id=1, replica_groups=mesh['row'=16,'col'=16] {'row','col'}, use_global_device_ids=true, to_apply=%region_19.0 | all-reduce | flops 1 | bytes 8 | tf_op jit(solution)/shard_map/psum | solution.py:145
  (279 shorter events, 142.5 us)
Async XLA Ops:
  7.2 100.9 %all-gather.9.cloned.1.call-start = ((), (), s32[]{:S(2)}) async-start(), calls=%async_computation.1 | async-start | bytes 6684672 | tf_op jit(solution)/shard_map/all_gather | solution.py:101
  7.9 240.2 %all-gather.7.cloned.1.call-start = ((), (), s32[]{:S(2)}) async-start(), calls=%async_computation | async-start | bytes 6684672 | tf_op jit(solution)/shard_map/all_gather | solution.py:100
  252.2 248.2 %copy-start = (f32[128]{0:T(128)S(1)}, f32[128]{0:T(128)}, u32[]{:S(2)}) copy-start(f32[128]{0:T(128)} %param.9) | copy-start | bytes 1540
Sparse Core Ops, SparseCore 0:
  10.7 97.3 all-gather.8
  109.9 138.2 all-gather.6
where the time goes:
time: 981 us; the launch traced here: 980 us
  blocking collectives  601 us (61%)
  waiting for transfers between devices  157 us (16%)
  local copies, waits for them, and re-layouts  152 us (15%)
  matrix products  35.8 us (4%)
  between operations  20.1 us (2%)
  other arithmetic  13.2 us (1%)
    unnamed x4, blocking collectives  241 us
    psum x2, blocking collectives, squares(): return lax.psum(jnp.sum(vector * vector), ('row', 'col'))  153 us
    all_gather x1, waiting for transfers between devices, body(): lax.all_gather(features, 'col', axis=0, tiled=True)  136 us
    psum x1, blocking collectives, body(): alpha = norm_now / lax.psum(jnp.sum(direction * image), ('row', 'col'))  73.1 us
    all_gather x2, blocking collectives, apply_kernel(): lax.all_gather(vector, 'col', axis=0, tiled=True).reshape(col_count, block)  69.8 us
    all_gather x2, blocking collectives, apply_kernel(): lax.all_gather(vector, 'row', axis=0, tiled=True).reshape(row_count, block)  63.3 us
    gather x16, local copies, waits for them, and re-layouts, advance(): row_blocks[take_row]  55 us
    gather x16, local copies, waits for them, and re-layouts, advance(): col_blocks[take_col]  54.9 us
  transfers between devices with their start and end apart: 2, of which 2 were waited for; matrix products, arithmetic and copies ran while one was open for 1% of the time, Pallas kernels for 0%

commit v1 on v0

v1 whole, which is shorter than its diff:
```python
import jax
import jax.numpy as jnp
from jax import lax
from jax.experimental import pallas as pl
from jax.experimental.pallas import tpu as pltpu
from jax.sharding import PartitionSpec as P

RIDGE = 1.0
GROUP = 4
AXES = ("row", "col")
LANES = 128
VMEM_BYTES = 40 * 1024 * 1024


def spread_columns(values, out_ref):
    turned = jnp.transpose(values)
    for k in range(values.shape[0]):
        out_ref[k] = jnp.broadcast_to(turned[:, k : k + 1], (LANES, LANES))


def write_slots(row_acc, col_acc, row_index, col_index, n_row, n_col, out_ref):
    out_ref[...] = jnp.zeros_like(out_ref)
    lane = lax.broadcasted_iota(jnp.int32, (LANES, LANES), 1)
    packed = jnp.zeros((LANES, LANES), jnp.float32)
    for a in range(n_col):
        column = jnp.sum(row_acc[a], axis=1, keepdims=True)
        packed = packed + jnp.where(lane == a, column, 0.0)
    first = pl.multiple_of(row_index * n_col, n_col)
    out_ref[pl.ds(first, n_col), :] = jnp.transpose(packed)[0:n_col, :]
    for b in range(n_row):
        at = pl.ds(b * n_col + col_index, 1)
        out_ref[at, :] = out_ref[at, :] + jnp.sum(col_acc[b], axis=0, keepdims=True)


def add_tile(kernel, slot, vec_ref, spread_ref, row_acc, col_acc, where, pairs, listed, n_col):
    row_index, col_index = where
    a = pairs[slot, 0]
    b = pairs[slot, 1]
    j = b * n_col + col_index
    live = jnp.where(slot < listed, 1.0, 0.0)
    other = jnp.where(row_index * n_col + a == j, 0.0, live)
    both = kernel * (spread_ref[a] + vec_ref[pl.ds(j, 1), :])
    row_acc[a] = row_acc[a] + both * live
    col_acc[b] = col_acc[b] + jnp.sum(both.reshape(16, 8, LANES), axis=0) * other


def first_sweep_kernel(
    place, pairs, count, rows_ref, cols_ref, known_ref, kernel_ref, out_ref,
    vec, norms, spread_v, spread_n, row_acc, col_acc,
):
    n_col = rows_ref.shape[0]
    n_row = cols_ref.shape[0]
    width = rows_ref.shape[2]
    row_index = place[0]
    col_index = place[1]
    listed = count[0]
    first = pl.multiple_of(row_index * n_col, n_col)
    vec[...] = known_ref[:, 0:LANES]
    norms[...] = known_ref[:, LANES : 2 * LANES]
    spread_columns(vec[pl.ds(first, n_col), :], spread_v)
    spread_columns(norms[pl.ds(first, n_col), :], spread_n)
    row_acc[...] = jnp.zeros_like(row_acc)
    col_acc[...] = jnp.zeros_like(col_acc)

    def step(turn, carry):
        for g in range(GROUP):
            slot = turn * GROUP + g
            a = pairs[slot, 0]
            b = pairs[slot, 1]
            inner = lax.dot_general(
                rows_ref[a], cols_ref[b], (((1,), (1,)), ((), ())),
                preferred_element_type=jnp.float32,
            )
            norm_j = norms[pl.ds(b * n_col + col_index, 1), :]
            distance = spread_n[a] + norm_j - 2.0 * inner
            kernel = jnp.exp(jnp.maximum(distance, 0.0) * (-1.0 / width))
            kernel_ref[slot] = kernel
            add_tile(
                kernel, slot, vec, spread_v, row_acc, col_acc,
                (row_index, col_index), pairs, listed, n_col,
            )
        return carry

    lax.fori_loop(0, pairs.shape[0] // GROUP, step, 0)
    write_slots(row_acc, col_acc, row_index, col_index, n_row, n_col, out_ref)


def second_sweep_kernel(
    place, pairs, count, kernel_ref, start_ref, image_ref, out_ref, own_ref,
    next_dir, sums, spread_v, row_acc, col_acc, *, n_row, n_col,
):
    row_index = place[0]
    col_index = place[1]
    listed = count[0]
    start = start_ref[...]
    image = image_ref[...]
    norm_0 = jnp.sum(start * start)
    alpha = norm_0 / jnp.sum(start * image)
    residual = start - alpha * image
    norm_1 = jnp.sum(residual * residual)
    direction = residual + (norm_1 / norm_0) * start
    next_dir[...] = direction
    first = pl.multiple_of(row_index * n_col, n_col)
    spread_columns(next_dir[pl.ds(first, n_col), :], spread_v)
    row_acc[...] = jnp.zeros_like(row_acc)
    col_acc[...] = jnp.zeros_like(col_acc)

    def step(turn, carry):
        for g in range(GROUP):
            slot = turn * GROUP + g
            add_tile(
                kernel_ref[slot], slot, next_dir, spread_v, row_acc, col_acc,
                (row_index, col_index), pairs, listed, n_col,
            )
        return carry

    lax.fori_loop(0, pairs.shape[0] // GROUP, step, 0)
    write_slots(row_acc, col_acc, row_index, col_index, n_row, n_col, sums)
    partial = jnp.sum(sums[...] * next_dir[...])
    out_ref[:, 0:LANES] = sums[...]
    out_ref[:, LANES : 2 * LANES] = jnp.full((n_row * n_col, LANES), partial, jnp.float32)
    mine = pl.ds(row_index * n_col + col_index, 1)
    own_start = start_ref[mine, :]
    own_dir = next_dir[mine, :]
    own_ref[0:1, :] = alpha * own_start
    own_ref[1:2, :] = own_start - alpha * image_ref[mine, :]
    own_ref[2:3, :] = own_dir
    own_ref[3:4, :] = jnp.full((1, LANES), norm_1, jnp.float32)
    own_ref[4:5, :] = jnp.full((1, LANES), jnp.sum(direction * direction), jnp.float32)
    own_ref[5:8, :] = jnp.zeros((3, LANES), jnp.float32)


def image_kernel(place, partial_ref, own_ref, out_ref, *, block):
    total = jnp.sum(partial_ref[...], axis=0, keepdims=True)
    image = RIDGE * own_ref[...] + total * (1.0 / block)
    out_ref[...] = jnp.broadcast_to(image, out_ref.shape)


def finish_kernel(partial_ref, own_ref, solution_ref, residual_ref, *, block):
    total = jnp.sum(partial_ref[...], axis=0, keepdims=True)
    direction = own_ref[2:3, :]
    image = RIDGE * direction + total[:, 0:LANES] * (1.0 / block)
    against = RIDGE * own_ref[4:5, :] + total[:, LANES : 2 * LANES] * (1.0 / block)
    alpha = own_ref[3:4, :] / against
    solution_ref[...] = own_ref[0:1, :] + alpha * direction
    residual_ref[...] = own_ref[1:2, :] - alpha * image


def swap(slots):
    return lax.all_to_all(slots, AXES, 0, 0, tiled=True)


VM = pl.BlockSpec(memory_space=pltpu.VMEM)
SM = pl.BlockSpec(memory_space=pltpu.SMEM)


def body(features, targets, tile_pairs, tile_count):
    n_row = lax.axis_size("row")
    n_col = lax.axis_size("col")
    total = n_row * n_col
    place = jnp.stack([lax.axis_index("row"), lax.axis_index("col")]).astype(jnp.int32)
    pairs = tile_pairs[0, 0]
    count = tile_count[0]
    slots = pairs.shape[0]
    block, width = features.shape
    params = pltpu.CompilerParams(vmem_limit_bytes=VMEM_BYTES)
    f32 = jnp.float32

    wide = features.astype(f32)
    norms = jnp.sum(wide * wide, axis=1)
    mine = jnp.concatenate([targets, norms])[None, :]
    known = swap(jnp.broadcast_to(mine, (total, 2 * block)))

    rows = lax.all_gather(features, "col", axis=0).reshape(n_col, block, width)
    cols = lax.all_gather(features, "row", axis=0).reshape(n_row, block, width)

    accumulators = [
        pltpu.VMEM((n_col, block, block), f32),
        pltpu.VMEM((n_row, 8, block), f32),
    ]
    kernel, partial = pl.pallas_call(
        first_sweep_kernel,
        out_shape=(
            jax.ShapeDtypeStruct((slots, block, block), f32),
            jax.ShapeDtypeStruct((total, block), f32),
        ),
        in_specs=[SM, SM, SM, VM, VM, VM],
        out_specs=(VM, VM),
        scratch_shapes=[pltpu.VMEM((total, block), f32)] * 2
        + [pltpu.VMEM((n_col, block, block), f32)] * 2 + accumulators,
        compiler_params=params,
    )(place, pairs, count, rows, cols, known)

    image = pl.pallas_call(
        lambda *refs: image_kernel(None, *refs, block=block),
        out_shape=jax.ShapeDtypeStruct((total, block), f32),
        in_specs=[VM, VM],
        out_specs=VM,
        compiler_params=params,
    )(swap(partial), targets[None, :])
    images = swap(image)

    partial_2, own = pl.pallas_call(
        lambda *refs: second_sweep_kernel(*refs, n_row=n_row, n_col=n_col),
        out_shape=(
            jax.ShapeDtypeStruct((total, 2 * block), f32),
            jax.ShapeDtypeStruct((8, block), f32),
        ),
        in_specs=[SM, SM, SM, VM, VM, VM],
        out_specs=(VM, VM),
        scratch_shapes=[
            pltpu.VMEM((total, block), f32),
            pltpu.VMEM((total, block), f32),
            pltpu.VMEM((n_col, block, block), f32),
        ] + accumulators,
        compiler_params=params,
    )(place, pairs, count, kernel, known[:, 0:block], images)

    result, residual = pl.pallas_call(
        lambda *refs: finish_kernel(*refs, block=block),
        out_shape=(jax.ShapeDtypeStruct((1, block), f32),) * 2,
        in_specs=[VM, VM],
        out_specs=(VM, VM),
        compiler_params=params,
    )(swap(partial_2), own)
    return (result[0], residual[0])


def solution(mesh):
    return jax.shard_map(
        body,
        mesh=mesh,
        in_specs=(
            P(("row", "col"), None),
            P(("row", "col")),
            P("row", "col", None, None),
            P("row", "col"),
        ),
        out_specs=(P(("row", "col")), P(("row", "col"))),
        check_vma=False,
    )
```

time: 981 us -> 337 us (0.34)
  blocking collectives: 601 us -> 43.8 us
  local copies, waits for them, and re-layouts: 152 us -> 4.71 us
  waiting for transfers between devices: 157 us -> 237 us
  matrix products: 35.8 us -> 0 us
  starting transfers between devices: 0.08 us -> 21.7 us
  Pallas kernels: 0 us -> 13 us
  other arithmetic: 13.2 us -> 1.89 us
    unnamed x4 -> x0, blocking collectives: 241 us -> none
    psum x3 -> x0, blocking collectives: 226 us -> none  [the longest x2 153 us: squares(): return lax.psum(jnp.sum(vector * vector), ('row', 'col'))]
    gather x96 -> x0, local copies, waits for them, and re-layouts: 146 us -> none  [the longest x16 55 us: advance(): row_blocks[take_row]]
    all_gather x4 -> x0, blocking collectives: 133 us -> none  [the longest x2 69.8 us: apply_kernel(): lax.all_gather(vector, 'col', axis=0, tiled=True).reshape(col_count, block)]
    all_gather x2, waiting for transfers between devices: 156 us -> 205 us  [the longest x1 140 us: body(): rows = lax.all_gather(features, 'col', axis=0).reshape(n_col, block, width)]
    all_to_all x0 -> x2, blocking collectives: none -> 43.8 us  [swap(): return lax.all_to_all(slots, AXES, 0, 0, tiled=True)]
    dot_general x96 -> x0, matrix products: 35.8 us -> none  [the longest x16 9.95 us: advance(): jnp.einsum('gid,gjd->gij', row_blocks[take_row], col_blocks[take_col], pr...]
    all_to_all x0 -> x2, waiting for transfers between devices: none -> 31 us  [swap(): return lax.all_to_all(slots, AXES, 0, 0, tiled=True)]
  transfers between devices with their start and end apart: 2 -> 4, of which waited for: 2 -> 4; matrix products, arithmetic and copies ran while one was open for 1% -> 1% of each run, Pallas kernels for 0% -> 0%
where the time goes in v1:
time: 337 us
  waiting for transfers between devices  237 us (70%)
  blocking collectives  43.8 us (13%)
  starting transfers between devices  21.7 us (6%)
  between operations  14.7 us (4%)
  Pallas kernels  13 us (4%)
  local copies, waits for them, and re-layouts  4.71 us (1%)
    all_gather x1, waiting for transfers between devices, body(): rows = lax.all_gather(features, 'col', axis=0).reshape(n_col, block, width)  140 us
    all_gather x1, waiting for transfers between devices, body(): cols = lax.all_gather(features, 'row', axis=0).reshape(n_row, block, width)  64.9 us
    all_to_all x2, blocking collectives, swap(): return lax.all_to_all(slots, AXES, 0, 0, tiled=True)  43.8 us
    all_to_all x2, waiting for transfers between devices, swap(): return lax.all_to_all(slots, AXES, 0, 0, tiled=True)  31 us
    all_to_all x2, starting transfers between devices, swap(): return lax.all_to_all(slots, AXES, 0, 0, tiled=True)  21.6 us
    pallas_call x1, Pallas kernels, body(): pl.pallas_call(first_sweep_kernel, out_shape=(jax.ShapeDtypeStruct((slots...  9 us
  transfers between devices with their start and end apart: 4, of which 4 were waited for; matrix products, arithmetic and copies ran while one was open for 1% of the time, Pallas kernels for 0%

profile of v1, /device:TPU:1, one launch (start us, length us, event | category | flops | bytes accessed | tf_op | source)
XLA Modules:
  0.0 337.1 jit_solution(1744561286114244919)
XLA Ops:
  7.2 0.0 all-gather.7.cloned.1.call-start
  7.2 0.7 all-gather.7.cloned.1.call-update
  7.9 0.0 all-gather.5.cloned.1.call-start
  7.9 0.7 all-gather.5.cloned.1.call-update
  8.6 1.2 multiply_reduce_fusion
  9.8 0.7 pad_maximum_fusion
  10.5 0.8 broadcast_in_dim.4
  11.3 15.7 %all-to-all-start = ((f32[256,1,256]{2,1,0:T(1,128)}), f32[256,1,256]{2,1,0:T(1,128)S(1)}, u32[]{:S(2)}, u32[]{:S(2)}) async-start(f32[256,1,256]{2,1,0:T(1,128)} %broadcast_in_dim.4), calls=%async_computation | async-start | bytes 524288 | tf_op jit(solution)/shard_map/all_to_all | solution.py:150
  27.6 0.8 copy.11.pairs.refs_1_
  28.4 0.1 pad_add_fusion.place.refs_0_
  28.5 18.0 %all-to-all-done = f32[256,1,256]{2,1,0:T(1,128)S(1)} async-done(((f32[256,1,256]{2,1,0:T(1,128)}), f32[256,1,256]{2,1,0:T(1,128)S(1)}, u32[]{:S(2)}, u32[]{:S(2)}) %all-to-all-start) | async-done | bytes 262176 | tf_op jit(solution)/shard_map/all_to_all | solution.py:150
  46.5 64.9 %all-gather.7.cloned.1.call-done = bf16[2048,1536]{1,0:T(8,128)(2,1)} async-done(((bf16[128,1536]{1,0:T(8,128)(2,1)}), bf16[2048,1536]{1,0:T(8,128)(2,1)}) %all-gather.7.cloned.1.call-update) | async-done | bytes 6291472 | tf_op jit(solution)/shard_map/all_gather | solution.py:175
  111.5 140.1 %all-gather.5.cloned.1.call-done = bf16[2048,1536]{1,0:T(8,128)(2,1)} async-done(((bf16[128,1536]{1,0:T(8,128)(2,1)}), bf16[2048,1536]{1,0:T(8,128)(2,1)}) %all-gather.5.cloned.1.call-update) | async-done | bytes 6291472 | tf_op jit(solution)/shard_map/all_gather | solution.py:174
  251.5 0.0 copy-start
  251.5 2.8 copy-done
  254.3 0.0 copy-start.1
  254.3 9.0 %shard_map.59 = (f32[32,128,128]{2,1,0:T(8,128)S(1)}, f32[256,128]{1,0:T(8,128)S(1)}) custom-call(s32[2]{0:T(128)S(1)} %pad_add_fusion.place.refs_0_, s32[32,2]{1,0:T(8,128)S(1)} %copy.11.pairs.refs_1_, s32[1]{0:T(128)} %bitcast.24.count, bf16[16,128,1536]{2,1,0:T(8,128)(2,1)S(1)} %bitcast.26, bf16[16,128,1536]{2,1,0:T(8,128)(2,1)} %bitcast.35, ...), custom_call_target="tpu_custom_call" | custom-call | tf_op jit(solution)/shard_map/pallas_call | solution.py:181
  263.3 22.3 %all_to_all.41 = f32[256,1,128]{2,1,0:T(1,128)S(1)} all-to-all(f32[256,1,128]{2,1,0:T(1,128)S(1)} %bitcast.33), channel_id=1, replica_groups=mesh['row'=16,'col'=16] {'row','col'}, dimensions={0} | all-to-all | bytes 262144 | tf_op jit(solution)/shard_map/all_to_all | solution.py:150
  285.6 0.0 copy-done.1
  285.6 0.7 shard_map.60
  286.3 6.0 %all-to-all-start.2 = ((f32[256,1,128]{2,1,0:T(1,128)}), f32[256,1,128]{2,1,0:T(1,128)S(1)}, u32[]{:S(2)}, u32[]{:S(2)}) async-start(f32[256,1,128]{2,1,0:T(1,128)} %bitcast.11), calls=%async_computation.2 | async-start | bytes 262144 | tf_op jit(solution)/shard_map/all_to_all | solution.py:150
  292.3 12.9 %all-to-all-done.2 = f32[256,1,128]{2,1,0:T(1,128)S(1)} async-done(((f32[256,1,128]{2,1,0:T(1,128)}), f32[256,1,128]{2,1,0:T(1,128)S(1)}, u32[]{:S(2)}, u32[]{:S(2)}) %all-to-all-start.2) | async-done | bytes 131104 | tf_op jit(solution)/shard_map/all_to_all | solution.py:150
  305.2 2.7 shard_map.61
  307.9 0.3 copy.12
  308.2 21.5 %all_to_all.42 = f32[256,1,256]{2,1,0:T(1,128)S(1)} all-to-all(f32[256,1,256]{2,1,0:T(1,128)S(1)} %copy.12), channel_id=1, replica_groups=mesh['row'=16,'col'=16] {'row','col'}, dimensions={0} | all-to-all | bytes 524288 | tf_op jit(solution)/shard_map/all_to_all | solution.py:150
  329.7 0.6 shard_map.62
  (3 shorter events, 0.0 us)
Async XLA Ops:
  7.2 104.3 %all-gather.7.cloned.1.call-start = ((), (), s32[]{:S(2)}) async-start(), calls=%async_computation.5 | async-start | bytes 6684672 | tf_op jit(solution)/shard_map/all_gather | solution.py:175
  7.9 243.6 %all-gather.5.cloned.1.call-start = ((), (), s32[]{:S(2)}) async-start(), calls=%async_computation.4 | async-start | bytes 6684672 | tf_op jit(solution)/shard_map/all_gather | solution.py:174
  11.3 35.2 %all-to-all-start = ((f32[256,1,256]{2,1,0:T(1,128)}), f32[256,1,256]{2,1,0:T(1,128)S(1)}, u32[]{:S(2)}, u32[]{:S(2)}) async-start(f32[256,1,256]{2,1,0:T(1,128)} %broadcast_in_dim.4), calls=%async_computation | async-start | bytes 524288 | tf_op jit(solution)/shard_map/all_to_all | solution.py:150
  251.5 2.8 copy-start
  254.3 31.3 %copy-start.1 = (f32[128]{0:T(128)S(1)}, f32[128]{0:T(128)}, u32[]{:S(2)}) copy-start(f32[128]{0:T(128)} %param.5) | copy-start | bytes 1540
  286.3 18.9 %all-to-all-start.2 = ((f32[256,1,128]{2,1,0:T(1,128)}), f32[256,1,128]{2,1,0:T(1,128)S(1)}, u32[]{:S(2)}, u32[]{:S(2)}) async-start(f32[256,1,128]{2,1,0:T(1,128)} %bitcast.11), calls=%async_computation.2 | async-start | bytes 262144 | tf_op jit(solution)/shard_map/all_to_all | solution.py:150
Sparse Core Ops, SparseCore 0:
  10.7 100.7 all-gather.6
  113.3 138.2 all-gather.4

commit v2 on v1

--- a/solution.py
+++ b/solution.py
@@ -1,5 +1,6 @@
 import jax
 import jax.numpy as jnp
+import numpy as np
 from jax import lax
 from jax.experimental import pallas as pl
 from jax.experimental.pallas import tpu as pltpu
@@ -45,12 +46,21 @@
 
 
 def first_sweep_kernel(
-    place, pairs, count, rows_ref, cols_ref, known_ref, kernel_ref, out_ref,
-    vec, norms, spread_v, spread_n, row_acc, col_acc,
+    row_plan, col_plan, place, pairs, count, row_spot, col_spot, known_ref, *rest
 ):
+    n_pieces = len(row_plan) + len(col_plan)
+    pieces = rest[:n_pieces]
+    (kernel_ref, out_ref, rows_ref, cols_ref, sems, vec, norms, spread_v, spread_n,
+     row_acc, col_acc) = rest[n_pieces:]
     n_col = rows_ref.shape[0]
     n_row = cols_ref.shape[0]
     width = rows_ref.shape[2]
+    copies = []
+    for k, (index, low, high) in enumerate(row_plan + col_plan):
+        target = rows_ref if k < len(row_plan) else cols_ref
+        copy = pltpu.make_async_copy(pieces[k], target.at[index, low:high], sems.at[k])
+        copy.start()
+        copies.append(copy)
     row_index = place[0]
     col_index = place[1]
     listed = count[0]
@@ -62,13 +72,16 @@
     row_acc[...] = jnp.zeros_like(row_acc)
     col_acc[...] = jnp.zeros_like(col_acc)
 
+    for copy in copies:
+        copy.wait()
+
     def step(turn, carry):
         for g in range(GROUP):
             slot = turn * GROUP + g
             a = pairs[slot, 0]
             b = pairs[slot, 1]
             inner = lax.dot_general(
-                rows_ref[a], cols_ref[b], (((1,), (1,)), ((), ())),
+                rows_ref[row_spot[col_index, a]], cols_ref[col_spot[row_index, b]], (((1,), (1,)), ((), ())),
                 preferred_element_type=jnp.float32,
             )
             norm_j = norms[pl.ds(b * n_col + col_index, 1), :]
@@ -152,6 +165,99 @@
 
 VM = pl.BlockSpec(memory_space=pltpu.VMEM)
 SM = pl.BlockSpec(memory_space=pltpu.SMEM)
+ANY = pl.BlockSpec(memory_space=pl.ANY)
+NX, NZ = 4, 4
+NY, NH, NK = 4, 2, 2
+Z_ORDER = ((0, 1, 2, 3), (1, 0, 2, 3), (2, 1, 3, 0), (3, 2, 1, 0))
+
+
+def along_x(array, step):
+    pairs = [(x * NZ + z, (x + step) % NX * NZ + z) for x in range(NX) for z in range(NZ)]
+    return lax.ppermute(array, "col", pairs)
+
+
+def along_z(array, step):
+    pairs = [
+        (x * NZ + z, x * NZ + z + step) for x in range(NX) for z in range(NZ) if 0 <= z + step < NZ
+    ]
+    return lax.ppermute(array, "col", pairs)
+
+
+def along_row(array, step, half, core):
+    pairs = []
+    for y in range(NY):
+        for h in range(NH):
+            for k in range(NK):
+                to = ((y + step) % NY * NH + (h + half) % NH) * NK + (k + core) % NK
+                pairs.append(((y * NH + h) * NK + k, to))
+    return lax.ppermute(array, "row", pairs)
+
+
+def ring(array, send):
+    middle = array.shape[-2] // 2
+    before = send(array, 1)
+    after = send(array, -1)
+    far_low = send(before[..., :middle, :], 1)
+    far_high = send(after[..., middle:, :], -1)
+    return before, after, far_low, far_high
+
+
+def gather_rows(features):
+    block = features.shape[0]
+    z = lax.axis_index("col") % NZ
+    up1 = along_z(features, 1)
+    down1 = along_z(features, -1)
+    up2 = along_z(up1, 1)
+    down2 = along_z(down1, -1)
+    up3 = along_z(up2, 1)
+    down3 = along_z(down2, -1)
+    kept = [
+        features,
+        jnp.where(z == 0, down1, up1),
+        jnp.where(z == 0, down2, jnp.where(z == 3, up2, down1)),
+        jnp.where(z == 0, down3, jnp.where(z == 1, down2, jnp.where(z == 2, up2, up3))),
+    ]
+    pieces, plan = [], []
+    for m, array in enumerate(kept):
+        before, after, far_low, far_high = ring(array, along_x)
+        pieces += [array, before, after, far_low, far_high]
+        plan += [
+            (m, 0, block), (3 * NZ + m, 0, block), (NZ + m, 0, block),
+            (2 * NZ + m, 0, block // 2), (2 * NZ + m, block // 2, block),
+        ]
+    return pieces, plan
+
+
+def gather_cols(features):
+    block = features.shape[0]
+    across = along_row(features, 0, 1, 0)
+    both = jnp.stack([features, across])
+    before, after, far_low, far_high = ring(both, lambda array, step: along_row(array, step, 0, 0))
+    pieces = [both, before, after, far_low, far_high]
+    plan = [
+        (slice(0, 2), 0, block), (slice(6, 8), 0, block), (slice(2, 4), 0, block),
+        (slice(4, 6), 0, block // 2), (slice(4, 6), block // 2, block),
+    ]
+    pieces += [along_row(piece, 0, 0, 1) for piece in pieces]
+    plan += [(slice(at.start + 8, at.stop + 8), low, high) for at, low, high in plan]
+    return pieces, plan
+
+
+def spots():
+    row_spot = np.zeros((NX * NZ, NX * NZ), np.int32)
+    for x in range(NX):
+        for z in range(NZ):
+            for ax in range(NX):
+                for az in range(NZ):
+                    row_spot[x * NZ + z, ax * NZ + az] = (ax - x) % NX * NZ + Z_ORDER[z].index(az)
+    col_spot = np.zeros((NY * NH * NK,) * 2, np.int32)
+    for here in range(NY * NH * NK):
+        for there in range(NY * NH * NK):
+            dy = (there // 4 - here // 4) % NY
+            dh = (there // 2 - here // 2) % 2
+            dk = (there - here) % 2
+            col_spot[here, there] = dk * 8 + dy * 2 + dh
+    return jnp.asarray(row_spot), jnp.asarray(col_spot)
 
 
 def body(features, targets, tile_pairs, tile_count):
@@ -171,25 +277,31 @@
     mine = jnp.concatenate([targets, norms])[None, :]
     known = swap(jnp.broadcast_to(mine, (total, 2 * block)))
 
-    rows = lax.all_gather(features, "col", axis=0).reshape(n_col, block, width)
-    cols = lax.all_gather(features, "row", axis=0).reshape(n_row, block, width)
+    row_pieces, row_plan = gather_rows(features)
+    col_pieces, col_plan = gather_cols(features)
+    row_spot, col_spot = spots()
 
     accumulators = [
         pltpu.VMEM((n_col, block, block), f32),
         pltpu.VMEM((n_row, 8, block), f32),
     ]
     kernel, partial = pl.pallas_call(
-        first_sweep_kernel,
+        lambda *refs: first_sweep_kernel(row_plan, col_plan, *refs),
         out_shape=(
             jax.ShapeDtypeStruct((slots, block, block), f32),
             jax.ShapeDtypeStruct((total, block), f32),
         ),
-        in_specs=[SM, SM, SM, VM, VM, VM],
+        in_specs=[SM, SM, SM, SM, SM, VM] + [ANY] * (len(row_plan) + len(col_plan)),
         out_specs=(VM, VM),
-        scratch_shapes=[pltpu.VMEM((total, block), f32)] * 2
+        scratch_shapes=[
+            pltpu.VMEM((n_col, block, width), jnp.bfloat16),
+            pltpu.VMEM((n_row, block, width), jnp.bfloat16),
+            pltpu.SemaphoreType.DMA((len(row_plan) + len(col_plan),)),
+        ]
+        + [pltpu.VMEM((total, block), f32)] * 2
         + [pltpu.VMEM((n_col, block, block), f32)] * 2 + accumulators,
         compiler_params=params,
-    )(place, pairs, count, rows, cols, known)
+    )(place, pairs, count, row_spot, col_spot, known, *row_pieces, *col_pieces)
 
     image = pl.pallas_call(
         lambda *refs: image_kernel(None, *refs, block=block),

time: 337 us -> 238 us (0.71)
  waiting for transfers between devices: 237 us -> 52.7 us
  starting transfers between devices: 21.7 us -> 82 us
  local copies, waits for them, and re-layouts: 4.71 us -> 31.2 us
  between operations: 14.7 us -> 1.69 us
  blocking collectives: 43.8 us -> 48.1 us
  Pallas kernels: 13 us -> 17.1 us
    all_gather x2 -> x0, waiting for transfers between devices: 205 us -> none  [the longest x1 140 us: body(): rows = lax.all_gather(features, 'col', axis=0).reshape(n_col, block, width)]
    ppermute x0 -> x32, starting transfers between devices: none -> 68.6 us  [the longest x10 27.6 us: along_row(): return lax.ppermute(array, 'row', pairs)]
    ppermute x0 -> x32, waiting for transfers between devices: none -> 38.7 us  [the longest x16 25.7 us: along_x(): return lax.ppermute(array, 'col', pairs)]
    unnamed x6 -> x84, local copies, waits for them, and re-layouts: 2.82 us -> 25.5 us
    all_to_all x2, waiting for transfers between devices: 31 us -> 14.1 us  [swap(): return lax.all_to_all(slots, AXES, 0, 0, tiled=True)]
    all_to_all x2, starting transfers between devices: 21.6 us -> 13.4 us  [swap(): return lax.all_to_all(slots, AXES, 0, 0, tiled=True)]
    all_to_all x2, blocking collectives: 43.8 us -> 48.1 us  [swap(): return lax.all_to_all(slots, AXES, 0, 0, tiled=True)]
    pallas_call x1, Pallas kernels: 9 us -> 13 us  [body(): pl.pallas_call(lambda *refs: first_sweep_kernel(row_plan, col_plan, *refs...]
  transfers between devices with their start and end apart: 4 -> 34, of which waited for: 4 -> 9; matrix products, arithmetic and copies ran while one was open for 1% -> 4% of each run, Pallas kernels for 0% -> 0%
where the time goes in v2:
time: 238 us; the launch traced here: 236 us
  starting transfers between devices  82 us (34%)
  waiting for transfers between devices  52.7 us (22%)
  blocking collectives  48.1 us (20%)
  local copies, waits for them, and re-layouts  31.2 us (13%)
  Pallas kernels  17.1 us (7%)
  other arithmetic  3.38 us (1%)
    all_to_all x2, blocking collectives, swap(): return lax.all_to_all(slots, AXES, 0, 0, tiled=True)  48.1 us
    ppermute x10, starting transfers between devices, along_row(): return lax.ppermute(array, 'row', pairs)  27.6 us
    ppermute x16, waiting for transfers between devices, along_x(): return lax.ppermute(array, 'col', pairs)  25.7 us
    unnamed x84, local copies, waits for them, and re-layouts  25.5 us
    ppermute x16, starting transfers between devices, along_x(): return lax.ppermute(array, 'col', pairs)  20.6 us
    ppermute x6, starting transfers between devices, along_z(): return lax.ppermute(array, 'col', pairs)  20.4 us
    all_to_all x2, waiting for transfers between devices, swap(): return lax.all_to_all(slots, AXES, 0, 0, tiled=True)  14.1 us
    all_to_all x2, starting transfers between devices, swap(): return lax.all_to_all(slots, AXES, 0, 0, tiled=True)  13.4 us
  transfers between devices with their start and end apart: 34, of which 9 were waited for; matrix products, arithmetic and copies ran while one was open for 4% of the time, Pallas kernels for 0%

profile of v2, /device:TPU:1, one launch (start us, length us, event | category | flops | bytes accessed | tf_op | source)
XLA Modules:
  0.0 236.2 jit_solution(2851169519012469981)
XLA Ops:
  1.9 5.0 %collective-permute-start.5 = (bf16[128,1536]{1,0:T(8,128)(2,1)}, bf16[128,1536]{1,0:T(8,128)(2,1)S(1)}, u32[]{:S(2)}, u32[]{:S(2)}) collective-permute-start(bf16[128,1536]{1,0:T(8,128)(2,1)} %refs_6_.1), channel_id=1, source_target_pairs={{0,1},{1,2},{2,3},{4,5},{5,6},{6,7},{8,9},{9,10},{10,11},{12,13},{... | collective-permute-start | bytes 1179656 | tf_op jit(solution)/shard_map/ppermute | solution.py:183
  7.0 5.2 %collective-permute-done.4 = bf16[128,1536]{1,0:T(8,128)(2,1)S(1)} collective-permute-done((bf16[128,1536]{1,0:T(8,128)(2,1)}, bf16[128,1536]{1,0:T(8,128)(2,1)S(1)}, u32[]{:S(2)}, u32[]{:S(2)}) %collective-permute-start.4) | collective-permute-done | bytes 393248 | tf_op jit(solution)/shard_map/ppermute | solution.py:183
  13.4 6.8 %collective-permute-start.11 = (bf16[128,1536]{1,0:T(8,128)(2,1)S(1)}, bf16[128,1536]{1,0:T(8,128)(2,1)}, u32[]{:S(2)}, u32[]{:S(2)}) collective-permute-start(bf16[128,1536]{1,0:T(8,128)(2,1)S(1)} %collective-permute-done.5), channel_id=1, source_target_pairs={{0,1},{1,2},{2,3},{4,5},{5,6},{6,7},{8,9},{9,10},{10,11},{12,13},{... | collective-permute-start | bytes 1179656 | tf_op jit(solution)/shard_map/ppermute | solution.py:183
  20.2 6.3 %collective-permute-start.22 = (bf16[128,1536]{1,0:T(8,128)(2,1)}, bf16[128,1536]{1,0:T(8,128)(2,1)S(1)}, u32[]{:S(2)}, u32[]{:S(2)}) collective-permute-start(bf16[128,1536]{1,0:T(8,128)(2,1)} %refs_6_.1), channel_id=1, source_target_pairs={{0,32},{16,48},{32,0},{48,16},{64,96},{80,112},{96,64},{112,80},{1... | collective-permute-start | bytes 1179656 | tf_op jit(solution)/shard_map/ppermute | solution.py:193
  30.5 4.7 %collective-permute-start.17 = (bf16[128,1536]{1,0:T(8,128)(2,1)}, bf16[128,1536]{1,0:T(8,128)(2,1)}, u32[]{:S(2)}, u32[]{:S(2)}) collective-permute-start(bf16[128,1536]{1,0:T(8,128)(2,1)} %collective-permute-done.11), channel_id=1, source_target_pairs={{0,1},{1,2},{2,3},{4,5},{5,6},{6,7},{8,9},{9,10},{10,11},{12,13},{... | collective-permute-start | bytes 1179656 | tf_op jit(solution)/shard_map/ppermute | solution.py:183
  35.2 7.8 %collective-permute-done.22 = bf16[128,1536]{1,0:T(8,128)(2,1)S(1)} collective-permute-done((bf16[128,1536]{1,0:T(8,128)(2,1)}, bf16[128,1536]{1,0:T(8,128)(2,1)S(1)}, u32[]{:S(2)}, u32[]{:S(2)}) %collective-permute-start.22) | collective-permute-done | bytes 393248 | tf_op jit(solution)/shard_map/ppermute | solution.py:193
  45.5 1.6 collective-permute-start.24
  47.1 12.5 %collective-permute-start.27 = (bf16[2,128,1536]{2,1,0:T(8,128)(2,1)S(1)}, bf16[2,128,1536]{2,1,0:T(8,128)(2,1)S(1)}, u32[]{:S(2)}, u32[]{:S(2)}) collective-permute-start(bf16[2,128,1536]{2,1,0:T(8,128)(2,1)S(1)} %pad_maximum_fusion.refs_26_), channel_id=1, source_target_pairs={{0,16},{16,0},{32,48},{48,32},{64,80},{80,64},{96,112},{112,96},{1... | collective-permute-start | bytes 2359304 | tf_op jit(solution)/shard_map/ppermute | solution.py:193
  60.9 1.5 collective-permute-start.3
  62.3 1.5 select_select_fusion
  63.9 3.5 %collective-permute-done.2.refs_9_ = bf16[64,1536]{1,0:T(8,128)(2,1)S(1)} collective-permute-done((bf16[64,1536]{1,0:T(8,128)(2,1)S(1)}, bf16[64,1536]{1,0:T(8,128)(2,1)S(1)}, u32[]{:S(2)}, u32[]{:S(2)}) %collective-permute-start.2) | collective-permute-done | bytes 196640 | tf_op jit(solution)/shard_map/ppermute | solution.py:176
  68.7 2.7 %collective-permute-start.13 = (bf16[128,1536]{1,0:T(8,128)(2,1)S(1)}, bf16[128,1536]{1,0:T(8,128)(2,1)S(1)}, u32[]{:S(2)}, u32[]{:S(2)}) collective-permute-start(bf16[128,1536]{1,0:T(8,128)(2,1)S(1)} %get-tuple-element.15.refs_16_), channel_id=1, source_target_pairs={{0,12},{1,13},{2,14},{3,15},{4,0},{5,1},{6,2},{7,3},{8,4},{9,5},{1... | collective-permute-start | bytes 1179656 | tf_op jit(solution)/shard_map/ppermute | solution.py:176
  71.4 2.7 %collective-permute-start.19 = (bf16[128,1536]{1,0:T(8,128)(2,1)S(1)}, bf16[128,1536]{1,0:T(8,128)(2,1)S(1)}, u32[]{:S(2)}, u32[]{:S(2)}) collective-permute-start(bf16[128,1536]{1,0:T(8,128)(2,1)S(1)} %get-tuple-element.14.refs_21_), channel_id=1, source_target_pairs={{0,12},{1,13},{2,14},{3,15},{4,0},{5,1},{6,2},{7,3},{8,4},{9,5},{1... | collective-permute-start | bytes 1179656 | tf_op jit(solution)/shard_map/ppermute | solution.py:176
  75.0 4.1 %collective-permute-done.12.refs_17_ = bf16[128,1536]{1,0:T(8,128)(2,1)S(1)} collective-permute-done((bf16[128,1536]{1,0:T(8,128)(2,1)S(1)}, bf16[128,1536]{1,0:T(8,128)(2,1)S(1)}, u32[]{:S(2)}, u32[]{:S(2)}) %collective-permute-start.12) | collective-permute-done | bytes 393248 | tf_op jit(solution)/shard_map/ppermute | solution.py:176
  79.3 8.2 %collective-permute-done.18.refs_22_ = bf16[128,1536]{1,0:T(8,128)(2,1)S(1)} collective-permute-done((bf16[128,1536]{1,0:T(8,128)(2,1)S(1)}, bf16[128,1536]{1,0:T(8,128)(2,1)S(1)}, u32[]{:S(2)}, u32[]{:S(2)}) %collective-permute-start.18) | collective-permute-done | bytes 393248 | tf_op jit(solution)/shard_map/ppermute | solution.py:176
  87.5 1.5 collective-permute-start.26
  89.2 6.8 %collective-permute-done.6.refs_12_ = bf16[128,1536]{1,0:T(8,128)(2,1)S(1)} collective-permute-done((bf16[128,1536]{1,0:T(8,128)(2,1)S(1)}, bf16[128,1536]{1,0:T(8,128)(2,1)S(1)}, u32[]{:S(2)}, u32[]{:S(2)}) %collective-permute-start.6) | collective-permute-done | bytes 393248 | tf_op jit(solution)/shard_map/ppermute | solution.py:176
  96.0 3.0 %collective-permute-start.28 = (bf16[2,128,1536]{2,1,0:T(8,128)(2,1)S(1)}, bf16[2,128,1536]{2,1,0:T(8,128)(2,1)}, u32[]{:S(2)}, u32[]{:S(2)}) collective-permute-start(bf16[2,128,1536]{2,1,0:T(8,128)(2,1)S(1)} %collective-permute-done.23.refs_27_), channel_id=1, source_target_pairs={{0,16},{16,0},{32,48},{48,32},{64,80},{80,64},{96,112},{112,96},{1... | collective-permute-start | bytes 2359304 | tf_op jit(solution)/shard_map/ppermute | solution.py:193
  102.1 1.9 collective-permute-start.15
  104.8 2.7 %collective-permute-start.21 = (bf16[64,1536]{1,0:T(8,128)(2,1)}, bf16[64,1536]{1,0:T(8,128)(2,1)}, u32[]{:S(2)}, u32[]{:S(2)}) collective-permute-start(bf16[64,1536]{1,0:T(8,128)(2,1)} %slice.51), channel_id=1, source_target_pairs={{0,12},{1,13},{2,14},{3,15},{4,0},{5,1},{6,2},{7,3},{8,4},{9,5},{1... | collective-permute-start | bytes 589832 | tf_op jit(solution)/shard_map/ppermute | solution.py:176
  108.3 7.4 %all-to-all-start = ((f32[256,1,256]{2,1,0:T(1,128)}), f32[256,1,256]{2,1,0:T(1,128)}, u32[]{:S(2)}, u32[]{:S(2)}) async-start(f32[256,1,256]{2,1,0:T(1,128)} %broadcast_in_dim.4), calls=%async_computation | async-start | bytes 524288 | tf_op jit(solution)/shard_map/all_to_all | solution.py:163
  115.7 1.5 collective-permute-start.8
  118.4 1.6 slice.47
  120.0 3.1 %collective-permute-done.8.refs_14_ = bf16[64,1536]{1,0:T(8,128)(2,1)S(1)} collective-permute-done((bf16[64,1536]{1,0:T(8,128)(2,1)S(1)}, bf16[64,1536]{1,0:T(8,128)(2,1)S(1)}, u32[]{:S(2)}, u32[]{:S(2)}) %collective-permute-start.8) | collective-permute-done | bytes 196640 | tf_op jit(solution)/shard_map/ppermute | solution.py:176
  123.7 3.6 %collective-permute-start.9 = (bf16[64,1536]{1,0:T(8,128)(2,1)}, bf16[64,1536]{1,0:T(8,128)(2,1)}, u32[]{:S(2)}, u32[]{:S(2)}) collective-permute-start(bf16[64,1536]{1,0:T(8,128)(2,1)} %slice.47), channel_id=1, source_target_pairs={{0,12},{1,13},{2,14},{3,15},{4,0},{5,1},{6,2},{7,3},{8,4},{9,5},{1... | collective-permute-start | bytes 589832 | tf_op jit(solution)/shard_map/ppermute | solution.py:176
  149.5 13.0 %shard_map.77 = (f32[32,128,128]{2,1,0:T(8,128)}, f32[256,128]{1,0:T(8,128)S(1)}) custom-call(s32[2]{0:T(128)S(1)} %copy-done.36, s32[32,2]{1,0:T(8,128)S(1)} %copy.13.refs_1_, s32[1]{0:T(128)} %bitcast.24.refs_2_, s32[16,16]{1,0:T(8,128)S(1)} %copy-done.34, s32[16,16]{1,0:T(8,128)S(1)} %copy-done.35, f32[256,256]{1,0:T(8,128)S(1)} %bitcast.27, ...), custom_call_target="tpu_custom_call" | custom-call | tf_op jit(solution)/shard_map/pallas_call | solution.py:288
  162.5 26.7 %all_to_all.41 = f32[256,1,128]{2,1,0:T(1,128)S(1)} all-to-all(f32[256,1,128]{2,1,0:T(1,128)S(1)} %bitcast.33), channel_id=1, replica_groups=mesh['row'=16,'col'=16] {'row','col'}, dimensions={0} | all-to-all | bytes 262144 | tf_op jit(solution)/shard_map/all_to_all | solution.py:163
  189.9 6.0 %all-to-all-start.2 = ((f32[256,1,128]{2,1,0:T(1,128)}), f32[256,1,128]{2,1,0:T(1,128)S(1)}, u32[]{:S(2)}, u32[]{:S(2)}) async-start(f32[256,1,128]{2,1,0:T(1,128)} %bitcast.11), calls=%async_computation.2 | async-start | bytes 262144 | tf_op jit(solution)/shard_map/all_to_all | solution.py:163
  196.0 12.9 %all-to-all-done.2 = f32[256,1,128]{2,1,0:T(1,128)S(1)} async-done(((f32[256,1,128]{2,1,0:T(1,128)}), f32[256,1,128]{2,1,0:T(1,128)S(1)}, u32[]{:S(2)}, u32[]{:S(2)}) %all-to-all-start.2) | async-done | bytes 131104 | tf_op jit(solution)/shard_map/all_to_all | solution.py:163
  208.9 1.6 copy-done.1
  211.1 2.7 %shard_map.79 = (f32[256,256]{1,0:T(8,128)S(1)}, f32[8,128]{1,0:T(8,128)S(1)}) custom-call(s32[2]{0:T(128)S(1)} %copy-done.37, s32[32,2]{1,0:T(8,128)S(1)} %copy.13.refs_1_, s32[1]{0:T(128)} %bitcast.25.refs_2_, f32[32,128,128]{2,1,0:T(8,128)S(1)} %copy-done.1, f32[256,128]{1,0:T(8,128)S(1)} %slice.54.refs_4_, f32[256,128]{1,0:T(8,128)S(1)} %bitcast.30), custom_call_target="tpu_custom_call" | custom-call | tf_op jit(solution)/shard_map/pallas_call | solution.py:315
  214.2 21.5 %all_to_all.42 = f32[256,1,256]{2,1,0:T(1,128)S(1)} all-to-all(f32[256,1,256]{2,1,0:T(1,128)S(1)} %copy.14), channel_id=1, replica_groups=mesh['row'=16,'col'=16] {'row','col'}, dimensions={0} | all-to-all | bytes 524288 | tf_op jit(solution)/shard_map/all_to_all | solution.py:163
  (145 shorter events, 43.1 us)
Async XLA Ops:
  0.6 11.5 %collective-permute-start.4 = (bf16[128,1536]{1,0:T(8,128)(2,1)}, bf16[128,1536]{1,0:T(8,128)(2,1)S(1)}, u32[]{:S(2)}, u32[]{:S(2)}) collective-permute-start(bf16[128,1536]{1,0:T(8,128)(2,1)} %refs_6_.1), channel_id=1, source_target_pairs={{1,0},{2,1},{3,2},{5,4},{6,5},{7,6},{9,8},{10,9},{11,10},{13,12},{... | collective-permute-start | bytes 1179656 | tf_op jit(solution)/shard_map/ppermute | solution.py:183
  1.9 11.5 %collective-permute-start.5 = (bf16[128,1536]{1,0:T(8,128)(2,1)}, bf16[128,1536]{1,0:T(8,128)(2,1)S(1)}, u32[]{:S(2)}, u32[]{:S(2)}) collective-permute-start(bf16[128,1536]{1,0:T(8,128)(2,1)} %refs_6_.1), channel_id=1, source_target_pairs={{0,1},{1,2},{2,3},{4,5},{5,6},{6,7},{8,9},{9,10},{10,11},{12,13},{... | collective-permute-start | bytes 1179656 | tf_op jit(solution)/shard_map/ppermute | solution.py:183
  12.1 17.1 %collective-permute-start.10 = (bf16[128,1536]{1,0:T(8,128)(2,1)S(1)}, bf16[128,1536]{1,0:T(8,128)(2,1)}, u32[]{:S(2)}, u32[]{:S(2)}) collective-permute-start(bf16[128,1536]{1,0:T(8,128)(2,1)S(1)} %collective-permute-done.4), channel_id=1, source_target_pairs={{1,0},{2,1},{3,2},{5,4},{6,5},{7,6},{9,8},{10,9},{11,10},{13,12},{... | collective-permute-start | bytes 1179656 | tf_op jit(solution)/shard_map/ppermute | solution.py:183
  13.4 17.1 %collective-permute-start.11 = (bf16[128,1536]{1,0:T(8,128)(2,1)S(1)}, bf16[128,1536]{1,0:T(8,128)(2,1)}, u32[]{:S(2)}, u32[]{:S(2)}) collective-permute-start(bf16[128,1536]{1,0:T(8,128)(2,1)S(1)} %collective-permute-done.5), channel_id=1, source_target_pairs={{0,1},{1,2},{2,3},{4,5},{5,6},{6,7},{8,9},{9,10},{10,11},{12,13},{... | collective-permute-start | bytes 1179656 | tf_op jit(solution)/shard_map/ppermute | solution.py:183
  20.2 22.8 %collective-permute-start.22 = (bf16[128,1536]{1,0:T(8,128)(2,1)}, bf16[128,1536]{1,0:T(8,128)(2,1)S(1)}, u32[]{:S(2)}, u32[]{:S(2)}) collective-permute-start(bf16[128,1536]{1,0:T(8,128)(2,1)} %refs_6_.1), channel_id=1, source_target_pairs={{0,32},{16,48},{32,0},{48,16},{64,96},{80,112},{96,64},{112,80},{1... | collective-permute-start | bytes 1179656 | tf_op jit(solution)/shard_map/ppermute | solution.py:193
  26.5 18.9 %collective-permute-start = (bf16[128,1536]{1,0:T(8,128)(2,1)}, bf16[128,1536]{1,0:T(8,128)(2,1)S(1)}, u32[]{:S(2)}, u32[]{:S(2)}) collective-permute-start(bf16[128,1536]{1,0:T(8,128)(2,1)} %refs_6_.1), channel_id=1, source_target_pairs={{0,4},{1,5},{2,6},{3,7},{4,8},{5,9},{6,10},{7,11},{8,12},{9,13},{1... | collective-permute-start | bytes 1179656 | tf_op jit(solution)/shard_map/ppermute | solution.py:176
  27.7 19.3 %collective-permute-start.1 = (bf16[128,1536]{1,0:T(8,128)(2,1)}, bf16[128,1536]{1,0:T(8,128)(2,1)S(1)}, u32[]{:S(2)}, u32[]{:S(2)}) collective-permute-start(bf16[128,1536]{1,0:T(8,128)(2,1)} %refs_6_.1), channel_id=1, source_target_pairs={{0,12},{1,13},{2,14},{3,15},{4,0},{5,1},{6,2},{7,3},{8,4},{9,5},{1... | collective-permute-start | bytes 1179656 | tf_op jit(solution)/shard_map/ppermute | solution.py:176
  29.2 30.4 %collective-permute-start.16 = (bf16[128,1536]{1,0:T(8,128)(2,1)}, bf16[128,1536]{1,0:T(8,128)(2,1)}, u32[]{:S(2)}, u32[]{:S(2)}) collective-permute-start(bf16[128,1536]{1,0:T(8,128)(2,1)} %collective-permute-done.10), channel_id=1, source_target_pairs={{1,0},{2,1},{3,2},{5,4},{6,5},{7,6},{9,8},{10,9},{11,10},{13,12},{... | collective-permute-start | bytes 1179656 | tf_op jit(solution)/shard_map/ppermute | solution.py:183
  30.5 30.4 %collective-permute-start.17 = (bf16[128,1536]{1,0:T(8,128)(2,1)}, bf16[128,1536]{1,0:T(8,128)(2,1)}, u32[]{:S(2)}, u32[]{:S(2)}) collective-permute-start(bf16[128,1536]{1,0:T(8,128)(2,1)} %collective-permute-done.11), channel_id=1, source_target_pairs={{0,1},{1,2},{2,3},{4,5},{5,6},{6,7},{8,9},{9,10},{10,11},{12,13},{... | collective-permute-start | bytes 1179656 | tf_op jit(solution)/shard_map/ppermute | solution.py:183
  44.1 27.3 %collective-permute-start.23 = (bf16[2,128,1536]{2,1,0:T(8,128)(2,1)S(1)}, bf16[2,128,1536]{2,1,0:T(8,128)(2,1)S(1)}, u32[]{:S(2)}, u32[]{:S(2)}) collective-permute-start(bf16[2,128,1536]{2,1,0:T(8,128)(2,1)S(1)} %pad_maximum_fusion.refs_26_), channel_id=1, source_target_pairs={{0,64},{16,80},{32,96},{48,112},{64,128},{80,144},{96,160},{112,17... | collective-permute-start | bytes 2359304 | tf_op jit(solution)/shard_map/ppermute | solution.py:193
  45.5 25.9 %collective-permute-start.24 = (bf16[2,128,1536]{2,1,0:T(8,128)(2,1)S(1)}, bf16[2,128,1536]{2,1,0:T(8,128)(2,1)S(1)}, u32[]{:S(2)}, u32[]{:S(2)}) collective-permute-start(bf16[2,128,1536]{2,1,0:T(8,128)(2,1)S(1)} %pad_maximum_fusion.refs_26_), channel_id=1, source_target_pairs={{0,192},{16,208},{32,224},{48,240},{64,0},{80,16},{96,32},{112,48}... | collective-permute-start | bytes 2359304 | tf_op jit(solution)/shard_map/ppermute | solution.py:193
  47.1 27.0 %collective-permute-start.27 = (bf16[2,128,1536]{2,1,0:T(8,128)(2,1)S(1)}, bf16[2,128,1536]{2,1,0:T(8,128)(2,1)S(1)}, u32[]{:S(2)}, u32[]{:S(2)}) collective-permute-start(bf16[2,128,1536]{2,1,0:T(8,128)(2,1)S(1)} %pad_maximum_fusion.refs_26_), channel_id=1, source_target_pairs={{0,16},{16,0},{32,48},{48,32},{64,80},{80,64},{96,112},{112,96},{1... | collective-permute-start | bytes 2359304 | tf_op jit(solution)/shard_map/ppermute | solution.py:193
  59.6 7.8 %collective-permute-start.2 = (bf16[64,1536]{1,0:T(8,128)(2,1)S(1)}, bf16[64,1536]{1,0:T(8,128)(2,1)S(1)}, u32[]{:S(2)}, u32[]{:S(2)}) collective-permute-start(bf16[64,1536]{1,0:T(8,128)(2,1)S(1)} %slice.44), channel_id=1, source_target_pairs={{0,4},{1,5},{2,6},{3,7},{4,8},{5,9},{6,10},{7,11},{8,12},{9,13},{1... | collective-permute-start | bytes 589832 | tf_op jit(solution)/shard_map/ppermute | solution.py:176
  68.1 11.0 %collective-permute-start.12 = (bf16[128,1536]{1,0:T(8,128)(2,1)S(1)}, bf16[128,1536]{1,0:T(8,128)(2,1)S(1)}, u32[]{:S(2)}, u32[]{:S(2)}) collective-permute-start(bf16[128,1536]{1,0:T(8,128)(2,1)S(1)} %get-tuple-element.15.refs_16_), channel_id=1, source_target_pairs={{0,4},{1,5},{2,6},{3,7},{4,8},{5,9},{6,10},{7,11},{8,12},{9,13},{1... | collective-permute-start | bytes 1179656 | tf_op jit(solution)/shard_map/ppermute | solution.py:176
  68.7 10.5 %collective-permute-start.13 = (bf16[128,1536]{1,0:T(8,128)(2,1)S(1)}, bf16[128,1536]{1,0:T(8,128)(2,1)S(1)}, u32[]{:S(2)}, u32[]{:S(2)}) collective-permute-start(bf16[128,1536]{1,0:T(8,128)(2,1)S(1)} %get-tuple-element.15.refs_16_), channel_id=1, source_target_pairs={{0,12},{1,13},{2,14},{3,15},{4,0},{5,1},{6,2},{7,3},{8,4},{9,5},{1... | collective-permute-start | bytes 1179656 | tf_op jit(solution)/shard_map/ppermute | solution.py:176
  71.4 16.1 %collective-permute-start.18 = (bf16[128,1536]{1,0:T(8,128)(2,1)S(1)}, bf16[128,1536]{1,0:T(8,128)(2,1)S(1)}, u32[]{:S(2)}, u32[]{:S(2)}) collective-permute-start(bf16[128,1536]{1,0:T(8,128)(2,1)S(1)} %get-tuple-element.14.refs_21_), channel_id=1, source_target_pairs={{0,4},{1,5},{2,6},{3,7},{4,8},{5,9},{6,10},{7,11},{8,12},{9,13},{1... | collective-permute-start | bytes 1179656 | tf_op jit(solution)/shard_map/ppermute | solution.py:176
  71.4 17.7 %collective-permute-start.19 = (bf16[128,1536]{1,0:T(8,128)(2,1)S(1)}, bf16[128,1536]{1,0:T(8,128)(2,1)S(1)}, u32[]{:S(2)}, u32[]{:S(2)}) collective-permute-start(bf16[128,1536]{1,0:T(8,128)(2,1)S(1)} %get-tuple-element.14.refs_21_), channel_id=1, source_target_pairs={{0,12},{1,13},{2,14},{3,15},{4,0},{5,1},{6,2},{7,3},{8,4},{9,5},{1... | collective-permute-start | bytes 1179656 | tf_op jit(solution)/shard_map/ppermute | solution.py:176
  75.0 21.0 %collective-permute-start.6 = (bf16[128,1536]{1,0:T(8,128)(2,1)S(1)}, bf16[128,1536]{1,0:T(8,128)(2,1)S(1)}, u32[]{:S(2)}, u32[]{:S(2)}) collective-permute-start(bf16[128,1536]{1,0:T(8,128)(2,1)S(1)} %get-tuple-element.16.refs_11_), channel_id=1, source_target_pairs={{0,4},{1,5},{2,6},{3,7},{4,8},{5,9},{6,10},{7,11},{8,12},{9,13},{1... | collective-permute-start | bytes 1179656 | tf_op jit(solution)/shard_map/ppermute | solution.py:176
  79.1 19.8 %collective-permute-start.7 = (bf16[128,1536]{1,0:T(8,128)(2,1)S(1)}, bf16[128,1536]{1,0:T(8,128)(2,1)S(1)}, u32[]{:S(2)}, u32[]{:S(2)}) collective-permute-start(bf16[128,1536]{1,0:T(8,128)(2,1)S(1)} %get-tuple-element.16.refs_11_), channel_id=1, source_target_pairs={{0,12},{1,13},{2,14},{3,15},{4,0},{5,1},{6,2},{7,3},{8,4},{9,5},{1... | collective-permute-start | bytes 1179656 | tf_op jit(solution)/shard_map/ppermute | solution.py:176
  79.3 22.1 %collective-permute-start.25 = (bf16[2,64,1536]{2,1,0:T(8,128)(2,1)S(1)}, bf16[2,64,1536]{2,1,0:T(8,128)(2,1)S(1)}, u32[]{:S(2)}, u32[]{:S(2)}) collective-permute-start(bf16[2,64,1536]{2,1,0:T(8,128)(2,1)S(1)} %slice.52), channel_id=1, source_target_pairs={{0,64},{16,80},{32,96},{48,112},{64,128},{80,144},{96,160},{112,17... | collective-permute-start | bytes 1179656 | tf_op jit(solution)/shard_map/ppermute | solution.py:193
  87.5 16.5 %collective-permute-start.26 = (bf16[2,64,1536]{2,1,0:T(8,128)(2,1)S(1)}, bf16[2,64,1536]{2,1,0:T(8,128)(2,1)}, u32[]{:S(2)}, u32[]{:S(2)}) collective-permute-start(bf16[2,64,1536]{2,1,0:T(8,128)(2,1)S(1)} %slice.53), channel_id=1, source_target_pairs={{0,192},{16,208},{32,224},{48,240},{64,0},{80,16},{96,32},{112,48}... | collective-permute-start | bytes 1179656 | tf_op jit(solution)/shard_map/ppermute | solution.py:193
  89.1 15.0 %collective-permute-start.14 = (bf16[64,1536]{1,0:T(8,128)(2,1)S(1)}, bf16[64,1536]{1,0:T(8,128)(2,1)S(1)}, u32[]{:S(2)}, u32[]{:S(2)}) collective-permute-start(bf16[64,1536]{1,0:T(8,128)(2,1)S(1)} %slice.48), channel_id=1, source_target_pairs={{0,4},{1,5},{2,6},{3,7},{4,8},{5,9},{6,10},{7,11},{8,12},{9,13},{1... | collective-permute-start | bytes 589832 | tf_op jit(solution)/shard_map/ppermute | solution.py:176
  96.0 35.6 %collective-permute-start.28 = (bf16[2,128,1536]{2,1,0:T(8,128)(2,1)S(1)}, bf16[2,128,1536]{2,1,0:T(8,128)(2,1)}, u32[]{:S(2)}, u32[]{:S(2)}) collective-permute-start(bf16[2,128,1536]{2,1,0:T(8,128)(2,1)S(1)} %collective-permute-done.23.refs_27_), channel_id=1, source_target_pairs={{0,16},{16,0},{32,48},{48,32},{64,80},{80,64},{96,112},{112,96},{1... | collective-permute-start | bytes 2359304 | tf_op jit(solution)/shard_map/ppermute | solution.py:193
  99.0 32.6 %collective-permute-start.29 = (bf16[2,128,1536]{2,1,0:T(8,128)(2,1)S(1)}, bf16[2,128,1536]{2,1,0:T(8,128)(2,1)}, u32[]{:S(2)}, u32[]{:S(2)}) collective-permute-start(bf16[2,128,1536]{2,1,0:T(8,128)(2,1)S(1)} %collective-permute-done.24.refs_28_), channel_id=1, source_target_pairs={{0,16},{16,0},{32,48},{48,32},{64,80},{80,64},{96,112},{112,96},{1... | collective-permute-start | bytes 2359304 | tf_op jit(solution)/shard_map/ppermute | solution.py:193
  102.1 13.6 %collective-permute-start.15 = (bf16[64,1536]{1,0:T(8,128)(2,1)}, bf16[64,1536]{1,0:T(8,128)(2,1)}, u32[]{:S(2)}, u32[]{:S(2)}) collective-permute-start(bf16[64,1536]{1,0:T(8,128)(2,1)} %slice.49), channel_id=1, source_target_pairs={{0,12},{1,13},{2,14},{3,15},{4,0},{5,1},{6,2},{7,3},{8,4},{9,5},{1... | collective-permute-start | bytes 589832 | tf_op jit(solution)/shard_map/ppermute | solution.py:176
  104.1 13.1 %collective-permute-start.20 = (bf16[64,1536]{1,0:T(8,128)(2,1)}, bf16[64,1536]{1,0:T(8,128)(2,1)}, u32[]{:S(2)}, u32[]{:S(2)}) collective-permute-start(bf16[64,1536]{1,0:T(8,128)(2,1)} %slice.50), channel_id=1, source_target_pairs={{0,4},{1,5},{2,6},{3,7},{4,8},{5,9},{6,10},{7,11},{8,12},{9,13},{1... | collective-permute-start | bytes 589832 | tf_op jit(solution)/shard_map/ppermute | solution.py:176
  104.8 13.5 %collective-permute-start.21 = (bf16[64,1536]{1,0:T(8,128)(2,1)}, bf16[64,1536]{1,0:T(8,128)(2,1)}, u32[]{:S(2)}, u32[]{:S(2)}) collective-permute-start(bf16[64,1536]{1,0:T(8,128)(2,1)} %slice.51), channel_id=1, source_target_pairs={{0,12},{1,13},{2,14},{3,15},{4,0},{5,1},{6,2},{7,3},{8,4},{9,5},{1... | collective-permute-start | bytes 589832 | tf_op jit(solution)/shard_map/ppermute | solution.py:176
  108.3 22.3 %all-to-all-start = ((f32[256,1,256]{2,1,0:T(1,128)}), f32[256,1,256]{2,1,0:T(1,128)}, u32[]{:S(2)}, u32[]{:S(2)}) async-start(f32[256,1,256]{2,1,0:T(1,128)} %broadcast_in_dim.4), calls=%async_computation | async-start | bytes 524288 | tf_op jit(solution)/shard_map/all_to_all | solution.py:163
  117.2 14.4 %collective-permute-start.30 = (bf16[2,64,1536]{2,1,0:T(8,128)(2,1)}, bf16[2,64,1536]{2,1,0:T(8,128)(2,1)}, u32[]{:S(2)}, u32[]{:S(2)}) collective-permute-start(bf16[2,64,1536]{2,1,0:T(8,128)(2,1)} %copy-done.24), channel_id=1, source_target_pairs={{0,16},{16,0},{32,48},{48,32},{64,80},{80,64},{96,112},{112,96},{1... | collective-permute-start | bytes 1179656 | tf_op jit(solution)/shard_map/ppermute | solution.py:193
  118.3 13.3 %collective-permute-start.31 = (bf16[2,64,1536]{2,1,0:T(8,128)(2,1)}, bf16[2,64,1536]{2,1,0:T(8,128)(2,1)}, u32[]{:S(2)}, u32[]{:S(2)}) collective-permute-start(bf16[2,64,1536]{2,1,0:T(8,128)(2,1)} %collective-permute-done.26.refs_30_), channel_id=1, source_target_pairs={{0,16},{16,0},{32,48},{48,32},{64,80},{80,64},{96,112},{112,96},{1... | collective-permute-start | bytes 1179656 | tf_op jit(solution)/shard_map/ppermute | solution.py:193
  123.7 7.8 %collective-permute-start.9 = (bf16[64,1536]{1,0:T(8,128)(2,1)}, bf16[64,1536]{1,0:T(8,128)(2,1)}, u32[]{:S(2)}, u32[]{:S(2)}) collective-permute-start(bf16[64,1536]{1,0:T(8,128)(2,1)} %slice.47), channel_id=1, source_target_pairs={{0,12},{1,13},{2,14},{3,15},{4,0},{5,1},{6,2},{7,3},{8,4},{9,5},{1... | collective-permute-start | bytes 589832 | tf_op jit(solution)/shard_map/ppermute | solution.py:176
  189.9 18.9 %all-to-all-start.2 = ((f32[256,1,128]{2,1,0:T(1,128)}), f32[256,1,128]{2,1,0:T(1,128)S(1)}, u32[]{:S(2)}, u32[]{:S(2)}) async-start(f32[256,1,128]{2,1,0:T(1,128)} %bitcast.11), calls=%async_computation.2 | async-start | bytes 262144 | tf_op jit(solution)/shard_map/all_to_all | solution.py:163
  (43 other events, 389.5 us)

commit v3 on v1

--- a/solution.py
+++ b/solution.py
@@ -1,5 +1,6 @@
 import jax
 import jax.numpy as jnp
+import numpy as np
 from jax import lax
 from jax.experimental import pallas as pl
 from jax.experimental.pallas import tpu as pltpu
@@ -9,7 +10,8 @@
 GROUP = 4
 AXES = ("row", "col")
 LANES = 128
-VMEM_BYTES = 40 * 1024 * 1024
+LARGE = 58 * 1024 * 1024
+SMALL = 8 * 1024 * 1024
 
 
 def spread_columns(values, out_ref):
@@ -32,68 +34,111 @@
         out_ref[at, :] = out_ref[at, :] + jnp.sum(col_acc[b], axis=0, keepdims=True)
 
 
-def add_tile(kernel, slot, vec_ref, spread_ref, row_acc, col_acc, where, pairs, listed, n_col):
+def split3(value):
+    high = value.astype(jnp.bfloat16)
+    rest = value - high.astype(jnp.float32)
+    middle = rest.astype(jnp.bfloat16)
+    return high, middle, (rest - middle.astype(jnp.float32)).astype(jnp.bfloat16)
+
+
+def pack_kernel(features_ref, targets_ref, out_ref):
+    width = features_ref.shape[1]
+    wide = features_ref[...].astype(jnp.float32)
+    norm = jnp.broadcast_to(jnp.sum(wide * wide, axis=1, keepdims=True), (LANES, LANES))
+    target = jnp.transpose(jnp.broadcast_to(targets_ref[...], (LANES, LANES)))
+    lane = lax.broadcasted_iota(jnp.int32, (LANES, LANES), 1)
+    extra = jnp.zeros((LANES, LANES), jnp.float32)
+    for k, part in enumerate(split3(target) + split3(norm)):
+        extra = jnp.where(lane == k, part.astype(jnp.float32), extra)
+    out_ref[:, 0:width] = features_ref[...]
+    out_ref[:, width : width + LANES] = extra.astype(jnp.bfloat16)
+
+
+def add_tile(kernel, slot, spread, across, row_acc, col_acc, where, pairs, listed, n_col):
     row_index, col_index = where
     a = pairs[slot, 0]
     b = pairs[slot, 1]
-    j = b * n_col + col_index
     live = jnp.where(slot < listed, 1.0, 0.0)
-    other = jnp.where(row_index * n_col + a == j, 0.0, live)
-    both = kernel * (spread_ref[a] + vec_ref[pl.ds(j, 1), :])
+    other = jnp.where(row_index * n_col + a == b * n_col + col_index, 0.0, live)
+    both = kernel * (spread + across)
     row_acc[a] = row_acc[a] + both * live
     col_acc[b] = col_acc[b] + jnp.sum(both.reshape(16, 8, LANES), axis=0) * other
 
 
 def first_sweep_kernel(
-    place, pairs, count, rows_ref, cols_ref, known_ref, kernel_ref, out_ref,
-    vec, norms, spread_v, spread_n, row_acc, col_acc,
+    row_plan, col_plan, width, place, pairs, count, row_spot, col_spot, *rest
 ):
+    n_pieces = len(row_plan) + len(col_plan)
+    pieces = rest[:n_pieces]
+    (kernel_ref, out_ref, held, held_sems, rows_ref, cols_ref, sems, vec, norms,
+     spread_v, spread_n, row_acc, col_acc) = rest[n_pieces:]
     n_col = rows_ref.shape[0]
     n_row = cols_ref.shape[0]
-    width = rows_ref.shape[2]
+    copies = []
+    for k, taken in enumerate(row_plan + col_plan):
+        target = rows_ref if k < len(row_plan) else cols_ref
+        for index, part in taken:
+            source = pieces[k] if part is None else pieces[k].at[part]
+            copy = pltpu.make_async_copy(source, target.at[index], sems.at[len(copies)])
+            copy.start()
+            copies.append(copy)
     row_index = place[0]
     col_index = place[1]
     listed = count[0]
-    first = pl.multiple_of(row_index * n_col, n_col)
-    vec[...] = known_ref[:, 0:LANES]
-    norms[...] = known_ref[:, LANES : 2 * LANES]
-    spread_columns(vec[pl.ds(first, n_col), :], spread_v)
-    spread_columns(norms[pl.ds(first, n_col), :], spread_n)
     row_acc[...] = jnp.zeros_like(row_acc)
     col_acc[...] = jnp.zeros_like(col_acc)
+    for copy in copies:
+        copy.wait()
+    for k in range(n_col):
+        extra = rows_ref[k, :, width : width + LANES].astype(jnp.float32)
+        value = extra[:, 0:1] + (extra[:, 1:2] + extra[:, 2:3])
+        spread_v[k] = jnp.broadcast_to(value, (LANES, LANES))
+        value = extra[:, 3:4] + (extra[:, 4:5] + extra[:, 5:6])
+        spread_n[k] = jnp.broadcast_to(value, (LANES, LANES))
+    for k in range(n_row):
+        extra = jnp.transpose(cols_ref[k, :, width : width + LANES].astype(jnp.float32))
+        vec[k : k + 1, :] = extra[0:1, :] + (extra[1:2, :] + extra[2:3, :])
+        norms[k : k + 1, :] = extra[3:4, :] + (extra[4:5, :] + extra[5:6, :])
 
     def step(turn, carry):
         for g in range(GROUP):
             slot = turn * GROUP + g
-            a = pairs[slot, 0]
-            b = pairs[slot, 1]
+            a = row_spot[pairs[slot, 0]]
+            b = col_spot[pairs[slot, 1]]
             inner = lax.dot_general(
-                rows_ref[a], cols_ref[b], (((1,), (1,)), ((), ())),
+                rows_ref[a, :, 0:width], cols_ref[b, :, 0:width], (((1,), (1,)), ((), ())),
                 preferred_element_type=jnp.float32,
             )
-            norm_j = norms[pl.ds(b * n_col + col_index, 1), :]
-            distance = spread_n[a] + norm_j - 2.0 * inner
+            distance = spread_n[a] + norms[pl.ds(b, 1), :] - 2.0 * inner
             kernel = jnp.exp(jnp.maximum(distance, 0.0) * (-1.0 / width))
-            kernel_ref[slot] = kernel
+            held[slot] = kernel
             add_tile(
-                kernel, slot, vec, spread_v, row_acc, col_acc,
+                kernel, slot, spread_v[a], vec[pl.ds(b, 1), :], row_acc, col_acc,
                 (row_index, col_index), pairs, listed, n_col,
             )
         return carry
 
     lax.fori_loop(0, pairs.shape[0] // GROUP, step, 0)
+    save = pltpu.make_async_copy(held, kernel_ref, held_sems.at[0])
+    save.start()
     write_slots(row_acc, col_acc, row_index, col_index, n_row, n_col, out_ref)
+    save.wait()
 
 
 def second_sweep_kernel(
-    place, pairs, count, kernel_ref, start_ref, image_ref, out_ref, own_ref,
-    next_dir, sums, spread_v, row_acc, col_acc, *, n_row, n_col,
+    place, pairs, count, kernel_ref, known_ref, out_ref, own_ref,
+    held, held_sems, start_ref, image_ref, next_dir, sums, spread_v, row_acc, col_acc,
+    *, n_row, n_col,
 ):
+    fetch = pltpu.make_async_copy(kernel_ref, held, held_sems.at[0])
+    fetch.start()
     row_index = place[0]
     col_index = place[1]
     listed = count[0]
-    start = start_ref[...]
-    image = image_ref[...]
+    image = known_ref[:, 0:LANES]
+    start = known_ref[:, LANES : 2 * LANES]
+    image_ref[...] = image
+    start_ref[...] = start
     norm_0 = jnp.sum(start * start)
     alpha = norm_0 / jnp.sum(start * image)
     residual = start - alpha * image
@@ -105,11 +150,15 @@
     row_acc[...] = jnp.zeros_like(row_acc)
     col_acc[...] = jnp.zeros_like(col_acc)
 
+    fetch.wait()
+
     def step(turn, carry):
         for g in range(GROUP):
             slot = turn * GROUP + g
+            j = pairs[slot, 1] * n_col + col_index
             add_tile(
-                kernel_ref[slot], slot, next_dir, spread_v, row_acc, col_acc,
+                held[slot], slot, spread_v[pairs[slot, 0]], next_dir[pl.ds(j, 1), :],
+                row_acc, col_acc,
                 (row_index, col_index), pairs, listed, n_col,
             )
         return carry
@@ -133,7 +182,8 @@
 def image_kernel(place, partial_ref, own_ref, out_ref, *, block):
     total = jnp.sum(partial_ref[...], axis=0, keepdims=True)
     image = RIDGE * own_ref[...] + total * (1.0 / block)
-    out_ref[...] = jnp.broadcast_to(image, out_ref.shape)
+    both = jnp.concatenate([image, own_ref[...]], axis=1)
+    out_ref[...] = jnp.broadcast_to(both, out_ref.shape)
 
 
 def finish_kernel(partial_ref, own_ref, solution_ref, residual_ref, *, block):
@@ -152,6 +202,114 @@
 
 VM = pl.BlockSpec(memory_space=pltpu.VMEM)
 SM = pl.BlockSpec(memory_space=pltpu.SMEM)
+HB = pl.BlockSpec(memory_space=pltpu.HBM)
+NX, NZ = 4, 4
+NY, NH, NK = 4, 2, 2
+
+
+def coords(device):
+    row, col = divmod(device, NX * NZ)
+    return row // 4, row // 2 % 2, row % 2, col // NZ, col % NZ
+
+
+def device_at(y, half, core, x, z):
+    return ((y % NY * NH + half) * NK + core) * NX * NZ + x % NX * NZ + z
+
+
+def send(array, move):
+    pairs = [(d, device_at(*move(*coords(d)))) for d in range(NY * NH * NK * NX * NZ)]
+    return lax.ppermute(array, AXES, pairs)
+
+
+def along_z(array, bit, only=range(NZ)):
+    pairs = []
+    for d in range(NY * NH * NK * NX * NZ):
+        y, h, k, x, z = coords(d)
+        if z in only:
+            pairs.append((d, device_at(y, h, k, x, z ^ bit)))
+    return lax.ppermute(array, AXES, pairs)
+
+
+def along_x(array, step):
+    return send(array, lambda y, h, k, x, z: (y, h, k, x + (step if k == 0 else -step), z))
+
+
+def along_y(array, step):
+    return send(array, lambda y, h, k, x, z: (y + (step if k == 0 else -step), h, k, x, z))
+
+
+def across(array):
+    return send(array, lambda y, h, k, x, z: (y, 1 - h, k, x, z))
+
+
+def sibling(array):
+    return send(array, lambda y, h, k, x, z: (y, h, 1 - k, x, z))
+
+
+def together(*arrays):
+    return lax.optimization_barrier(arrays[::-1])[::-1]
+
+
+def gather(mine):
+    z = lax.axis_index("col") % NZ
+    middle = (z == 1) | (z == 2)
+    inside = (1, 2)
+    half = mine.shape[0] // 2
+
+    one, two = along_x(mine, 1), along_x(mine, -1)
+    z1, inner = along_z(mine, 1), along_z(mine, 3, inside)
+    over_low = across(mine[:half])
+    one, two, z1, inner, over_low = together(one, two, z1, inner, over_low)
+
+    one1, two1, far = along_x(z1, 1), along_x(z1, -1), along_x(one, 1)
+    over_high = across(mine[half:])
+    inner2, outer = along_z(z1, 3, inside), along_z(inner, 1, inside)
+    one1, two1, far, over_high, inner2, outer = together(
+        one1, two1, far, over_high, inner2, outer
+    )
+
+    pair = jnp.stack([mine, jnp.concatenate([over_low, over_high])])
+    z2 = jnp.where(middle, inner, outer)
+    one2, two2, far1 = along_x(z2, 1), along_x(z2, -1), along_x(one1, 1)
+    near, back = along_y(pair, 1), along_y(pair, -1)
+    outer2 = along_z(inner2, 1, inside)
+    one2, two2, far1, near, back, outer2 = together(one2, two2, far1, near, back, outer2)
+
+    z3 = jnp.where(middle, inner2, outer2)
+    one3, two3, far2 = along_x(z3, 1), along_x(z3, -1), along_x(one2, 1)
+    rim = along_y(near, 1)
+    twin = sibling(jnp.concatenate([pair, near, back]))
+    one3, two3, far2, rim, twin = together(one3, two3, far2, rim, twin)
+
+    far3, rim_twin = together(along_x(one3, 1), sibling(rim))
+
+    rows = [mine, one, far, two, z1, one1, far1, two1, z2, one2, far2, two2, z3, one3, far3, two3]
+    row_plan = [((NZ * turn + m, None),) for m in range(NZ) for turn in range(NX)]
+    cols = [pair, near, rim, back, twin, rim_twin]
+    col_plan = [((turn, 0), (4 + turn, 1)) for turn in range(NY)]
+    col_plan += [
+        ((8, 0), (12, 1), (9, 2), (13, 3), (11, 4), (15, 5)), ((10, 0), (14, 1)),
+    ]
+    return rows, row_plan, cols, col_plan
+
+
+def spots():
+    total = NY * NH * NK * NX * NZ
+    row_spot = np.zeros((total, NX * NZ), np.int32)
+    col_spot = np.zeros((total, NY * NH * NK), np.int32)
+    for d in range(total):
+        y, h, k, x, z = coords(d)
+        sign = 1 if k == 0 else -1
+        order = [z, z ^ 1, z ^ 3, z ^ 2] if z in (1, 2) else [z, z ^ 1, z ^ 2, z ^ 3]
+        for a in range(NX * NZ):
+            turn = sign * (x - a // NZ) % NX
+            row_spot[d, a] = NZ * turn + order.index(a % NZ)
+        for b in range(NY * NH * NK):
+            swap_k = (b ^ k) & 1
+            turn = (-sign if swap_k else sign) * (y - b // 4) % NY
+            col_spot[d, b] = 8 * swap_k + 4 * ((b // 2 ^ h) & 1) + turn
+    here = lax.axis_index("row") * NX * NZ + lax.axis_index("col")
+    return jnp.asarray(row_spot)[here], jnp.asarray(col_spot)[here]
 
 
 def body(features, targets, tile_pairs, tile_count):
@@ -163,37 +321,46 @@
     count = tile_count[0]
     slots = pairs.shape[0]
     block, width = features.shape
-    params = pltpu.CompilerParams(vmem_limit_bytes=VMEM_BYTES)
+    params = pltpu.CompilerParams(vmem_limit_bytes=SMALL)
     f32 = jnp.float32
 
-    wide = features.astype(f32)
-    norms = jnp.sum(wide * wide, axis=1)
-    mine = jnp.concatenate([targets, norms])[None, :]
-    known = swap(jnp.broadcast_to(mine, (total, 2 * block)))
-
-    rows = lax.all_gather(features, "col", axis=0).reshape(n_col, block, width)
-    cols = lax.all_gather(features, "row", axis=0).reshape(n_row, block, width)
+    packed = pl.pallas_call(
+        pack_kernel,
+        out_shape=jax.ShapeDtypeStruct((block, width + LANES), jnp.bfloat16),
+        in_specs=[VM, VM],
+        out_specs=VM,
+        compiler_params=params,
+    )(features, targets[None, :])
+    row_pieces, row_plan, col_pieces, col_plan = gather(packed)
+    row_spot, col_spot = spots()
 
     accumulators = [
         pltpu.VMEM((n_col, block, block), f32),
         pltpu.VMEM((n_row, 8, block), f32),
     ]
     kernel, partial = pl.pallas_call(
-        first_sweep_kernel,
+        lambda *refs: first_sweep_kernel(row_plan, col_plan, width, *refs),
         out_shape=(
             jax.ShapeDtypeStruct((slots, block, block), f32),
             jax.ShapeDtypeStruct((total, block), f32),
         ),
-        in_specs=[SM, SM, SM, VM, VM, VM],
-        out_specs=(VM, VM),
-        scratch_shapes=[pltpu.VMEM((total, block), f32)] * 2
+        in_specs=[SM, SM, SM, SM, SM] + [HB] * (len(row_plan) + len(col_plan)),
+        out_specs=(HB, VM),
+        scratch_shapes=[
+            pltpu.VMEM((slots, block, block), f32),
+            pltpu.SemaphoreType.DMA((1,)),
+            pltpu.VMEM((n_col, block, width + LANES), jnp.bfloat16),
+            pltpu.VMEM((n_row, block, width + LANES), jnp.bfloat16),
+        ]
+        + [pltpu.SemaphoreType.DMA((sum(len(taken) for taken in row_plan + col_plan),))]
+        + [pltpu.VMEM((n_row, block), f32)] * 2
         + [pltpu.VMEM((n_col, block, block), f32)] * 2 + accumulators,
-        compiler_params=params,
-    )(place, pairs, count, rows, cols, known)
+        compiler_params=pltpu.CompilerParams(vmem_limit_bytes=LARGE),
+    )(place, pairs, count, row_spot, col_spot, *row_pieces, *col_pieces)
 
     image = pl.pallas_call(
         lambda *refs: image_kernel(None, *refs, block=block),
-        out_shape=jax.ShapeDtypeStruct((total, block), f32),
+        out_shape=jax.ShapeDtypeStruct((total, 2 * block), f32),
         in_specs=[VM, VM],
         out_specs=VM,
         compiler_params=params,
@@ -206,15 +373,19 @@
             jax.ShapeDtypeStruct((total, 2 * block), f32),
             jax.ShapeDtypeStruct((8, block), f32),
         ),
-        in_specs=[SM, SM, SM, VM, VM, VM],
+        in_specs=[SM, SM, SM, HB, VM],
         out_specs=(VM, VM),
         scratch_shapes=[
+            pltpu.VMEM((slots, block, block), f32),
+            pltpu.SemaphoreType.DMA((1,)),
+            pltpu.VMEM((total, block), f32),
+            pltpu.VMEM((total, block), f32),
             pltpu.VMEM((total, block), f32),
             pltpu.VMEM((total, block), f32),
             pltpu.VMEM((n_col, block, block), f32),
         ] + accumulators,
         compiler_params=params,
-    )(place, pairs, count, kernel, known[:, 0:block], images)
+    )(place, pairs, count, kernel, images)
 
     result, residual = pl.pallas_call(
         lambda *refs: finish_kernel(*refs, block=block),

time: 337 us -> 197 us (0.58)
  waiting for transfers between devices: 237 us -> 55.8 us
  blocking collectives: 43.8 us -> 68.2 us
  starting transfers between devices: 21.7 us -> 42.8 us
  between operations: 14.7 us -> 1.69 us
  Pallas kernels: 13 us -> 19.8 us
    all_gather x2 -> x0, waiting for transfers between devices: 205 us -> none  [the longest x1 140 us: body(): rows = lax.all_gather(features, 'col', axis=0).reshape(n_col, block, width)]
    ppermute x0 -> x24, waiting for transfers between devices: none -> 55.8 us  [the longest x19 38.3 us: send(): return lax.ppermute(array, AXES, pairs)]
    ppermute x0 -> x24, starting transfers between devices: none -> 42.8 us  [the longest x19 37.2 us: send(): return lax.ppermute(array, AXES, pairs)]
    all_to_all x2 -> x0, waiting for transfers between devices: 31 us -> none  [swap(): return lax.all_to_all(slots, AXES, 0, 0, tiled=True)]
    all_to_all x2 -> x3, blocking collectives: 43.8 us -> 68.2 us  [swap(): return lax.all_to_all(slots, AXES, 0, 0, tiled=True)]
    all_to_all x2 -> x0, starting transfers between devices: 21.6 us -> none  [swap(): return lax.all_to_all(slots, AXES, 0, 0, tiled=True)]
    pallas_call x1 -> x2, Pallas kernels: 9 us -> 16.3 us  [the longest x1 16 us: body(): pl.pallas_call(lambda *refs: first_sweep_kernel(row_plan, col_plan, width...]
  transfers between devices with their start and end apart: 4 -> 24, of which waited for: 4 -> 12; matrix products, arithmetic and copies ran while one was open for 1% -> 2% of each run, Pallas kernels for 0% -> 0%
where the time goes in v3:
time: 197 us
  blocking collectives  68.2 us (35%)
  waiting for transfers between devices  55.8 us (28%)
  starting transfers between devices  42.8 us (22%)
  Pallas kernels  19.8 us (10%)
  local copies, waits for them, and re-layouts  6.31 us (3%)
  other arithmetic  2.3 us (1%)
    all_to_all x3, blocking collectives, swap(): return lax.all_to_all(slots, AXES, 0, 0, tiled=True)  68.2 us
    ppermute x19, waiting for transfers between devices, send(): return lax.ppermute(array, AXES, pairs)  38.3 us
    ppermute x19, starting transfers between devices, send(): return lax.ppermute(array, AXES, pairs)  37.2 us
    ppermute x5, waiting for transfers between devices, along_z(): return lax.ppermute(array, AXES, pairs)  17.5 us
    pallas_call x1, Pallas kernels, body(): pl.pallas_call(lambda *refs: first_sweep_kernel(row_plan, col_plan, width...  16 us
    ppermute x5, starting transfers between devices, along_z(): return lax.ppermute(array, AXES, pairs)  5.55 us
  transfers between devices with their start and end apart: 24, of which 12 were waited for; matrix products, arithmetic and copies ran while one was open for 2% of the time, Pallas kernels for 0%

profile of v3, /device:TPU:1, one launch (start us, length us, event | category | flops | bytes accessed | tf_op | source)
XLA Modules:
  0.0 196.8 jit_solution(4597977640767248367)
XLA Ops:
  2.5 3.4 %collective-permute-start.4 = (bf16[128,1664]{1,0:T(8,128)(2,1)S(1)}, bf16[128,1664]{1,0:T(8,128)(2,1)S(1)}, u32[]{:S(2)}, u32[]{:S(2)}) collective-permute-start(bf16[128,1664]{1,0:T(8,128)(2,1)S(1)} %shard_map.77.refs_5_), channel_id=1, source_target_pairs={{0,4},{1,5},{2,6},{3,7},{4,8},{5,9},{6,10},{7,11},{8,12},{9,13},{1... | collective-permute-start | bytes 1277960 | tf_op jit(solution)/shard_map/ppermute | solution.py:221
  5.9 1.6 collective-permute-start.2
  8.3 6.1 %collective-permute-start = (bf16[64,1664]{1,0:T(8,128)(2,1)S(1)}, bf16[64,1664]{1,0:T(8,128)(2,1)S(1)}, u32[]{:S(2)}, u32[]{:S(2)}) collective-permute-start(bf16[64,1664]{1,0:T(8,128)(2,1)S(1)} %get-tuple-element.63), channel_id=1, source_target_pairs={{0,32},{1,33},{2,34},{3,35},{4,36},{5,37},{6,38},{7,39},{8,40},{9,... | collective-permute-start | bytes 638984 | tf_op jit(solution)/shard_map/ppermute | solution.py:221
  14.4 13.0 %collective-permute-done = bf16[64,1664]{1,0:T(8,128)(2,1)S(1)} collective-permute-done((bf16[64,1664]{1,0:T(8,128)(2,1)S(1)}, bf16[64,1664]{1,0:T(8,128)(2,1)S(1)}, u32[]{:S(2)}, u32[]{:S(2)}) %collective-permute-start) | collective-permute-done | bytes 213024 | tf_op jit(solution)/shard_map/ppermute | solution.py:221
  28.1 3.4 %collective-permute-start.8 = (bf16[128,1664]{1,0:T(8,128)(2,1)S(1)}, bf16[128,1664]{1,0:T(8,128)(2,1)S(1)}, u32[]{:S(2)}, u32[]{:S(2)}) collective-permute-start(bf16[128,1664]{1,0:T(8,128)(2,1)S(1)} %collective-permute-done.4.refs_6_), channel_id=1, source_target_pairs={{0,4},{1,5},{2,6},{3,7},{4,8},{5,9},{6,10},{7,11},{8,12},{9,13},{1... | collective-permute-start | bytes 1277960 | tf_op jit(solution)/shard_map/ppermute | solution.py:221
  31.5 1.3 collective-permute-start.5
  32.9 1.4 collective-permute-start.9
  34.4 1.9 collective-permute-done.7
  37.0 13.1 %collective-permute-done.5 = bf16[128,1664]{1,0:T(8,128)(2,1)S(1)} collective-permute-done((bf16[128,1664]{1,0:T(8,128)(2,1)S(1)}, bf16[128,1664]{1,0:T(8,128)(2,1)S(1)}, u32[]{:S(2)}, u32[]{:S(2)}) %collective-permute-start.5) | collective-permute-done | bytes 426016 | tf_op jit(solution)/shard_map/ppermute | solution.py:230
  50.2 1.1 collective-permute-start.16
  51.3 1.1 maximum_bitcast_fusion
  52.4 2.8 %collective-permute-start.13 = (bf16[2,128,1664]{2,1,0:T(8,128)(2,1)S(1)}, bf16[2,128,1664]{2,1,0:T(8,128)(2,1)S(1)}, u32[]{:S(2)}, u32[]{:S(2)}) collective-permute-start(bf16[2,128,1664]{2,1,0:T(8,128)(2,1)S(1)} %pad_maximum_fusion.1.refs_21_), channel_id=1, source_target_pairs={{0,64},{1,65},{2,66},{3,67},{4,68},{5,69},{6,70},{7,71},{8,72},{9,... | collective-permute-start | bytes 2555912 | tf_op jit(solution)/shard_map/ppermute | solution.py:221
  55.7 2.2 %collective-permute-start.14 = (bf16[128,1664]{1,0:T(8,128)(2,1)}, bf16[128,1664]{1,0:T(8,128)(2,1)S(1)}, u32[]{:S(2)}, u32[]{:S(2)}) collective-permute-start(bf16[128,1664]{1,0:T(8,128)(2,1)} %collective-permute-done.10.refs_10_), channel_id=1, source_target_pairs={{0,4},{1,5},{2,6},{3,7},{4,8},{5,9},{6,10},{7,11},{8,12},{9,13},{1... | collective-permute-start | bytes 1277960 | tf_op jit(solution)/shard_map/ppermute | solution.py:221
  57.9 1.3 collective-permute-start.11
  59.2 6.2 %collective-permute-done.15.refs_16_ = bf16[128,1664]{1,0:T(8,128)(2,1)S(1)} collective-permute-done((bf16[128,1664]{1,0:T(8,128)(2,1)S(1)}, bf16[128,1664]{1,0:T(8,128)(2,1)S(1)}, u32[]{:S(2)}, u32[]{:S(2)}) %collective-permute-start.15) | collective-permute-done | bytes 426016 | tf_op jit(solution)/shard_map/ppermute | solution.py:221
  65.5 2.2 %collective-permute-done.14.refs_11_ = bf16[128,1664]{1,0:T(8,128)(2,1)S(1)} collective-permute-done((bf16[128,1664]{1,0:T(8,128)(2,1)}, bf16[128,1664]{1,0:T(8,128)(2,1)S(1)}, u32[]{:S(2)}, u32[]{:S(2)}) %collective-permute-start.14) | collective-permute-done | bytes 426016 | tf_op jit(solution)/shard_map/ppermute | solution.py:221
  67.7 4.4 %collective-permute-done.11 = bf16[128,1664]{1,0:T(8,128)(2,1)S(1)} collective-permute-done((bf16[128,1664]{1,0:T(8,128)(2,1)S(1)}, bf16[128,1664]{1,0:T(8,128)(2,1)S(1)}, u32[]{:S(2)}, u32[]{:S(2)}) %collective-permute-start.11) | collective-permute-done | bytes 426016 | tf_op jit(solution)/shard_map/ppermute | solution.py:230
  72.1 1.6 collective-permute-done.13.refs_22_
  75.6 2.5 %collective-permute-start.17 = (bf16[6,128,1664]{2,1,0:T(8,128)(2,1)S(1)}, bf16[6,128,1664]{2,1,0:T(8,128)(2,1)}, u32[]{:S(2)}, u32[]{:S(2)}) collective-permute-start(bf16[6,128,1664]{2,1,0:T(8,128)(2,1)S(1)} %pad_maximum_fusion), channel_id=1, source_target_pairs={{0,16},{1,17},{2,18},{3,19},{4,20},{5,21},{6,22},{7,23},{8,24},{9,... | collective-permute-start | bytes 7667720 | tf_op jit(solution)/shard_map/ppermute | solution.py:221
  78.1 2.7 %collective-permute-start.18 = (bf16[2,128,1664]{2,1,0:T(8,128)(2,1)S(1)}, bf16[2,128,1664]{2,1,0:T(8,128)(2,1)S(1)}, u32[]{:S(2)}, u32[]{:S(2)}) collective-permute-start(bf16[2,128,1664]{2,1,0:T(8,128)(2,1)S(1)} %collective-permute-done.13.refs_22_), channel_id=1, source_target_pairs={{0,64},{1,65},{2,66},{3,67},{4,68},{5,69},{6,70},{7,71},{8,72},{9,... | collective-permute-start | bytes 2555912 | tf_op jit(solution)/shard_map/ppermute | solution.py:221
  80.9 4.9 %collective-permute-start.21 = (bf16[128,1664]{1,0:T(8,128)(2,1)S(1)}, bf16[128,1664]{1,0:T(8,128)(2,1)S(1)}, u32[]{:S(2)}, u32[]{:S(2)}) collective-permute-start(bf16[128,1664]{1,0:T(8,128)(2,1)S(1)} %broadcast_select_fusion.refs_17_), channel_id=1, source_target_pairs={{0,4},{1,5},{2,6},{3,7},{4,8},{5,9},{6,10},{7,11},{8,12},{9,13},{1... | collective-permute-start | bytes 1277960 | tf_op jit(solution)/shard_map/ppermute | solution.py:221
  85.8 2.7 %collective-permute-start.19 = (bf16[128,1664]{1,0:T(8,128)(2,1)S(1)}, bf16[128,1664]{1,0:T(8,128)(2,1)S(1)}, u32[]{:S(2)}, u32[]{:S(2)}) collective-permute-start(bf16[128,1664]{1,0:T(8,128)(2,1)S(1)} %collective-permute-done.16.refs_14_), channel_id=1, source_target_pairs={{0,4},{1,5},{2,6},{3,7},{4,8},{5,9},{6,10},{7,11},{8,12},{9,13},{1... | collective-permute-start | bytes 1277960 | tf_op jit(solution)/shard_map/ppermute | solution.py:221
  88.5 6.0 %collective-permute-done.21.refs_18_ = bf16[128,1664]{1,0:T(8,128)(2,1)S(1)} collective-permute-done((bf16[128,1664]{1,0:T(8,128)(2,1)S(1)}, bf16[128,1664]{1,0:T(8,128)(2,1)S(1)}, u32[]{:S(2)}, u32[]{:S(2)}) %collective-permute-start.21) | collective-permute-done | bytes 426016 | tf_op jit(solution)/shard_map/ppermute | solution.py:221
  94.5 4.5 %collective-permute-done.20.refs_20_ = bf16[128,1664]{1,0:T(8,128)(2,1)S(1)} collective-permute-done((bf16[128,1664]{1,0:T(8,128)(2,1)S(1)}, bf16[128,1664]{1,0:T(8,128)(2,1)S(1)}, u32[]{:S(2)}, u32[]{:S(2)}) %collective-permute-start.20) | collective-permute-done | bytes 426016 | tf_op jit(solution)/shard_map/ppermute | solution.py:221
  100.0 2.4 %collective-permute-start.23 = (bf16[128,1664]{1,0:T(8,128)(2,1)S(1)}, bf16[128,1664]{1,0:T(8,128)(2,1)}, u32[]{:S(2)}, u32[]{:S(2)}) collective-permute-start(bf16[128,1664]{1,0:T(8,128)(2,1)S(1)} %collective-permute-done.21.refs_18_), channel_id=1, source_target_pairs={{0,4},{1,5},{2,6},{3,7},{4,8},{5,9},{6,10},{7,11},{8,12},{9,13},{1... | collective-permute-start | bytes 1277960 | tf_op jit(solution)/shard_map/ppermute | solution.py:221
  104.3 1.2 dynamic-slice_bitcast_fusion
  105.6 1.8 collective-permute-done.23.refs_19_
  108.4 16.0 %shard_map.78 = (f32[32,128,128]{2,1,0:T(8,128)}, f32[256,128]{1,0:T(8,128)}) custom-call(s32[2]{0:T(128)} %pad_add_fusion.refs_0_, s32[32,2]{1,0:T(8,128)} %copy.13.refs_1_, s32[1]{0:T(128)} %bitcast.26.refs_2_, s32[16]{0:T(128)} %get-tuple-element.65.refs_3_, s32[16]{0:T(128)} %get-tuple-element.64.refs_4_, bf16[128,1664]{1,0:T(8,128)(2,1)} %copy-done, ...), custom_call_target="tpu_custom_call" | custom-call | tf_op jit(solution)/shard_map/pallas_call | solution.py:341
  124.4 25.4 %all_to_all.33 = f32[256,1,128]{2,1,0:T(1,128)S(1)} all-to-all(f32[256,1,128]{2,1,0:T(1,128)} %bitcast.37), channel_id=1, replica_groups=mesh['row'=16,'col'=16] {'row','col'}, dimensions={0} | all-to-all | bytes 262144 | tf_op jit(solution)/shard_map/all_to_all | solution.py:200
  150.2 21.5 %all_to_all.34 = f32[256,1,256]{2,1,0:T(1,128)S(1)} all-to-all(f32[256,1,256]{2,1,0:T(1,128)S(1)} %copy.12), channel_id=1, replica_groups=mesh['row'=16,'col'=16] {'row','col'}, dimensions={0} | all-to-all | bytes 524288 | tf_op jit(solution)/shard_map/all_to_all | solution.py:200
  171.7 2.9 %shard_map.80 = (f32[256,256]{1,0:T(8,128)S(1)}, f32[8,128]{1,0:T(8,128)S(1)}) custom-call(s32[2]{0:T(128)S(1)} %copy-done.4, s32[32,2]{1,0:T(8,128)S(1)} %copy-done.3, s32[1]{0:T(128)} %bitcast.27.refs_2_, f32[32,128,128]{2,1,0:T(8,128)S(1)} %copy-done.1, f32[256,256]{1,0:T(8,128)S(1)} %bitcast.30), custom_call_target="tpu_custom_call" | custom-call | tf_op jit(solution)/shard_map/pallas_call | solution.py:370
  174.9 21.3 %all_to_all.35 = f32[256,1,256]{2,1,0:T(1,128)S(1)} all-to-all(f32[256,1,256]{2,1,0:T(1,128)S(1)} %copy.14), channel_id=1, replica_groups=mesh['row'=16,'col'=16] {'row','col'}, dimensions={0} | all-to-all | bytes 524288 | tf_op jit(solution)/shard_map/all_to_all | solution.py:200
  (89 shorter events, 11.0 us)
Async XLA Ops:
  2.5 72.4 %copy-start = (bf16[128,1664]{1,0:T(8,128)(2,1)}, bf16[128,1664]{1,0:T(8,128)(2,1)S(1)}, u32[]{:S(2)}) copy-start(bf16[128,1664]{1,0:T(8,128)(2,1)S(1)} %shard_map.77.refs_5_) | copy-start | bytes 1277956
  2.5 24.9 %collective-permute-start.4 = (bf16[128,1664]{1,0:T(8,128)(2,1)S(1)}, bf16[128,1664]{1,0:T(8,128)(2,1)S(1)}, u32[]{:S(2)}, u32[]{:S(2)}) collective-permute-start(bf16[128,1664]{1,0:T(8,128)(2,1)S(1)} %shard_map.77.refs_5_), channel_id=1, source_target_pairs={{0,4},{1,5},{2,6},{3,7},{4,8},{5,9},{6,10},{7,11},{8,12},{9,13},{1... | collective-permute-start | bytes 1277960 | tf_op jit(solution)/shard_map/ppermute | solution.py:221
  5.9 21.5 %collective-permute-start.3 = (bf16[128,1664]{1,0:T(8,128)(2,1)S(1)}, bf16[128,1664]{1,0:T(8,128)(2,1)S(1)}, u32[]{:S(2)}, u32[]{:S(2)}) collective-permute-start(bf16[128,1664]{1,0:T(8,128)(2,1)S(1)} %shard_map.77.refs_5_), channel_id=1, source_target_pairs={{0,12},{1,13},{2,14},{3,15},{4,0},{5,1},{6,2},{7,3},{8,4},{9,5},{1... | collective-permute-start | bytes 1277960 | tf_op jit(solution)/shard_map/ppermute | solution.py:221
  5.9 21.5 %collective-permute-start.2 = (bf16[128,1664]{1,0:T(8,128)(2,1)S(1)}, bf16[128,1664]{1,0:T(8,128)(2,1)S(1)}, u32[]{:S(2)}, u32[]{:S(2)}) collective-permute-start(bf16[128,1664]{1,0:T(8,128)(2,1)S(1)} %shard_map.77.refs_5_), channel_id=1, source_target_pairs={{0,1},{1,0},{2,3},{3,2},{4,5},{5,4},{6,7},{7,6},{8,9},{9,8},{10,11... | collective-permute-start | bytes 1277960 | tf_op jit(solution)/shard_map/ppermute | solution.py:230
  7.6 20.5 %collective-permute-start.1 = (bf16[128,1664]{1,0:T(8,128)(2,1)S(1)}, bf16[128,1664]{1,0:T(8,128)(2,1)S(1)}, u32[]{:S(2)}, u32[]{:S(2)}) collective-permute-start(bf16[128,1664]{1,0:T(8,128)(2,1)S(1)} %shard_map.77.refs_5_), channel_id=1, source_target_pairs={{1,2},{2,1},{5,6},{6,5},{9,10},{10,9},{13,14},{14,13},{17,18},{18,... | collective-permute-start | bytes 1277960 | tf_op jit(solution)/shard_map/ppermute | solution.py:230
  8.3 19.1 %collective-permute-start = (bf16[64,1664]{1,0:T(8,128)(2,1)S(1)}, bf16[64,1664]{1,0:T(8,128)(2,1)S(1)}, u32[]{:S(2)}, u32[]{:S(2)}) collective-permute-start(bf16[64,1664]{1,0:T(8,128)(2,1)S(1)} %get-tuple-element.63), channel_id=1, source_target_pairs={{0,32},{1,33},{2,34},{3,35},{4,36},{5,37},{6,38},{7,39},{8,40},{9,... | collective-permute-start | bytes 638984 | tf_op jit(solution)/shard_map/ppermute | solution.py:221
  27.4 8.8 %collective-permute-start.7 = (bf16[64,1664]{1,0:T(8,128)(2,1)S(1)}, bf16[64,1664]{1,0:T(8,128)(2,1)}, u32[]{:S(2)}, u32[]{:S(2)}) collective-permute-start(bf16[64,1664]{1,0:T(8,128)(2,1)S(1)} %get-tuple-element.62), channel_id=1, source_target_pairs={{0,32},{1,33},{2,34},{3,35},{4,36},{5,37},{6,38},{7,39},{8,40},{9,... | collective-permute-start | bytes 638984 | tf_op jit(solution)/shard_map/ppermute | solution.py:221
  27.4 47.5 %copy-start.14 = (bf16[128,1664]{1,0:T(8,128)(2,1)}, bf16[128,1664]{1,0:T(8,128)(2,1)S(1)}, u32[]{:S(2)}) copy-start(bf16[128,1664]{1,0:T(8,128)(2,1)S(1)} %collective-permute-done.4.refs_6_) | copy-start | bytes 1277956
  27.4 47.5 %copy-start.15 = (bf16[128,1664]{1,0:T(8,128)(2,1)}, bf16[128,1664]{1,0:T(8,128)(2,1)S(1)}, u32[]{:S(2)}) copy-start(bf16[128,1664]{1,0:T(8,128)(2,1)S(1)} %collective-permute-done.3.refs_8_) | copy-start | bytes 1277956
  28.1 46.9 %copy-start.16 = (bf16[128,1664]{1,0:T(8,128)(2,1)}, bf16[128,1664]{1,0:T(8,128)(2,1)S(1)}, u32[]{:S(2)}) copy-start(bf16[128,1664]{1,0:T(8,128)(2,1)S(1)} %collective-permute-done.2.refs_9_) | copy-start | bytes 1277956
  28.1 8.8 %collective-permute-start.8 = (bf16[128,1664]{1,0:T(8,128)(2,1)S(1)}, bf16[128,1664]{1,0:T(8,128)(2,1)S(1)}, u32[]{:S(2)}, u32[]{:S(2)}) collective-permute-start(bf16[128,1664]{1,0:T(8,128)(2,1)S(1)} %collective-permute-done.4.refs_6_), channel_id=1, source_target_pairs={{0,4},{1,5},{2,6},{3,7},{4,8},{5,9},{6,10},{7,11},{8,12},{9,13},{1... | collective-permute-start | bytes 1277960 | tf_op jit(solution)/shard_map/ppermute | solution.py:221
  31.5 18.5 %collective-permute-start.5 = (bf16[128,1664]{1,0:T(8,128)(2,1)S(1)}, bf16[128,1664]{1,0:T(8,128)(2,1)S(1)}, u32[]{:S(2)}, u32[]{:S(2)}) collective-permute-start(bf16[128,1664]{1,0:T(8,128)(2,1)S(1)} %collective-permute-done.1), channel_id=1, source_target_pairs={{1,0},{2,3},{5,4},{6,7},{9,8},{10,11},{13,12},{14,15},{17,16},{18,... | collective-permute-start | bytes 1277960 | tf_op jit(solution)/shard_map/ppermute | solution.py:230
  32.8 17.3 %collective-permute-start.10 = (bf16[128,1664]{1,0:T(8,128)(2,1)S(1)}, bf16[128,1664]{1,0:T(8,128)(2,1)}, u32[]{:S(2)}, u32[]{:S(2)}) collective-permute-start(bf16[128,1664]{1,0:T(8,128)(2,1)S(1)} %collective-permute-done.2.refs_9_), channel_id=1, source_target_pairs={{0,4},{1,5},{2,6},{3,7},{4,8},{5,9},{6,10},{7,11},{8,12},{9,13},{1... | collective-permute-start | bytes 1277960 | tf_op jit(solution)/shard_map/ppermute | solution.py:221
  32.9 17.2 %collective-permute-start.9 = (bf16[128,1664]{1,0:T(8,128)(2,1)S(1)}, bf16[128,1664]{1,0:T(8,128)(2,1)}, u32[]{:S(2)}, u32[]{:S(2)}) collective-permute-start(bf16[128,1664]{1,0:T(8,128)(2,1)S(1)} %collective-permute-done.2.refs_9_), channel_id=1, source_target_pairs={{0,12},{1,13},{2,14},{3,15},{4,0},{5,1},{6,2},{7,3},{8,4},{9,5},{1... | collective-permute-start | bytes 1277960 | tf_op jit(solution)/shard_map/ppermute | solution.py:221
  36.2 13.9 %collective-permute-start.6 = (bf16[128,1664]{1,0:T(8,128)(2,1)S(1)}, bf16[128,1664]{1,0:T(8,128)(2,1)S(1)}, u32[]{:S(2)}, u32[]{:S(2)}) collective-permute-start(bf16[128,1664]{1,0:T(8,128)(2,1)S(1)} %collective-permute-done.2.refs_9_), channel_id=1, source_target_pairs={{1,2},{2,1},{5,6},{6,5},{9,10},{10,9},{13,14},{14,13},{17,18},{18,... | collective-permute-start | bytes 1277960 | tf_op jit(solution)/shard_map/ppermute | solution.py:230
  50.2 7.8 %collective-permute-start.16 = (bf16[128,1664]{1,0:T(8,128)(2,1)S(1)}, bf16[128,1664]{1,0:T(8,128)(2,1)S(1)}, u32[]{:S(2)}, u32[]{:S(2)}) collective-permute-start(bf16[128,1664]{1,0:T(8,128)(2,1)S(1)} %broadcast_select_fusion.1.refs_13_), channel_id=1, source_target_pairs={{0,4},{1,5},{2,6},{3,7},{4,8},{5,9},{6,10},{7,11},{8,12},{9,13},{1... | collective-permute-start | bytes 1277960 | tf_op jit(solution)/shard_map/ppermute | solution.py:221
  52.4 50.6 %copy-start.25 = (s32[1,1,32,2]{2,3,1,0:T(2,128)S(1)}, s32[1,1,32,2]{2,3,1,0:T(2,128)}, u32[]{:S(2)}) copy-start(s32[1,1,32,2]{2,3,1,0:T(2,128)} %param.8) | copy-start | bytes 772
  52.4 21.3 %collective-permute-start.13 = (bf16[2,128,1664]{2,1,0:T(8,128)(2,1)S(1)}, bf16[2,128,1664]{2,1,0:T(8,128)(2,1)S(1)}, u32[]{:S(2)}, u32[]{:S(2)}) collective-permute-start(bf16[2,128,1664]{2,1,0:T(8,128)(2,1)S(1)} %pad_maximum_fusion.1.refs_21_), channel_id=1, source_target_pairs={{0,64},{1,65},{2,66},{3,67},{4,68},{5,69},{6,70},{7,71},{8,72},{9,... | collective-permute-start | bytes 2555912 | tf_op jit(solution)/shard_map/ppermute | solution.py:221
  55.3 19.3 %collective-permute-start.12 = (bf16[2,128,1664]{2,1,0:T(8,128)(2,1)S(1)}, bf16[2,128,1664]{2,1,0:T(8,128)(2,1)S(1)}, u32[]{:S(2)}, u32[]{:S(2)}) collective-permute-start(bf16[2,128,1664]{2,1,0:T(8,128)(2,1)S(1)} %pad_maximum_fusion.1.refs_21_), channel_id=1, source_target_pairs={{0,192},{1,193},{2,194},{3,195},{4,196},{5,197},{6,198},{7,199},{8... | collective-permute-start | bytes 2555912 | tf_op jit(solution)/shard_map/ppermute | solution.py:221
  55.3 10.2 %collective-permute-start.15 = (bf16[128,1664]{1,0:T(8,128)(2,1)S(1)}, bf16[128,1664]{1,0:T(8,128)(2,1)S(1)}, u32[]{:S(2)}, u32[]{:S(2)}) collective-permute-start(bf16[128,1664]{1,0:T(8,128)(2,1)S(1)} %broadcast_select_fusion.1.refs_13_), channel_id=1, source_target_pairs={{0,12},{1,13},{2,14},{3,15},{4,0},{5,1},{6,2},{7,3},{8,4},{9,5},{1... | collective-permute-start | bytes 1277960 | tf_op jit(solution)/shard_map/ppermute | solution.py:221
  55.7 12.0 %collective-permute-start.14 = (bf16[128,1664]{1,0:T(8,128)(2,1)}, bf16[128,1664]{1,0:T(8,128)(2,1)S(1)}, u32[]{:S(2)}, u32[]{:S(2)}) collective-permute-start(bf16[128,1664]{1,0:T(8,128)(2,1)} %collective-permute-done.10.refs_10_), channel_id=1, source_target_pairs={{0,4},{1,5},{2,6},{3,7},{4,8},{5,9},{6,10},{7,11},{8,12},{9,13},{1... | collective-permute-start | bytes 1277960 | tf_op jit(solution)/shard_map/ppermute | solution.py:221
  57.9 14.2 %collective-permute-start.11 = (bf16[128,1664]{1,0:T(8,128)(2,1)S(1)}, bf16[128,1664]{1,0:T(8,128)(2,1)S(1)}, u32[]{:S(2)}, u32[]{:S(2)}) collective-permute-start(bf16[128,1664]{1,0:T(8,128)(2,1)S(1)} %collective-permute-done.6), channel_id=1, source_target_pairs={{1,0},{2,3},{5,4},{6,7},{9,8},{10,11},{13,12},{14,15},{17,16},{18,... | collective-permute-start | bytes 1277960 | tf_op jit(solution)/shard_map/ppermute | solution.py:230
  75.6 23.5 %collective-permute-start.17 = (bf16[6,128,1664]{2,1,0:T(8,128)(2,1)S(1)}, bf16[6,128,1664]{2,1,0:T(8,128)(2,1)}, u32[]{:S(2)}, u32[]{:S(2)}) collective-permute-start(bf16[6,128,1664]{2,1,0:T(8,128)(2,1)S(1)} %pad_maximum_fusion), channel_id=1, source_target_pairs={{0,16},{1,17},{2,18},{3,19},{4,20},{5,21},{6,22},{7,23},{8,24},{9,... | collective-permute-start | bytes 7667720 | tf_op jit(solution)/shard_map/ppermute | solution.py:221
  78.1 21.0 %collective-permute-start.18 = (bf16[2,128,1664]{2,1,0:T(8,128)(2,1)S(1)}, bf16[2,128,1664]{2,1,0:T(8,128)(2,1)S(1)}, u32[]{:S(2)}, u32[]{:S(2)}) collective-permute-start(bf16[2,128,1664]{2,1,0:T(8,128)(2,1)S(1)} %collective-permute-done.13.refs_22_), channel_id=1, source_target_pairs={{0,64},{1,65},{2,66},{3,67},{4,68},{5,69},{6,70},{7,71},{8,72},{9,... | collective-permute-start | bytes 2555912 | tf_op jit(solution)/shard_map/ppermute | solution.py:221
  80.9 13.6 %collective-permute-start.21 = (bf16[128,1664]{1,0:T(8,128)(2,1)S(1)}, bf16[128,1664]{1,0:T(8,128)(2,1)S(1)}, u32[]{:S(2)}, u32[]{:S(2)}) collective-permute-start(bf16[128,1664]{1,0:T(8,128)(2,1)S(1)} %broadcast_select_fusion.refs_17_), channel_id=1, source_target_pairs={{0,4},{1,5},{2,6},{3,7},{4,8},{5,9},{6,10},{7,11},{8,12},{9,13},{1... | collective-permute-start | bytes 1277960 | tf_op jit(solution)/shard_map/ppermute | solution.py:221
  85.8 13.1 %collective-permute-start.20 = (bf16[128,1664]{1,0:T(8,128)(2,1)S(1)}, bf16[128,1664]{1,0:T(8,128)(2,1)S(1)}, u32[]{:S(2)}, u32[]{:S(2)}) collective-permute-start(bf16[128,1664]{1,0:T(8,128)(2,1)S(1)} %broadcast_select_fusion.refs_17_), channel_id=1, source_target_pairs={{0,12},{1,13},{2,14},{3,15},{4,0},{5,1},{6,2},{7,3},{8,4},{9,5},{1... | collective-permute-start | bytes 1277960 | tf_op jit(solution)/shard_map/ppermute | solution.py:221
  85.8 13.2 %collective-permute-start.19 = (bf16[128,1664]{1,0:T(8,128)(2,1)S(1)}, bf16[128,1664]{1,0:T(8,128)(2,1)S(1)}, u32[]{:S(2)}, u32[]{:S(2)}) collective-permute-start(bf16[128,1664]{1,0:T(8,128)(2,1)S(1)} %collective-permute-done.16.refs_14_), channel_id=1, source_target_pairs={{0,4},{1,5},{2,6},{3,7},{4,8},{5,9},{6,10},{7,11},{8,12},{9,13},{1... | collective-permute-start | bytes 1277960 | tf_op jit(solution)/shard_map/ppermute | solution.py:221
  99.0 8.4 %collective-permute-start.22 = (bf16[2,128,1664]{2,1,0:T(8,128)(2,1)S(1)}, bf16[2,128,1664]{2,1,0:T(8,128)(2,1)S(1)}, u32[]{:S(2)}, u32[]{:S(2)}) collective-permute-start(bf16[2,128,1664]{2,1,0:T(8,128)(2,1)S(1)} %collective-permute-done.18.refs_23_), channel_id=1, source_target_pairs={{0,16},{1,17},{2,18},{3,19},{4,20},{5,21},{6,22},{7,23},{8,24},{9,... | collective-permute-start | bytes 2555912 | tf_op jit(solution)/shard_map/ppermute | solution.py:221
  100.0 7.4 %collective-permute-start.23 = (bf16[128,1664]{1,0:T(8,128)(2,1)S(1)}, bf16[128,1664]{1,0:T(8,128)(2,1)}, u32[]{:S(2)}, u32[]{:S(2)}) collective-permute-start(bf16[128,1664]{1,0:T(8,128)(2,1)S(1)} %collective-permute-done.21.refs_18_), channel_id=1, source_target_pairs={{0,4},{1,5},{2,6},{3,7},{4,8},{5,9},{6,10},{7,11},{8,12},{9,13},{1... | collective-permute-start | bytes 1277960 | tf_op jit(solution)/shard_map/ppermute | solution.py:221
  108.4 63.3 %copy-start.3 = (s32[32,2]{1,0:T(8,128)S(1)}, s32[32,2]{1,0:T(8,128)}, u32[]{:S(2)}) copy-start(s32[32,2]{1,0:T(8,128)} %copy.13.refs_1_) | copy-start | bytes 772
  108.4 63.3 %copy-start.4 = (s32[2]{0:T(128)S(1)}, s32[2]{0:T(128)}, u32[]{:S(2)}) copy-start(s32[2]{0:T(128)} %pad_add_fusion.refs_0_) | copy-start | bytes 28
  124.4 47.3 %copy-start.1 = (f32[32,128,128]{2,1,0:T(8,128)S(1)}, f32[32,128,128]{2,1,0:T(8,128)}, u32[]{:S(2)}) copy-start(f32[32,128,128]{2,1,0:T(8,128)} %get-tuple-element.56.refs_3_) | copy-start | bytes 6291460
  (18 other events, 245.2 us)

commit v4 on v3

--- a/solution.py
+++ b/solution.py
@@ -8,6 +8,7 @@
 
 RIDGE = 1.0
 GROUP = 4
+STAGES = 4
 AXES = ("row", "col")
 LANES = 128
 LARGE = 58 * 1024 * 1024
@@ -54,11 +55,11 @@
     out_ref[:, width : width + LANES] = extra.astype(jnp.bfloat16)
 
 
-def add_tile(kernel, slot, spread, across, row_acc, col_acc, where, pairs, listed, n_col):
+def add_tile(kernel, slot, spread, across, row_acc, col_acc, where, tiles, n_col):
     row_index, col_index = where
-    a = pairs[slot, 0]
-    b = pairs[slot, 1]
-    live = jnp.where(slot < listed, 1.0, 0.0)
+    a = tiles[slot, 0]
+    b = tiles[slot, 1]
+    live = tiles[slot, 2].astype(jnp.float32)
     other = jnp.where(row_index * n_col + a == b * n_col + col_index, 0.0, live)
     both = kernel * (spread + across)
     row_acc[a] = row_acc[a] + both * live
@@ -66,45 +67,55 @@
 
 
 def first_sweep_kernel(
-    row_plan, col_plan, width, place, pairs, count, row_spot, col_spot, *rest
+    row_plan, col_plan, width, place, tiles, ready, row_spot, col_spot, *rest
 ):
     n_pieces = len(row_plan) + len(col_plan)
     pieces = rest[:n_pieces]
-    (kernel_ref, out_ref, held, held_sems, rows_ref, cols_ref, sems, vec, norms,
+    (kernel_ref, out_ref, held, held_sems, rows_ref, cols_ref, row_sems, col_sems, vec, norms,
      spread_v, spread_n, row_acc, col_acc) = rest[n_pieces:]
     n_col = rows_ref.shape[0]
     n_row = cols_ref.shape[0]
-    copies = []
+    copies = [[] for _ in range(STAGES)]
     for k, taken in enumerate(row_plan + col_plan):
-        target = rows_ref if k < len(row_plan) else cols_ref
+        target, sems = (rows_ref, row_sems) if k < len(row_plan) else (cols_ref, col_sems)
         for index, part in taken:
             source = pieces[k] if part is None else pieces[k].at[part]
-            copy = pltpu.make_async_copy(source, target.at[index], sems.at[len(copies)])
-            copy.start()
-            copies.append(copy)
+            copy = pltpu.make_async_copy(source, target.at[index], sems.at[index])
+            copies[index * STAGES // n_col].append(copy)
+    for copy in copies[0] + copies[1]:
+        copy.start()
     row_index = place[0]
     col_index = place[1]
-    listed = count[0]
     row_acc[...] = jnp.zeros_like(row_acc)
     col_acc[...] = jnp.zeros_like(col_acc)
-    for copy in copies:
-        copy.wait()
-    for k in range(n_col):
-        extra = rows_ref[k, :, width : width + LANES].astype(jnp.float32)
-        value = extra[:, 0:1] + (extra[:, 1:2] + extra[:, 2:3])
-        spread_v[k] = jnp.broadcast_to(value, (LANES, LANES))
-        value = extra[:, 3:4] + (extra[:, 4:5] + extra[:, 5:6])
-        spread_n[k] = jnp.broadcast_to(value, (LANES, LANES))
-    for k in range(n_row):
-        extra = jnp.transpose(cols_ref[k, :, width : width + LANES].astype(jnp.float32))
-        vec[k : k + 1, :] = extra[0:1, :] + (extra[1:2, :] + extra[2:3, :])
-        norms[k : k + 1, :] = extra[3:4, :] + (extra[4:5, :] + extra[5:6, :])
+
+    lane = lax.broadcasted_iota(jnp.int32, (LANES, LANES), 0)
+    take_v = (lane < 3).astype(jnp.float32).astype(jnp.bfloat16)
+    take_n = ((lane >= 3) & (lane < 6)).astype(jnp.float32).astype(jnp.bfloat16)
+    lane = lax.broadcasted_iota(jnp.int32, (16, LANES), 1)
+    line = lax.broadcasted_iota(jnp.int32, (16, LANES), 0)
+    take_both = (lane // 3 == line).astype(jnp.float32).astype(jnp.bfloat16)
+
+    def spread(k):
+        extra = rows_ref[k, :, width : width + LANES]
+        spread_v[k] = jnp.dot(extra, take_v, preferred_element_type=jnp.float32)
+        spread_n[k] = jnp.dot(extra, take_n, preferred_element_type=jnp.float32)
+        both = lax.dot_general(
+            take_both, cols_ref[k, :, width : width + LANES], (((1,), (1,)), ((), ())),
+            preferred_element_type=jnp.float32,
+        )
+        vec[k : k + 1, :] = both[0:1, :]
+        norms[k : k + 1, :] = both[1:2, :]
+
+    def save(turn):
+        at = pl.ds(turn * GROUP, GROUP)
+        return pltpu.make_async_copy(held.at[at], kernel_ref.at[at], held_sems.at[turn])
 
     def step(turn, carry):
         for g in range(GROUP):
             slot = turn * GROUP + g
-            a = row_spot[pairs[slot, 0]]
-            b = col_spot[pairs[slot, 1]]
+            a = row_spot[tiles[slot, 0]]
+            b = col_spot[tiles[slot, 1]]
             inner = lax.dot_general(
                 rows_ref[a, :, 0:width], cols_ref[b, :, 0:width], (((1,), (1,)), ((), ())),
                 preferred_element_type=jnp.float32,
@@ -114,19 +125,31 @@
             held[slot] = kernel
             add_tile(
                 kernel, slot, spread_v[a], vec[pl.ds(b, 1), :], row_acc, col_acc,
-                (row_index, col_index), pairs, listed, n_col,
+                (row_index, col_index), tiles, n_col,
             )
+        save(turn).start()
         return carry
 
-    lax.fori_loop(0, pairs.shape[0] // GROUP, step, 0)
-    save = pltpu.make_async_copy(held, kernel_ref, held_sems.at[0])
-    save.start()
+    turns = tiles.shape[0] // GROUP
+    done = 0
+    for stage in range(STAGES):
+        for copy in copies[stage]:
+            copy.wait()
+        if stage + 2 < STAGES:
+            for copy in copies[stage + 2]:
+                copy.start()
+        for k in range(n_col * stage // STAGES, n_col * (stage + 1) // STAGES):
+            spread(k)
+        upto = ready[stage] if stage + 1 < STAGES else turns
+        lax.fori_loop(done, upto, step, 0)
+        done = upto
     write_slots(row_acc, col_acc, row_index, col_index, n_row, n_col, out_ref)
-    save.wait()
+    for turn in range(turns):
+        save(turn).wait()
 
 
 def second_sweep_kernel(
-    place, pairs, count, kernel_ref, known_ref, out_ref, own_ref,
+    place, tiles, kernel_ref, known_ref, out_ref, own_ref,
     held, held_sems, start_ref, image_ref, next_dir, sums, spread_v, row_acc, col_acc,
     *, n_row, n_col,
 ):
@@ -134,7 +157,6 @@
     fetch.start()
     row_index = place[0]
     col_index = place[1]
-    listed = count[0]
     image = known_ref[:, 0:LANES]
     start = known_ref[:, LANES : 2 * LANES]
     image_ref[...] = image
@@ -155,15 +177,15 @@
     def step(turn, carry):
         for g in range(GROUP):
             slot = turn * GROUP + g
-            j = pairs[slot, 1] * n_col + col_index
+            j = tiles[slot, 1] * n_col + col_index
             add_tile(
-                held[slot], slot, spread_v[pairs[slot, 0]], next_dir[pl.ds(j, 1), :],
+                held[slot], slot, spread_v[tiles[slot, 0]], next_dir[pl.ds(j, 1), :],
                 row_acc, col_acc,
-                (row_index, col_index), pairs, listed, n_col,
+                (row_index, col_index), tiles, n_col,
             )
         return carry
 
-    lax.fori_loop(0, pairs.shape[0] // GROUP, step, 0)
+    lax.fori_loop(0, tiles.shape[0] // GROUP, step, 0)
     write_slots(row_acc, col_acc, row_index, col_index, n_row, n_col, sums)
     partial = jnp.sum(sums[...] * next_dir[...])
     out_ref[:, 0:LANES] = sums[...]
@@ -196,6 +218,23 @@
     residual_ref[...] = own_ref[1:2, :] - alpha * image
 
 
+def in_order(pairs, count, row_spot, col_spot):
+    slots = pairs.shape[0]
+    spots_of = jnp.arange(row_spot.shape[0], dtype=jnp.int32)[None, :]
+    row_at = jnp.sum(jnp.where(pairs[:, 0:1] == spots_of, row_spot[None, :], 0), axis=1)
+    col_at = jnp.sum(jnp.where(pairs[:, 1:2] == spots_of, col_spot[None, :], 0), axis=1)
+    slot = jnp.arange(slots, dtype=jnp.int32)
+    arrival = jnp.maximum(row_at, col_at)
+    key = arrival * slots + slot
+    rank = jnp.sum((key[None, :] < key[:, None]).astype(jnp.int32), axis=1)
+    known = jnp.stack([pairs[:, 0], pairs[:, 1], (slot < count).astype(jnp.int32)], axis=1)
+    chosen = rank[None, :] == slot[:, None]
+    tiles = jnp.sum(jnp.where(chosen[:, :, None], known[None, :, :], 0), axis=1)
+    fetched = (jnp.arange(STAGES, dtype=jnp.int32) + 1) * (row_spot.shape[0] // STAGES)
+    ready = jnp.sum((arrival[None, :] < fetched[:, None]).astype(jnp.int32), axis=1) // GROUP
+    return tiles, ready
+
+
 def swap(slots):
     return lax.all_to_all(slots, AXES, 0, 0, tiled=True)
 
@@ -254,42 +293,40 @@
     z = lax.axis_index("col") % NZ
     middle = (z == 1) | (z == 2)
     inside = (1, 2)
-    half = mine.shape[0] // 2
-
+
+    z3, z1 = along_z(mine, 3), along_z(mine, 1)
     one, two = along_x(mine, 1), along_x(mine, -1)
-    z1, inner = along_z(mine, 1), along_z(mine, 3, inside)
-    over_low = across(mine[:half])
-    one, two, z1, inner, over_low = together(one, two, z1, inner, over_low)
-
-    one1, two1, far = along_x(z1, 1), along_x(z1, -1), along_x(one, 1)
-    over_high = across(mine[half:])
-    inner2, outer = along_z(z1, 3, inside), along_z(inner, 1, inside)
-    one1, two1, far, over_high, inner2, outer = together(
-        one1, two1, far, over_high, inner2, outer
+    near, back = along_y(mine, 1), along_y(mine, -1)
+    z3, z1, one, two, near, back = together(z3, z1, one, two, near, back)
+
+    over = across(mine)
+    z13 = jnp.stack([z1, z3])
+    one13, two13 = along_x(z13, 1), along_x(z13, -1)
+    inner, outer = along_z(z1, 3, inside), along_z(z3, 1, inside)
+    far, rim = along_x(one, 1), along_y(near, 1)
+    over, one13, two13, inner, outer, far, rim = together(
+        over, one13, two13, inner, outer, far, rim
     )
 
-    pair = jnp.stack([mine, jnp.concatenate([over_low, over_high])])
     z2 = jnp.where(middle, inner, outer)
-    one2, two2, far1 = along_x(z2, 1), along_x(z2, -1), along_x(one1, 1)
-    near, back = along_y(pair, 1), along_y(pair, -1)
-    outer2 = along_z(inner2, 1, inside)
-    one2, two2, far1, near, back, outer2 = together(one2, two2, far1, near, back, outer2)
-
-    z3 = jnp.where(middle, inner2, outer2)
-    one3, two3, far2 = along_x(z3, 1), along_x(z3, -1), along_x(one2, 1)
-    rim = along_y(near, 1)
-    twin = sibling(jnp.concatenate([pair, near, back]))
-    one3, two3, far2, rim, twin = together(one3, two3, far2, rim, twin)
-
-    far3, rim_twin = together(along_x(one3, 1), sibling(rim))
-
-    rows = [mine, one, far, two, z1, one1, far1, two1, z2, one2, far2, two2, z3, one3, far3, two3]
-    row_plan = [((NZ * turn + m, None),) for m in range(NZ) for turn in range(NX)]
-    cols = [pair, near, rim, back, twin, rim_twin]
-    col_plan = [((turn, 0), (4 + turn, 1)) for turn in range(NY)]
-    col_plan += [
-        ((8, 0), (12, 1), (9, 2), (13, 3), (11, 4), (15, 5)), ((10, 0), (14, 1)),
-    ]
+    far13, one2, two2 = along_x(one13, 1), along_x(z2, 1), along_x(z2, -1)
+    near_c, back_c = along_y(over, 1), along_y(over, -1)
+    line = jnp.stack([mine, near, rim, back])
+    far13, one2, two2, near_c, back_c, line = together(far13, one2, two2, near_c, back_c, line)
+
+    far2, rim_c = along_x(one2, 1), along_y(near_c, 1)
+    twin, twin_c = sibling(line), sibling(jnp.stack([over, near_c, back_c]))
+    rim_c, far2, twin, twin_c = together(rim_c, far2, twin, twin_c)
+
+    rim_twin = sibling(rim_c)
+
+    rows = [mine, one, far, two, z13, one13, far13, two13, z2, one2, far2, two2]
+    row_plan = [((NZ * turn, None),) for turn in range(NX)]
+    row_plan += [((NZ * turn + 1, 0), (NZ * turn + 2, 1)) for turn in range(NX)]
+    row_plan += [((NZ * turn + 3, None),) for turn in range(NX)]
+    cols = [line, over, near_c, rim_c, back_c, twin, twin_c, rim_twin]
+    col_plan = [tuple((k, k) for k in range(NY))] + [((k, None),) for k in range(NY, 2 * NY)]
+    col_plan += [tuple((8 + k, k) for k in range(NY)), ((12, 0), (13, 1), (15, 2)), ((14, None),)]
     return rows, row_plan, cols, col_plan
 
 
@@ -300,7 +337,7 @@
     for d in range(total):
         y, h, k, x, z = coords(d)
         sign = 1 if k == 0 else -1
-        order = [z, z ^ 1, z ^ 3, z ^ 2] if z in (1, 2) else [z, z ^ 1, z ^ 2, z ^ 3]
+        order = [z, z ^ 1, z ^ 3, z ^ 2]
         for a in range(NX * NZ):
             turn = sign * (x - a // NZ) % NX
             row_spot[d, a] = NZ * turn + order.index(a % NZ)
@@ -318,7 +355,7 @@
     total = n_row * n_col
     place = jnp.stack([lax.axis_index("row"), lax.axis_index("col")]).astype(jnp.int32)
     pairs = tile_pairs[0, 0]
-    count = tile_count[0]
+    count = tile_count[0, 0]
     slots = pairs.shape[0]
     block, width = features.shape
     params = pltpu.CompilerParams(vmem_limit_bytes=SMALL)
@@ -333,6 +370,7 @@
     )(features, targets[None, :])
     row_pieces, row_plan, col_pieces, col_plan = gather(packed)
     row_spot, col_spot = spots()
+    tiles, ready = in_order(pairs, count, row_spot, col_spot)
 
     accumulators = [
         pltpu.VMEM((n_col, block, block), f32),
@@ -348,15 +386,15 @@
         out_specs=(HB, VM),
         scratch_shapes=[
             pltpu.VMEM((slots, block, block), f32),
-            pltpu.SemaphoreType.DMA((1,)),
+            pltpu.SemaphoreType.DMA((slots // GROUP,)),
             pltpu.VMEM((n_col, block, width + LANES), jnp.bfloat16),
             pltpu.VMEM((n_row, block, width + LANES), jnp.bfloat16),
         ]
-        + [pltpu.SemaphoreType.DMA((sum(len(taken) for taken in row_plan + col_plan),))]
+        + [pltpu.SemaphoreType.DMA((n_col,)), pltpu.SemaphoreType.DMA((n_row,))]
         + [pltpu.VMEM((n_row, block), f32)] * 2
         + [pltpu.VMEM((n_col, block, block), f32)] * 2 + accumulators,
         compiler_params=pltpu.CompilerParams(vmem_limit_bytes=LARGE),
-    )(place, pairs, count, row_spot, col_spot, *row_pieces, *col_pieces)
+    )(place, tiles, ready, row_spot, col_spot, *row_pieces, *col_pieces)
 
     image = pl.pallas_call(
         lambda *refs: image_kernel(None, *refs, block=block),
@@ -373,7 +411,7 @@
             jax.ShapeDtypeStruct((total, 2 * block), f32),
             jax.ShapeDtypeStruct((8, block), f32),
         ),
-        in_specs=[SM, SM, SM, HB, VM],
+        in_specs=[SM, SM, HB, VM],
         out_specs=(VM, VM),
         scratch_shapes=[
             pltpu.VMEM((slots, block, block), f32),
@@ -385,7 +423,7 @@
             pltpu.VMEM((n_col, block, block), f32),
         ] + accumulators,
         compiler_params=params,
-    )(place, pairs, count, kernel, images)
+    )(place, tiles, kernel, images)
 
     result, residual = pl.pallas_call(
         lambda *refs: finish_kernel(*refs, block=block),

time: 197 us -> 186 us (0.944)
  waiting for transfers between devices: 55.8 us -> 41.6 us
  other arithmetic: 2.3 us -> 8.85 us
  Pallas kernels: 19.8 us -> 15.3 us
  starting transfers between devices: 42.8 us -> 45.9 us
    ppermute x19, waiting for transfers between devices: 38.3 us -> 28 us  [send(): return lax.ppermute(array, AXES, pairs)]
    pallas_call x1, Pallas kernels: 16 us -> 11.5 us  [body(): pl.pallas_call(lambda *refs: first_sweep_kernel(row_plan, col_plan, width...]
    another operation x2 -> x4, other arithmetic: 1.16 us -> 5.13 us  [the longest x1 2.37 us: gather(): twin, twin_c = (sibling(line), sibling(jnp.stack([over, near_c, back_c])))]
    ppermute x5 -> x4, waiting for transfers between devices: 17.5 us -> 13.6 us  [along_z(): return lax.ppermute(array, AXES, pairs)]
    ppermute x5 -> x4, starting transfers between devices: 5.55 us -> 7.96 us  [along_z(): return lax.ppermute(array, AXES, pairs)]
  transfers between devices with their start and end apart: 24 -> 23, of which waited for: 12 -> 9; matrix products, arithmetic and copies ran while one was open for 2% -> 6% of each run, Pallas kernels for 0% -> 0%
where the time goes in v4:
time: 186 us; the launch traced here: 185 us
  blocking collectives  66.7 us (36%)
  starting transfers between devices  45.9 us (25%)
  waiting for transfers between devices  41.6 us (22%)
  Pallas kernels  15.3 us (8%)
  other arithmetic  8.85 us (5%)
  local copies, waits for them, and re-layouts  5.24 us (3%)
    all_to_all x3, blocking collectives, swap(): return lax.all_to_all(slots, AXES, 0, 0, tiled=True)  66.7 us
    ppermute x19, starting transfers between devices, send(): return lax.ppermute(array, AXES, pairs)  38 us
    ppermute x19, waiting for transfers between devices, send(): return lax.ppermute(array, AXES, pairs)  28 us
    ppermute x4, waiting for transfers between devices, along_z(): return lax.ppermute(array, AXES, pairs)  13.6 us
    pallas_call x1, Pallas kernels, body(): pl.pallas_call(lambda *refs: first_sweep_kernel(row_plan, col_plan, width...  11.5 us
    ppermute x4, starting transfers between devices, along_z(): return lax.ppermute(array, AXES, pairs)  7.96 us
  transfers between devices with their start and end apart: 23, of which 9 were waited for; matrix products, arithmetic and copies ran while one was open for 6% of the time, Pallas kernels for 0%

profile of v4, /device:TPU:1, one launch (start us, length us, event | category | flops | bytes accessed | tf_op | source)
XLA Modules:
  0.0 185.2 jit_solution(4583812090445811966)
XLA Ops:
  0.6 1.0 copy-done.2
  2.5 5.3 %collective-permute-start.5 = (bf16[128,1664]{1,0:T(8,128)(2,1)S(1)}, bf16[128,1664]{1,0:T(8,128)(2,1)}, u32[]{:S(2)}, u32[]{:S(2)}) collective-permute-start(bf16[128,1664]{1,0:T(8,128)(2,1)S(1)} %shard_map.77.refs_5_), channel_id=1, source_target_pairs={{0,3},{1,2},{2,1},{3,0},{4,7},{5,6},{6,5},{7,4},{8,11},{9,10},{10,... | collective-permute-start | bytes 1277960 | tf_op jit(solution)/shard_map/ppermute | solution.py:269
  7.8 2.5 %collective-permute-start.3 = (bf16[128,1664]{1,0:T(8,128)(2,1)S(1)}, bf16[128,1664]{1,0:T(8,128)(2,1)S(1)}, u32[]{:S(2)}, u32[]{:S(2)}) collective-permute-start(bf16[128,1664]{1,0:T(8,128)(2,1)S(1)} %shard_map.77.refs_5_), channel_id=1, source_target_pairs={{0,4},{1,5},{2,6},{3,7},{4,8},{5,9},{6,10},{7,11},{8,12},{9,13},{1... | collective-permute-start | bytes 1277960 | tf_op jit(solution)/shard_map/ppermute | solution.py:260
  10.3 2.7 %collective-permute-start.1 = (bf16[128,1664]{1,0:T(8,128)(2,1)S(1)}, bf16[128,1664]{1,0:T(8,128)(2,1)S(1)}, u32[]{:S(2)}, u32[]{:S(2)}) collective-permute-start(bf16[128,1664]{1,0:T(8,128)(2,1)S(1)} %shard_map.77.refs_5_), channel_id=1, source_target_pairs={{0,64},{1,65},{2,66},{3,67},{4,68},{5,69},{6,70},{7,71},{8,72},{9,... | collective-permute-start | bytes 1277960 | tf_op jit(solution)/shard_map/ppermute | solution.py:260
  13.0 3.5 %collective-permute-done.5 = bf16[128,1664]{1,0:T(8,128)(2,1)} collective-permute-done((bf16[128,1664]{1,0:T(8,128)(2,1)S(1)}, bf16[128,1664]{1,0:T(8,128)(2,1)}, u32[]{:S(2)}, u32[]{:S(2)}) %collective-permute-start.5) | collective-permute-done | bytes 426016 | tf_op jit(solution)/shard_map/ppermute | solution.py:269
  16.6 2.3 %collective-permute-start = (bf16[128,1664]{1,0:T(8,128)(2,1)S(1)}, bf16[128,1664]{1,0:T(8,128)(2,1)S(1)}, u32[]{:S(2)}, u32[]{:S(2)}) collective-permute-start(bf16[128,1664]{1,0:T(8,128)(2,1)S(1)} %shard_map.77.refs_5_), channel_id=1, source_target_pairs={{0,192},{1,193},{2,194},{3,195},{4,196},{5,197},{6,198},{7,199},{8... | collective-permute-start | bytes 1277960 | tf_op jit(solution)/shard_map/ppermute | solution.py:260
  18.8 8.6 %collective-permute-done.4 = bf16[128,1664]{1,0:T(8,128)(2,1)} collective-permute-done((bf16[128,1664]{1,0:T(8,128)(2,1)S(1)}, bf16[128,1664]{1,0:T(8,128)(2,1)}, u32[]{:S(2)}, u32[]{:S(2)}) %collective-permute-start.4) | collective-permute-done | bytes 426016 | tf_op jit(solution)/shard_map/ppermute | solution.py:269
  27.4 5.4 %collective-permute-start.12 = (bf16[128,1664]{1,0:T(8,128)(2,1)S(1)}, bf16[128,1664]{1,0:T(8,128)(2,1)S(1)}, u32[]{:S(2)}, u32[]{:S(2)}) collective-permute-start(bf16[128,1664]{1,0:T(8,128)(2,1)S(1)} %shard_map.77.refs_5_), channel_id=1, source_target_pairs={{0,32},{1,33},{2,34},{3,35},{4,36},{5,37},{6,38},{7,39},{8,40},{9,... | collective-permute-start | bytes 1277960 | tf_op jit(solution)/shard_map/ppermute | solution.py:260
  32.8 2.6 %collective-permute-start.7 = (bf16[128,1664]{1,0:T(8,128)(2,1)S(1)}, bf16[128,1664]{1,0:T(8,128)(2,1)S(1)}, u32[]{:S(2)}, u32[]{:S(2)}) collective-permute-start(bf16[128,1664]{1,0:T(8,128)(2,1)S(1)} %collective-permute-done.3.refs_6_), channel_id=1, source_target_pairs={{0,4},{1,5},{2,6},{3,7},{4,8},{5,9},{6,10},{7,11},{8,12},{9,13},{1... | collective-permute-start | bytes 1277960 | tf_op jit(solution)/shard_map/ppermute | solution.py:260
  35.4 1.2 pad_maximum_fusion.2.refs_9_
  38.2 1.3 collective-permute-start.8
  39.5 7.3 %collective-permute-done.12.refs_18_ = bf16[128,1664]{1,0:T(8,128)(2,1)S(1)} collective-permute-done((bf16[128,1664]{1,0:T(8,128)(2,1)S(1)}, bf16[128,1664]{1,0:T(8,128)(2,1)S(1)}, u32[]{:S(2)}, u32[]{:S(2)}) %collective-permute-start.12) | collective-permute-done | bytes 426016 | tf_op jit(solution)/shard_map/ppermute | solution.py:260
  46.8 5.5 %collective-permute-start.6 = (bf16[128,1664]{1,0:T(8,128)(2,1)S(1)}, bf16[128,1664]{1,0:T(8,128)(2,1)}, u32[]{:S(2)}, u32[]{:S(2)}) collective-permute-start(bf16[128,1664]{1,0:T(8,128)(2,1)S(1)} %collective-permute-done.1), channel_id=1, source_target_pairs={{0,64},{1,65},{2,66},{3,67},{4,68},{5,69},{6,70},{7,71},{8,72},{9,... | collective-permute-start | bytes 1277960 | tf_op jit(solution)/shard_map/ppermute | solution.py:260
  53.1 1.4 collective-permute-start.9
  54.5 2.9 %collective-permute-done.6 = bf16[128,1664]{1,0:T(8,128)(2,1)} collective-permute-done((bf16[128,1664]{1,0:T(8,128)(2,1)S(1)}, bf16[128,1664]{1,0:T(8,128)(2,1)}, u32[]{:S(2)}, u32[]{:S(2)}) %collective-permute-start.6) | collective-permute-done | bytes 426016 | tf_op jit(solution)/shard_map/ppermute | solution.py:260
  57.4 1.5 collective-permute-done.8
  59.7 2.3 %collective-permute-start.17 = (bf16[2,128,1664]{2,1,0:T(8,128)(2,1)}, bf16[2,128,1664]{2,1,0:T(8,128)(2,1)}, u32[]{:S(2)}, u32[]{:S(2)}) collective-permute-start(bf16[2,128,1664]{2,1,0:T(8,128)(2,1)} %collective-permute-done.11.refs_10_), channel_id=1, source_target_pairs={{0,4},{1,5},{2,6},{3,7},{4,8},{5,9},{6,10},{7,11},{8,12},{9,13},{1... | collective-permute-start | bytes 2555912 | tf_op jit(solution)/shard_map/ppermute | solution.py:260
  62.0 1.8 broadcast_select_fusion.refs_13_
  64.2 1.1 collective-permute-start.15
  65.3 2.6 %collective-permute-start.14 = (bf16[128,1664]{1,0:T(8,128)(2,1)S(1)}, bf16[128,1664]{1,0:T(8,128)(2,1)}, u32[]{:S(2)}, u32[]{:S(2)}) collective-permute-start(bf16[128,1664]{1,0:T(8,128)(2,1)S(1)} %collective-permute-done.12.refs_18_), channel_id=1, source_target_pairs={{0,64},{1,65},{2,66},{3,67},{4,68},{5,69},{6,70},{7,71},{8,72},{9,... | collective-permute-start | bytes 1277960 | tf_op jit(solution)/shard_map/ppermute | solution.py:260
  68.7 1.5 pad_maximum_fusion.refs_17_
  70.2 10.9 %collective-permute-done.16.refs_14_ = bf16[128,1664]{1,0:T(8,128)(2,1)} collective-permute-done((bf16[128,1664]{1,0:T(8,128)(2,1)}, bf16[128,1664]{1,0:T(8,128)(2,1)}, u32[]{:S(2)}, u32[]{:S(2)}) %collective-permute-start.16) | collective-permute-done | bytes 426016 | tf_op jit(solution)/shard_map/ppermute | solution.py:260
  81.1 3.9 %collective-permute-start.19 = (bf16[4,128,1664]{2,1,0:T(8,128)(2,1)S(1)}, bf16[4,128,1664]{2,1,0:T(8,128)(2,1)}, u32[]{:S(2)}, u32[]{:S(2)}) collective-permute-start(bf16[4,128,1664]{2,1,0:T(8,128)(2,1)S(1)} %pad_maximum_fusion.refs_17_), channel_id=1, source_target_pairs={{0,16},{1,17},{2,18},{3,19},{4,20},{5,21},{6,22},{7,23},{8,24},{9,... | collective-permute-start | bytes 5111816 | tf_op jit(solution)/shard_map/ppermute | solution.py:260
  85.1 2.4 %pad_maximum_fusion.1 = bf16[3,128,1664]{2,1,0:T(8,128)(2,1)} fusion(bf16[1,128,1664]{2,1,0:T(8,128)(2,1)} %bitcast.17, bf16[1,128,1664]{2,1,0:T(8,128)(2,1)} %bitcast.16, bf16[1,128,1664]{2,1,0:T(8,128)(2,1)S(1)} %bitcast.45), kind=kLoop, calls=%fused_computation.1 | loop fusion | flops 1277952 | bytes 2555904 | tf_op jit(solution)/shard_map/stack | solution.py:318
  88.6 2.8 %collective-permute-start.21 = (bf16[128,1664]{1,0:T(8,128)(2,1)}, bf16[128,1664]{1,0:T(8,128)(2,1)}, u32[]{:S(2)}, u32[]{:S(2)}) collective-permute-start(bf16[128,1664]{1,0:T(8,128)(2,1)} %collective-permute-done.14.refs_19_), channel_id=1, source_target_pairs={{0,64},{1,65},{2,66},{3,67},{4,68},{5,69},{6,70},{7,71},{8,72},{9,... | collective-permute-start | bytes 1277960 | tf_op jit(solution)/shard_map/ppermute | solution.py:260
  93.0 5.8 %collective-permute-done.20.refs_15_ = bf16[128,1664]{1,0:T(8,128)(2,1)S(1)} collective-permute-done((bf16[128,1664]{1,0:T(8,128)(2,1)}, bf16[128,1664]{1,0:T(8,128)(2,1)S(1)}, u32[]{:S(2)}, u32[]{:S(2)}) %collective-permute-start.20) | collective-permute-done | bytes 426016 | tf_op jit(solution)/shard_map/ppermute | solution.py:260
  98.9 1.5 collective-permute-start.22
  102.8 11.5 %shard_map.78 = (f32[32,128,128]{2,1,0:T(8,128)}, f32[256,128]{1,0:T(8,128)}) custom-call(s32[2]{0:T(128)} %pad_add_fusion.1.refs_0_, s32[32,3]{1,0:T(8,128)} %copy.16.refs_1_, s32[4]{0:T(128)} %and_select_fusion.refs_2_, s32[16]{0:T(128)} %copy-done.21, s32[16]{0:T(128)} %copy-done.20, bf16[128,1664]{1,0:T(8,128)(2,1)} %copy-done, ...), custom_call_target="tpu_custom_call" | custom-call | tf_op jit(solution)/shard_map/pallas_call | solution.py:379
  114.3 24.0 %all_to_all.33 = f32[256,1,128]{2,1,0:T(1,128)S(1)} all-to-all(f32[256,1,128]{2,1,0:T(1,128)} %bitcast.48), channel_id=1, replica_groups=mesh['row'=16,'col'=16] {'row','col'}, dimensions={0} | all-to-all | bytes 262144 | tf_op jit(solution)/shard_map/all_to_all | solution.py:239
  138.7 21.5 %all_to_all.34 = f32[256,1,256]{2,1,0:T(1,128)S(1)} all-to-all(f32[256,1,256]{2,1,0:T(1,128)S(1)} %copy.15), channel_id=1, replica_groups=mesh['row'=16,'col'=16] {'row','col'}, dimensions={0} | all-to-all | bytes 524288 | tf_op jit(solution)/shard_map/all_to_all | solution.py:239
  160.2 2.9 %shard_map.80 = (f32[256,256]{1,0:T(8,128)S(1)}, f32[8,128]{1,0:T(8,128)S(1)}) custom-call(s32[2]{0:T(128)S(1)} %copy-done.6, s32[32,3]{1,0:T(8,128)S(1)} %copy-done.3, f32[32,128,128]{2,1,0:T(8,128)S(1)} %copy-done.1, f32[256,256]{1,0:T(8,128)S(1)} %bitcast.40), custom_call_target="tpu_custom_call" | custom-call | tf_op jit(solution)/shard_map/pallas_call | solution.py:408
  163.4 21.3 %all_to_all.35 = f32[256,1,256]{2,1,0:T(1,128)S(1)} all-to-all(f32[256,1,256]{2,1,0:T(1,128)S(1)} %copy.17), channel_id=1, replica_groups=mesh['row'=16,'col'=16] {'row','col'}, dimensions={0} | all-to-all | bytes 524288 | tf_op jit(solution)/shard_map/all_to_all | solution.py:239
  (89 shorter events, 10.9 us)
Async XLA Ops:
  2.5 67.7 %copy-start = (bf16[128,1664]{1,0:T(8,128)(2,1)}, bf16[128,1664]{1,0:T(8,128)(2,1)S(1)}, u32[]{:S(2)}) copy-start(bf16[128,1664]{1,0:T(8,128)(2,1)S(1)} %shard_map.77.refs_5_) | copy-start | bytes 1277956
  2.5 14.0 %collective-permute-start.5 = (bf16[128,1664]{1,0:T(8,128)(2,1)S(1)}, bf16[128,1664]{1,0:T(8,128)(2,1)}, u32[]{:S(2)}, u32[]{:S(2)}) collective-permute-start(bf16[128,1664]{1,0:T(8,128)(2,1)S(1)} %shard_map.77.refs_5_), channel_id=1, source_target_pairs={{0,3},{1,2},{2,1},{3,0},{4,7},{5,6},{6,5},{7,4},{8,11},{9,10},{10,... | collective-permute-start | bytes 1277960 | tf_op jit(solution)/shard_map/ppermute | solution.py:269
  7.8 19.6 %collective-permute-start.4 = (bf16[128,1664]{1,0:T(8,128)(2,1)S(1)}, bf16[128,1664]{1,0:T(8,128)(2,1)}, u32[]{:S(2)}, u32[]{:S(2)}) collective-permute-start(bf16[128,1664]{1,0:T(8,128)(2,1)S(1)} %shard_map.77.refs_5_), channel_id=1, source_target_pairs={{0,1},{1,0},{2,3},{3,2},{4,5},{5,4},{6,7},{7,6},{8,9},{9,8},{10,11... | collective-permute-start | bytes 1277960 | tf_op jit(solution)/shard_map/ppermute | solution.py:269
  7.8 25.0 %collective-permute-start.3 = (bf16[128,1664]{1,0:T(8,128)(2,1)S(1)}, bf16[128,1664]{1,0:T(8,128)(2,1)S(1)}, u32[]{:S(2)}, u32[]{:S(2)}) collective-permute-start(bf16[128,1664]{1,0:T(8,128)(2,1)S(1)} %shard_map.77.refs_5_), channel_id=1, source_target_pairs={{0,4},{1,5},{2,6},{3,7},{4,8},{5,9},{6,10},{7,11},{8,12},{9,13},{1... | collective-permute-start | bytes 1277960 | tf_op jit(solution)/shard_map/ppermute | solution.py:260
  10.3 22.5 %collective-permute-start.2 = (bf16[128,1664]{1,0:T(8,128)(2,1)S(1)}, bf16[128,1664]{1,0:T(8,128)(2,1)S(1)}, u32[]{:S(2)}, u32[]{:S(2)}) collective-permute-start(bf16[128,1664]{1,0:T(8,128)(2,1)S(1)} %shard_map.77.refs_5_), channel_id=1, source_target_pairs={{0,12},{1,13},{2,14},{3,15},{4,0},{5,1},{6,2},{7,3},{8,4},{9,5},{1... | collective-permute-start | bytes 1277960 | tf_op jit(solution)/shard_map/ppermute | solution.py:260
  10.3 22.5 %collective-permute-start.1 = (bf16[128,1664]{1,0:T(8,128)(2,1)S(1)}, bf16[128,1664]{1,0:T(8,128)(2,1)S(1)}, u32[]{:S(2)}, u32[]{:S(2)}) collective-permute-start(bf16[128,1664]{1,0:T(8,128)(2,1)S(1)} %shard_map.77.refs_5_), channel_id=1, source_target_pairs={{0,64},{1,65},{2,66},{3,67},{4,68},{5,69},{6,70},{7,71},{8,72},{9,... | collective-permute-start | bytes 1277960 | tf_op jit(solution)/shard_map/ppermute | solution.py:260
  16.6 16.3 %collective-permute-start = (bf16[128,1664]{1,0:T(8,128)(2,1)S(1)}, bf16[128,1664]{1,0:T(8,128)(2,1)S(1)}, u32[]{:S(2)}, u32[]{:S(2)}) collective-permute-start(bf16[128,1664]{1,0:T(8,128)(2,1)S(1)} %shard_map.77.refs_5_), channel_id=1, source_target_pairs={{0,192},{1,193},{2,194},{3,195},{4,196},{5,197},{6,198},{7,199},{8... | collective-permute-start | bytes 1277960 | tf_op jit(solution)/shard_map/ppermute | solution.py:260
  27.4 19.3 %collective-permute-start.12 = (bf16[128,1664]{1,0:T(8,128)(2,1)S(1)}, bf16[128,1664]{1,0:T(8,128)(2,1)S(1)}, u32[]{:S(2)}, u32[]{:S(2)}) collective-permute-start(bf16[128,1664]{1,0:T(8,128)(2,1)S(1)} %shard_map.77.refs_5_), channel_id=1, source_target_pairs={{0,32},{1,33},{2,34},{3,35},{4,36},{5,37},{6,38},{7,39},{8,40},{9,... | collective-permute-start | bytes 1277960 | tf_op jit(solution)/shard_map/ppermute | solution.py:260
  32.8 35.8 %copy-start.12 = (bf16[128,1664]{1,0:T(8,128)(2,1)}, bf16[128,1664]{1,0:T(8,128)(2,1)S(1)}, u32[]{:S(2)}) copy-start(bf16[128,1664]{1,0:T(8,128)(2,1)S(1)} %collective-permute-done.1) | copy-start | bytes 1277956
  32.8 35.8 %copy-start.13 = (bf16[128,1664]{1,0:T(8,128)(2,1)}, bf16[128,1664]{1,0:T(8,128)(2,1)S(1)}, u32[]{:S(2)}) copy-start(bf16[128,1664]{1,0:T(8,128)(2,1)S(1)} %collective-permute-done) | copy-start | bytes 1277956
  32.8 19.5 %collective-permute-start.7 = (bf16[128,1664]{1,0:T(8,128)(2,1)S(1)}, bf16[128,1664]{1,0:T(8,128)(2,1)S(1)}, u32[]{:S(2)}, u32[]{:S(2)}) collective-permute-start(bf16[128,1664]{1,0:T(8,128)(2,1)S(1)} %collective-permute-done.3.refs_6_), channel_id=1, source_target_pairs={{0,4},{1,5},{2,6},{3,7},{4,8},{5,9},{6,10},{7,11},{8,12},{9,13},{1... | collective-permute-start | bytes 1277960 | tf_op jit(solution)/shard_map/ppermute | solution.py:260
  36.6 33.6 %copy-start.8 = (bf16[2,128,1664]{2,1,0:T(8,128)(2,1)}, bf16[2,128,1664]{2,1,0:T(8,128)(2,1)S(1)}, u32[]{:S(2)}) copy-start(bf16[2,128,1664]{2,1,0:T(8,128)(2,1)S(1)} %pad_maximum_fusion.2.refs_9_) | copy-start | bytes 2555908
  36.6 22.2 %collective-permute-start.11 = (bf16[2,128,1664]{2,1,0:T(8,128)(2,1)S(1)}, bf16[2,128,1664]{2,1,0:T(8,128)(2,1)}, u32[]{:S(2)}, u32[]{:S(2)}) collective-permute-start(bf16[2,128,1664]{2,1,0:T(8,128)(2,1)S(1)} %pad_maximum_fusion.2.refs_9_), channel_id=1, source_target_pairs={{0,4},{1,5},{2,6},{3,7},{4,8},{5,9},{6,10},{7,11},{8,12},{9,13},{1... | collective-permute-start | bytes 2555912 | tf_op jit(solution)/shard_map/ppermute | solution.py:260
  37.4 22.3 %collective-permute-start.10 = (bf16[2,128,1664]{2,1,0:T(8,128)(2,1)S(1)}, bf16[2,128,1664]{2,1,0:T(8,128)(2,1)S(1)}, u32[]{:S(2)}, u32[]{:S(2)}) collective-permute-start(bf16[2,128,1664]{2,1,0:T(8,128)(2,1)S(1)} %pad_maximum_fusion.2.refs_9_), channel_id=1, source_target_pairs={{0,12},{1,13},{2,14},{3,15},{4,0},{5,1},{6,2},{7,3},{8,4},{9,5},{1... | collective-permute-start | bytes 2555912 | tf_op jit(solution)/shard_map/ppermute | solution.py:260
  38.2 20.7 %collective-permute-start.8 = (bf16[128,1664]{1,0:T(8,128)(2,1)}, bf16[128,1664]{1,0:T(8,128)(2,1)}, u32[]{:S(2)}, u32[]{:S(2)}) collective-permute-start(bf16[128,1664]{1,0:T(8,128)(2,1)} %collective-permute-done.5), channel_id=1, source_target_pairs={{1,0},{2,3},{5,4},{6,7},{9,8},{10,11},{13,12},{14,15},{17,16},{18,... | collective-permute-start | bytes 1277960 | tf_op jit(solution)/shard_map/ppermute | solution.py:269
  46.8 38.3 %copy-start.9 = (bf16[128,1664]{1,0:T(8,128)(2,1)}, bf16[128,1664]{1,0:T(8,128)(2,1)S(1)}, u32[]{:S(2)}) copy-start(bf16[128,1664]{1,0:T(8,128)(2,1)S(1)} %collective-permute-done.12.refs_18_) | copy-start | bytes 1277956
  46.8 10.6 %collective-permute-start.6 = (bf16[128,1664]{1,0:T(8,128)(2,1)S(1)}, bf16[128,1664]{1,0:T(8,128)(2,1)}, u32[]{:S(2)}, u32[]{:S(2)}) collective-permute-start(bf16[128,1664]{1,0:T(8,128)(2,1)S(1)} %collective-permute-done.1), channel_id=1, source_target_pairs={{0,64},{1,65},{2,66},{3,67},{4,68},{5,69},{6,70},{7,71},{8,72},{9,... | collective-permute-start | bytes 1277960 | tf_op jit(solution)/shard_map/ppermute | solution.py:260
  53.1 5.8 %collective-permute-start.9 = (bf16[128,1664]{1,0:T(8,128)(2,1)}, bf16[128,1664]{1,0:T(8,128)(2,1)}, u32[]{:S(2)}, u32[]{:S(2)}) collective-permute-start(bf16[128,1664]{1,0:T(8,128)(2,1)} %collective-permute-done.4), channel_id=1, source_target_pairs={{1,2},{2,1},{5,6},{6,5},{9,10},{10,9},{13,14},{14,13},{17,18},{18,... | collective-permute-start | bytes 1277960 | tf_op jit(solution)/shard_map/ppermute | solution.py:269
  59.7 21.4 %collective-permute-start.17 = (bf16[2,128,1664]{2,1,0:T(8,128)(2,1)}, bf16[2,128,1664]{2,1,0:T(8,128)(2,1)}, u32[]{:S(2)}, u32[]{:S(2)}) collective-permute-start(bf16[2,128,1664]{2,1,0:T(8,128)(2,1)} %collective-permute-done.11.refs_10_), channel_id=1, source_target_pairs={{0,4},{1,5},{2,6},{3,7},{4,8},{5,9},{6,10},{7,11},{8,12},{9,13},{1... | collective-permute-start | bytes 2555912 | tf_op jit(solution)/shard_map/ppermute | solution.py:260
  63.9 17.2 %collective-permute-start.16 = (bf16[128,1664]{1,0:T(8,128)(2,1)}, bf16[128,1664]{1,0:T(8,128)(2,1)}, u32[]{:S(2)}, u32[]{:S(2)}) collective-permute-start(bf16[128,1664]{1,0:T(8,128)(2,1)} %broadcast_select_fusion.refs_13_), channel_id=1, source_target_pairs={{0,4},{1,5},{2,6},{3,7},{4,8},{5,9},{6,10},{7,11},{8,12},{9,13},{1... | collective-permute-start | bytes 1277960 | tf_op jit(solution)/shard_map/ppermute | solution.py:260
  64.2 16.9 %collective-permute-start.15 = (bf16[128,1664]{1,0:T(8,128)(2,1)}, bf16[128,1664]{1,0:T(8,128)(2,1)}, u32[]{:S(2)}, u32[]{:S(2)}) collective-permute-start(bf16[128,1664]{1,0:T(8,128)(2,1)} %broadcast_select_fusion.refs_13_), channel_id=1, source_target_pairs={{0,12},{1,13},{2,14},{3,15},{4,0},{5,1},{6,2},{7,3},{8,4},{9,5},{1... | collective-permute-start | bytes 1277960 | tf_op jit(solution)/shard_map/ppermute | solution.py:260
  65.3 15.8 %collective-permute-start.14 = (bf16[128,1664]{1,0:T(8,128)(2,1)S(1)}, bf16[128,1664]{1,0:T(8,128)(2,1)}, u32[]{:S(2)}, u32[]{:S(2)}) collective-permute-start(bf16[128,1664]{1,0:T(8,128)(2,1)S(1)} %collective-permute-done.12.refs_18_), channel_id=1, source_target_pairs={{0,64},{1,65},{2,66},{3,67},{4,68},{5,69},{6,70},{7,71},{8,72},{9,... | collective-permute-start | bytes 1277960 | tf_op jit(solution)/shard_map/ppermute | solution.py:260
  68.0 13.2 %collective-permute-start.13 = (bf16[128,1664]{1,0:T(8,128)(2,1)S(1)}, bf16[128,1664]{1,0:T(8,128)(2,1)}, u32[]{:S(2)}, u32[]{:S(2)}) collective-permute-start(bf16[128,1664]{1,0:T(8,128)(2,1)S(1)} %collective-permute-done.12.refs_18_), channel_id=1, source_target_pairs={{0,192},{1,193},{2,194},{3,195},{4,196},{5,197},{6,198},{7,199},{8... | collective-permute-start | bytes 1277960 | tf_op jit(solution)/shard_map/ppermute | solution.py:260
  81.1 17.8 %collective-permute-start.19 = (bf16[4,128,1664]{2,1,0:T(8,128)(2,1)S(1)}, bf16[4,128,1664]{2,1,0:T(8,128)(2,1)}, u32[]{:S(2)}, u32[]{:S(2)}) collective-permute-start(bf16[4,128,1664]{2,1,0:T(8,128)(2,1)S(1)} %pad_maximum_fusion.refs_17_), channel_id=1, source_target_pairs={{0,16},{1,17},{2,18},{3,19},{4,20},{5,21},{6,22},{7,23},{8,24},{9,... | collective-permute-start | bytes 5111816 | tf_op jit(solution)/shard_map/ppermute | solution.py:260
  87.5 11.4 %collective-permute-start.18 = (bf16[3,128,1664]{2,1,0:T(8,128)(2,1)}, bf16[3,128,1664]{2,1,0:T(8,128)(2,1)S(1)}, u32[]{:S(2)}, u32[]{:S(2)}) collective-permute-start(bf16[3,128,1664]{2,1,0:T(8,128)(2,1)} %pad_maximum_fusion.1), channel_id=1, source_target_pairs={{0,16},{1,17},{2,18},{3,19},{4,20},{5,21},{6,22},{7,23},{8,24},{9,... | collective-permute-start | bytes 3833864 | tf_op jit(solution)/shard_map/ppermute | solution.py:260
  88.6 10.3 %collective-permute-start.21 = (bf16[128,1664]{1,0:T(8,128)(2,1)}, bf16[128,1664]{1,0:T(8,128)(2,1)}, u32[]{:S(2)}, u32[]{:S(2)}) collective-permute-start(bf16[128,1664]{1,0:T(8,128)(2,1)} %collective-permute-done.14.refs_19_), channel_id=1, source_target_pairs={{0,64},{1,65},{2,66},{3,67},{4,68},{5,69},{6,70},{7,71},{8,72},{9,... | collective-permute-start | bytes 1277960 | tf_op jit(solution)/shard_map/ppermute | solution.py:260
  91.4 7.5 %collective-permute-start.20 = (bf16[128,1664]{1,0:T(8,128)(2,1)}, bf16[128,1664]{1,0:T(8,128)(2,1)S(1)}, u32[]{:S(2)}, u32[]{:S(2)}) collective-permute-start(bf16[128,1664]{1,0:T(8,128)(2,1)} %collective-permute-done.16.refs_14_), channel_id=1, source_target_pairs={{0,4},{1,5},{2,6},{3,7},{4,8},{5,9},{6,10},{7,11},{8,12},{9,13},{1... | collective-permute-start | bytes 1277960 | tf_op jit(solution)/shard_map/ppermute | solution.py:260
  98.9 3.1 %collective-permute-start.22 = (bf16[128,1664]{1,0:T(8,128)(2,1)}, bf16[128,1664]{1,0:T(8,128)(2,1)S(1)}, u32[]{:S(2)}, u32[]{:S(2)}) collective-permute-start(bf16[128,1664]{1,0:T(8,128)(2,1)} %collective-permute-done.21.refs_20_), channel_id=1, source_target_pairs={{0,16},{1,17},{2,18},{3,19},{4,20},{5,21},{6,22},{7,23},{8,24},{9,... | collective-permute-start | bytes 1277960 | tf_op jit(solution)/shard_map/ppermute | solution.py:260
  101.7 36.6 %copy-start.5 = (f32[128]{0:T(128)S(1)}, f32[128]{0:T(128)}, u32[]{:S(2)}) copy-start(f32[128]{0:T(128)} %param.7) | copy-start | bytes 1540
  114.3 45.9 %copy-start.1 = (f32[32,128,128]{2,1,0:T(8,128)S(1)}, f32[32,128,128]{2,1,0:T(8,128)}, u32[]{:S(2)}) copy-start(f32[32,128,128]{2,1,0:T(8,128)} %get-tuple-element.54.refs_2_) | copy-start | bytes 6291460
  114.3 45.9 %copy-start.3 = (s32[32,3]{1,0:T(8,128)S(1)}, s32[32,3]{1,0:T(8,128)}, u32[]{:S(2)}) copy-start(s32[32,3]{1,0:T(8,128)} %copy.16.refs_1_) | copy-start | bytes 1156
  114.3 45.9 %copy-start.6 = (s32[2]{0:T(128)S(1)}, s32[2]{0:T(128)}, u32[]{:S(2)}) copy-start(s32[2]{0:T(128)} %pad_add_fusion.1.refs_0_) | copy-start | bytes 28
  (13 other events, 109.9 us)

commit v5 on v4

--- a/solution.py
+++ b/solution.py
@@ -289,7 +289,7 @@
     return lax.optimization_barrier(arrays[::-1])[::-1]
 
 
-def gather(mine):
+def gather(mine, small):
     z = lax.axis_index("col") % NZ
     middle = (z == 1) | (z == 2)
     inside = (1, 2)
@@ -312,7 +312,9 @@
     far13, one2, two2 = along_x(one13, 1), along_x(z2, 1), along_x(z2, -1)
     near_c, back_c = along_y(over, 1), along_y(over, -1)
     line = jnp.stack([mine, near, rim, back])
-    far13, one2, two2, near_c, back_c, line = together(far13, one2, two2, near_c, back_c, line)
+    far13, one2, two2, near_c, back_c, line, *small = together(
+        far13, one2, two2, near_c, back_c, line, *small
+    )
 
     far2, rim_c = along_x(one2, 1), along_y(near_c, 1)
     twin, twin_c = sibling(line), sibling(jnp.stack([over, near_c, back_c]))
@@ -327,7 +329,7 @@
     cols = [line, over, near_c, rim_c, back_c, twin, twin_c, rim_twin]
     col_plan = [tuple((k, k) for k in range(NY))] + [((k, None),) for k in range(NY, 2 * NY)]
     col_plan += [tuple((8 + k, k) for k in range(NY)), ((12, 0), (13, 1), (15, 2)), ((14, None),)]
-    return rows, row_plan, cols, col_plan
+    return rows, row_plan, cols, col_plan, small
 
 
 def spots():
@@ -368,9 +370,11 @@
         out_specs=VM,
         compiler_params=params,
     )(features, targets[None, :])
-    row_pieces, row_plan, col_pieces, col_plan = gather(packed)
     row_spot, col_spot = spots()
     tiles, ready = in_order(pairs, count, row_spot, col_spot)
+    small = (place, tiles, ready, row_spot, col_spot)
+    row_pieces, row_plan, col_pieces, col_plan, small = gather(packed, small)
+    place, tiles, ready, row_spot, col_spot = small
 
     accumulators = [
         pltpu.VMEM((n_col, block, block), f32),

time: 186 us -> 183 us (0.984)
  other arithmetic: 8.85 us -> 3.19 us
  waiting for transfers between devices: 41.6 us -> 46.1 us
  starting transfers between devices: 45.9 us -> 42.8 us
    ppermute x19, waiting for transfers between devices: 28 us -> 35.2 us  [send(): return lax.ppermute(array, AXES, pairs)]
    ppermute x4, waiting for transfers between devices: 13.6 us -> 10.9 us  [along_z(): return lax.ppermute(array, AXES, pairs)]
    ppermute x19, starting transfers between devices: 38 us -> 35.6 us  [send(): return lax.ppermute(array, AXES, pairs)]
    another operation x1, other arithmetic: 2.37 us -> 0.17 us  [gather(): twin, twin_c = (sibling(line), sibling(jnp.stack([over, near_c, back_c])))]
  transfers between devices with their start and end apart: 23 -> 23, of which waited for: 9 -> 9; matrix products, arithmetic and copies ran while one was open for 6% -> 3% of each run, Pallas kernels for 0% -> 0%
where the time goes in v5:
time: 183 us
  blocking collectives  68.1 us (37%)
  waiting for transfers between devices  46.1 us (25%)
  starting transfers between devices  42.8 us (23%)
  Pallas kernels  15.3 us (8%)
  local copies, waits for them, and re-layouts  5.73 us (3%)
  other arithmetic  3.19 us (2%)
    all_to_all x3, blocking collectives, swap(): return lax.all_to_all(slots, AXES, 0, 0, tiled=True)  68.1 us
    ppermute x19, starting transfers between devices, send(): return lax.ppermute(array, AXES, pairs)  35.6 us
    ppermute x19, waiting for transfers between devices, send(): return lax.ppermute(array, AXES, pairs)  35.2 us
    pallas_call x1, Pallas kernels, body(): pl.pallas_call(lambda *refs: first_sweep_kernel(row_plan, col_plan, width...  11.5 us
    ppermute x4, waiting for transfers between devices, along_z(): return lax.ppermute(array, AXES, pairs)  10.9 us
    ppermute x4, starting transfers between devices, along_z(): return lax.ppermute(array, AXES, pairs)  7.23 us
  transfers between devices with their start and end apart: 23, of which 9 were waited for; matrix products, arithmetic and copies ran while one was open for 3% of the time, Pallas kernels for 0%

profile of v5, /device:TPU:1, one launch (start us, length us, event | category | flops | bytes accessed | tf_op | source)
XLA Modules:
  0.0 183.0 jit_solution(7950013682875206035)
XLA Ops:
  0.6 1.0 copy-done.2
  2.5 5.3 %collective-permute-start.5 = (bf16[128,1664]{1,0:T(8,128)(2,1)S(1)}, bf16[128,1664]{1,0:T(8,128)(2,1)S(1)}, u32[]{:S(2)}, u32[]{:S(2)}) collective-permute-start(bf16[128,1664]{1,0:T(8,128)(2,1)S(1)} %shard_map.77.refs_5_), channel_id=1, source_target_pairs={{0,3},{1,2},{2,1},{3,0},{4,7},{5,6},{6,5},{7,4},{8,11},{9,10},{10,... | collective-permute-start | bytes 1277960 | tf_op jit(solution)/shard_map/ppermute | solution.py:269
  7.8 2.5 %collective-permute-start.3 = (bf16[128,1664]{1,0:T(8,128)(2,1)S(1)}, bf16[128,1664]{1,0:T(8,128)(2,1)S(1)}, u32[]{:S(2)}, u32[]{:S(2)}) collective-permute-start(bf16[128,1664]{1,0:T(8,128)(2,1)S(1)} %shard_map.77.refs_5_), channel_id=1, source_target_pairs={{0,4},{1,5},{2,6},{3,7},{4,8},{5,9},{6,10},{7,11},{8,12},{9,13},{1... | collective-permute-start | bytes 1277960 | tf_op jit(solution)/shard_map/ppermute | solution.py:260
  10.3 2.7 %collective-permute-start.1 = (bf16[128,1664]{1,0:T(8,128)(2,1)S(1)}, bf16[128,1664]{1,0:T(8,128)(2,1)S(1)}, u32[]{:S(2)}, u32[]{:S(2)}) collective-permute-start(bf16[128,1664]{1,0:T(8,128)(2,1)S(1)} %shard_map.77.refs_5_), channel_id=1, source_target_pairs={{0,64},{1,65},{2,66},{3,67},{4,68},{5,69},{6,70},{7,71},{8,72},{9,... | collective-permute-start | bytes 1277960 | tf_op jit(solution)/shard_map/ppermute | solution.py:260
  13.7 0.7 dynamic-slice_bitcast_fusion
  15.1 1.3 collective-permute-done.5
  16.4 2.3 %collective-permute-start = (bf16[128,1664]{1,0:T(8,128)(2,1)S(1)}, bf16[128,1664]{1,0:T(8,128)(2,1)S(1)}, u32[]{:S(2)}, u32[]{:S(2)}) collective-permute-start(bf16[128,1664]{1,0:T(8,128)(2,1)S(1)} %shard_map.77.refs_5_), channel_id=1, source_target_pairs={{0,192},{1,193},{2,194},{3,195},{4,196},{5,197},{6,198},{7,199},{8... | collective-permute-start | bytes 1277960 | tf_op jit(solution)/shard_map/ppermute | solution.py:260
  18.7 0.8 slice_bitcast_fusion
  19.7 7.6 %collective-permute-done.4 = bf16[128,1664]{1,0:T(8,128)(2,1)S(1)} collective-permute-done((bf16[128,1664]{1,0:T(8,128)(2,1)S(1)}, bf16[128,1664]{1,0:T(8,128)(2,1)S(1)}, u32[]{:S(2)}, u32[]{:S(2)}) %collective-permute-start.4) | collective-permute-done | bytes 426016 | tf_op jit(solution)/shard_map/ppermute | solution.py:269
  27.3 5.4 %collective-permute-start.12 = (bf16[128,1664]{1,0:T(8,128)(2,1)S(1)}, bf16[128,1664]{1,0:T(8,128)(2,1)S(1)}, u32[]{:S(2)}, u32[]{:S(2)}) collective-permute-start(bf16[128,1664]{1,0:T(8,128)(2,1)S(1)} %shard_map.77.refs_5_), channel_id=1, source_target_pairs={{0,32},{1,33},{2,34},{3,35},{4,36},{5,37},{6,38},{7,39},{8,40},{9,... | collective-permute-start | bytes 1277960 | tf_op jit(solution)/shard_map/ppermute | solution.py:260
  32.8 2.6 %collective-permute-start.11 = (bf16[2,128,1664]{2,1,0:T(8,128)(2,1)S(1)}, bf16[2,128,1664]{2,1,0:T(8,128)(2,1)S(1)}, u32[]{:S(2)}, u32[]{:S(2)}) collective-permute-start(bf16[2,128,1664]{2,1,0:T(8,128)(2,1)S(1)} %pad_maximum_fusion.2.refs_9_), channel_id=1, source_target_pairs={{0,4},{1,5},{2,6},{3,7},{4,8},{5,9},{6,10},{7,11},{8,12},{9,13},{1... | collective-permute-start | bytes 2555912 | tf_op jit(solution)/shard_map/ppermute | solution.py:260
  35.4 2.7 %collective-permute-start.6 = (bf16[128,1664]{1,0:T(8,128)(2,1)S(1)}, bf16[128,1664]{1,0:T(8,128)(2,1)S(1)}, u32[]{:S(2)}, u32[]{:S(2)}) collective-permute-start(bf16[128,1664]{1,0:T(8,128)(2,1)S(1)} %collective-permute-done.1), channel_id=1, source_target_pairs={{0,64},{1,65},{2,66},{3,67},{4,68},{5,69},{6,70},{7,71},{8,72},{9,... | collective-permute-start | bytes 1277960 | tf_op jit(solution)/shard_map/ppermute | solution.py:260
  38.5 1.3 collective-permute-start.8
  39.8 4.8 %collective-permute-done.12.refs_18_ = bf16[128,1664]{1,0:T(8,128)(2,1)S(1)} collective-permute-done((bf16[128,1664]{1,0:T(8,128)(2,1)S(1)}, bf16[128,1664]{1,0:T(8,128)(2,1)S(1)}, u32[]{:S(2)}, u32[]{:S(2)}) %collective-permute-start.12) | collective-permute-done | bytes 426016 | tf_op jit(solution)/shard_map/ppermute | solution.py:260
  45.3 2.6 %collective-permute-start.7 = (bf16[128,1664]{1,0:T(8,128)(2,1)S(1)}, bf16[128,1664]{1,0:T(8,128)(2,1)S(1)}, u32[]{:S(2)}, u32[]{:S(2)}) collective-permute-start(bf16[128,1664]{1,0:T(8,128)(2,1)S(1)} %collective-permute-done.3.refs_6_), channel_id=1, source_target_pairs={{0,4},{1,5},{2,6},{3,7},{4,8},{5,9},{6,10},{7,11},{8,12},{9,13},{1... | collective-permute-start | bytes 1277960 | tf_op jit(solution)/shard_map/ppermute | solution.py:260
  48.4 10.3 %collective-permute-done.7.refs_7_ = bf16[128,1664]{1,0:T(8,128)(2,1)S(1)} collective-permute-done((bf16[128,1664]{1,0:T(8,128)(2,1)S(1)}, bf16[128,1664]{1,0:T(8,128)(2,1)S(1)}, u32[]{:S(2)}, u32[]{:S(2)}) %collective-permute-start.7) | collective-permute-done | bytes 426016 | tf_op jit(solution)/shard_map/ppermute | solution.py:260
  58.7 1.9 %collective-permute-done.8 = bf16[128,1664]{1,0:T(8,128)(2,1)S(1)} collective-permute-done((bf16[128,1664]{1,0:T(8,128)(2,1)S(1)}, bf16[128,1664]{1,0:T(8,128)(2,1)S(1)}, u32[]{:S(2)}, u32[]{:S(2)}) %collective-permute-start.8) | collective-permute-done | bytes 426016 | tf_op jit(solution)/shard_map/ppermute | solution.py:269
  60.7 2.6 %collective-permute-start.17 = (bf16[2,128,1664]{2,1,0:T(8,128)(2,1)S(1)}, bf16[2,128,1664]{2,1,0:T(8,128)(2,1)S(1)}, u32[]{:S(2)}, u32[]{:S(2)}) collective-permute-start(bf16[2,128,1664]{2,1,0:T(8,128)(2,1)S(1)} %collective-permute-done.11.refs_10_), channel_id=1, source_target_pairs={{0,4},{1,5},{2,6},{3,7},{4,8},{5,9},{6,10},{7,11},{8,12},{9,13},{1... | collective-permute-start | bytes 2555912 | tf_op jit(solution)/shard_map/ppermute | solution.py:260
  63.9 0.9 collective-permute-start.15
  64.9 2.1 %collective-permute-start.14 = (bf16[128,1664]{1,0:T(8,128)(2,1)S(1)}, bf16[128,1664]{1,0:T(8,128)(2,1)S(1)}, u32[]{:S(2)}, u32[]{:S(2)}) collective-permute-start(bf16[128,1664]{1,0:T(8,128)(2,1)S(1)} %collective-permute-done.12.refs_18_), channel_id=1, source_target_pairs={{0,64},{1,65},{2,66},{3,67},{4,68},{5,69},{6,70},{7,71},{8,72},{9,... | collective-permute-start | bytes 1277960 | tf_op jit(solution)/shard_map/ppermute | solution.py:260
  68.1 14.0 %collective-permute-done.16.refs_14_ = bf16[128,1664]{1,0:T(8,128)(2,1)S(1)} collective-permute-done((bf16[128,1664]{1,0:T(8,128)(2,1)S(1)}, bf16[128,1664]{1,0:T(8,128)(2,1)S(1)}, u32[]{:S(2)}, u32[]{:S(2)}) %collective-permute-start.16) | collective-permute-done | bytes 426016 | tf_op jit(solution)/shard_map/ppermute | solution.py:260
  82.1 3.5 %collective-permute-start.19 = (bf16[4,128,1664]{2,1,0:T(8,128)(2,1)S(1)}, bf16[4,128,1664]{2,1,0:T(8,128)(2,1)S(1)}, u32[]{:S(2)}, u32[]{:S(2)}) collective-permute-start(bf16[4,128,1664]{2,1,0:T(8,128)(2,1)S(1)} %pad_maximum_fusion.refs_17_), channel_id=1, source_target_pairs={{0,16},{1,17},{2,18},{3,19},{4,20},{5,21},{6,22},{7,23},{8,24},{9,... | collective-permute-start | bytes 5111816 | tf_op jit(solution)/shard_map/ppermute | solution.py:260
  86.1 2.5 %collective-permute-start.21 = (bf16[128,1664]{1,0:T(8,128)(2,1)S(1)}, bf16[128,1664]{1,0:T(8,128)(2,1)}, u32[]{:S(2)}, u32[]{:S(2)}) collective-permute-start(bf16[128,1664]{1,0:T(8,128)(2,1)S(1)} %collective-permute-done.14.refs_19_), channel_id=1, source_target_pairs={{0,64},{1,65},{2,66},{3,67},{4,68},{5,69},{6,70},{7,71},{8,72},{9,... | collective-permute-start | bytes 1277960 | tf_op jit(solution)/shard_map/ppermute | solution.py:260
  88.6 4.7 %collective-permute-done.20.refs_15_ = bf16[128,1664]{1,0:T(8,128)(2,1)S(1)} collective-permute-done((bf16[128,1664]{1,0:T(8,128)(2,1)S(1)}, bf16[128,1664]{1,0:T(8,128)(2,1)S(1)}, u32[]{:S(2)}, u32[]{:S(2)}) %collective-permute-start.20) | collective-permute-done | bytes 426016 | tf_op jit(solution)/shard_map/ppermute | solution.py:260
  93.7 1.3 copy-done.9
  95.0 2.4 %collective-permute-start.22 = (bf16[128,1664]{1,0:T(8,128)(2,1)}, bf16[128,1664]{1,0:T(8,128)(2,1)}, u32[]{:S(2)}, u32[]{:S(2)}) collective-permute-start(bf16[128,1664]{1,0:T(8,128)(2,1)} %collective-permute-done.21.refs_20_), channel_id=1, source_target_pairs={{0,16},{1,17},{2,18},{3,19},{4,20},{5,21},{6,22},{7,23},{8,24},{9,... | collective-permute-start | bytes 1277960 | tf_op jit(solution)/shard_map/ppermute | solution.py:260
  98.1 1.1 collective-permute-done.22.refs_24_
  99.1 11.5 %shard_map.78 = (f32[32,128,128]{2,1,0:T(8,128)}, f32[256,128]{1,0:T(8,128)}) custom-call(s32[2]{0:T(128)} %pad_add_fusion.1.refs_0_, s32[32,3]{1,0:T(8,128)} %copy.16.refs_1_, s32[4]{0:T(128)} %and_select_fusion.refs_2_, s32[16]{0:T(128)} %copy-done.24, s32[16]{0:T(128)} %copy-done.25, bf16[128,1664]{1,0:T(8,128)(2,1)} %copy-done, ...), custom_call_target="tpu_custom_call" | custom-call | tf_op jit(solution)/shard_map/pallas_call | solution.py:383
  110.7 25.4 %all_to_all.33 = f32[256,1,128]{2,1,0:T(1,128)S(1)} all-to-all(f32[256,1,128]{2,1,0:T(1,128)} %bitcast.53), channel_id=1, replica_groups=mesh['row'=16,'col'=16] {'row','col'}, dimensions={0} | all-to-all | bytes 262144 | tf_op jit(solution)/shard_map/all_to_all | solution.py:239
  136.4 21.5 %all_to_all.34 = f32[256,1,256]{2,1,0:T(1,128)S(1)} all-to-all(f32[256,1,256]{2,1,0:T(1,128)S(1)} %copy.15), channel_id=1, replica_groups=mesh['row'=16,'col'=16] {'row','col'}, dimensions={0} | all-to-all | bytes 524288 | tf_op jit(solution)/shard_map/all_to_all | solution.py:239
  157.9 2.9 %shard_map.80 = (f32[256,256]{1,0:T(8,128)S(1)}, f32[8,128]{1,0:T(8,128)S(1)}) custom-call(s32[2]{0:T(128)S(1)} %copy-done.6, s32[32,3]{1,0:T(8,128)S(1)} %copy-done.3, f32[32,128,128]{2,1,0:T(8,128)S(1)} %copy-done.1, f32[256,256]{1,0:T(8,128)S(1)} %bitcast.40), custom_call_target="tpu_custom_call" | custom-call | tf_op jit(solution)/shard_map/pallas_call | solution.py:412
  161.1 21.3 %all_to_all.35 = f32[256,1,256]{2,1,0:T(1,128)S(1)} all-to-all(f32[256,1,256]{2,1,0:T(1,128)S(1)} %copy.17), channel_id=1, replica_groups=mesh['row'=16,'col'=16] {'row','col'}, dimensions={0} | all-to-all | bytes 524288 | tf_op jit(solution)/shard_map/all_to_all | solution.py:239
  (97 shorter events, 8.1 us)
Async XLA Ops:
  2.5 65.5 %copy-start = (bf16[128,1664]{1,0:T(8,128)(2,1)}, bf16[128,1664]{1,0:T(8,128)(2,1)S(1)}, u32[]{:S(2)}) copy-start(bf16[128,1664]{1,0:T(8,128)(2,1)S(1)} %shard_map.77.refs_5_) | copy-start | bytes 1277956
  2.5 13.9 %collective-permute-start.5 = (bf16[128,1664]{1,0:T(8,128)(2,1)S(1)}, bf16[128,1664]{1,0:T(8,128)(2,1)S(1)}, u32[]{:S(2)}, u32[]{:S(2)}) collective-permute-start(bf16[128,1664]{1,0:T(8,128)(2,1)S(1)} %shard_map.77.refs_5_), channel_id=1, source_target_pairs={{0,3},{1,2},{2,1},{3,0},{4,7},{5,6},{6,5},{7,4},{8,11},{9,10},{10,... | collective-permute-start | bytes 1277960 | tf_op jit(solution)/shard_map/ppermute | solution.py:269
  7.8 19.5 %collective-permute-start.4 = (bf16[128,1664]{1,0:T(8,128)(2,1)S(1)}, bf16[128,1664]{1,0:T(8,128)(2,1)S(1)}, u32[]{:S(2)}, u32[]{:S(2)}) collective-permute-start(bf16[128,1664]{1,0:T(8,128)(2,1)S(1)} %shard_map.77.refs_5_), channel_id=1, source_target_pairs={{0,1},{1,0},{2,3},{3,2},{4,5},{5,4},{6,7},{7,6},{8,9},{9,8},{10,11... | collective-permute-start | bytes 1277960 | tf_op jit(solution)/shard_map/ppermute | solution.py:269
  7.8 24.9 %collective-permute-start.3 = (bf16[128,1664]{1,0:T(8,128)(2,1)S(1)}, bf16[128,1664]{1,0:T(8,128)(2,1)S(1)}, u32[]{:S(2)}, u32[]{:S(2)}) collective-permute-start(bf16[128,1664]{1,0:T(8,128)(2,1)S(1)} %shard_map.77.refs_5_), channel_id=1, source_target_pairs={{0,4},{1,5},{2,6},{3,7},{4,8},{5,9},{6,10},{7,11},{8,12},{9,13},{1... | collective-permute-start | bytes 1277960 | tf_op jit(solution)/shard_map/ppermute | solution.py:260
  10.3 22.4 %collective-permute-start.2 = (bf16[128,1664]{1,0:T(8,128)(2,1)S(1)}, bf16[128,1664]{1,0:T(8,128)(2,1)S(1)}, u32[]{:S(2)}, u32[]{:S(2)}) collective-permute-start(bf16[128,1664]{1,0:T(8,128)(2,1)S(1)} %shard_map.77.refs_5_), channel_id=1, source_target_pairs={{0,12},{1,13},{2,14},{3,15},{4,0},{5,1},{6,2},{7,3},{8,4},{9,5},{1... | collective-permute-start | bytes 1277960 | tf_op jit(solution)/shard_map/ppermute | solution.py:260
  10.3 22.4 %collective-permute-start.1 = (bf16[128,1664]{1,0:T(8,128)(2,1)S(1)}, bf16[128,1664]{1,0:T(8,128)(2,1)S(1)}, u32[]{:S(2)}, u32[]{:S(2)}) collective-permute-start(bf16[128,1664]{1,0:T(8,128)(2,1)S(1)} %shard_map.77.refs_5_), channel_id=1, source_target_pairs={{0,64},{1,65},{2,66},{3,67},{4,68},{5,69},{6,70},{7,71},{8,72},{9,... | collective-permute-start | bytes 1277960 | tf_op jit(solution)/shard_map/ppermute | solution.py:260
  14.4 53.6 %copy-start.24 = (s32[16]{0:T(128)}, s32[16]{0:T(128)S(1)}, u32[]{:S(2)}) copy-start(s32[16]{0:T(128)S(1)} %get-tuple-element.49.refs_3_) | copy-start | bytes 196
  14.4 53.6 %copy-start.25 = (s32[16]{0:T(128)}, s32[16]{0:T(128)S(1)}, u32[]{:S(2)}) copy-start(s32[16]{0:T(128)S(1)} %get-tuple-element.50.refs_4_) | copy-start | bytes 196
  16.4 16.3 %collective-permute-start = (bf16[128,1664]{1,0:T(8,128)(2,1)S(1)}, bf16[128,1664]{1,0:T(8,128)(2,1)S(1)}, u32[]{:S(2)}, u32[]{:S(2)}) collective-permute-start(bf16[128,1664]{1,0:T(8,128)(2,1)S(1)} %shard_map.77.refs_5_), channel_id=1, source_target_pairs={{0,192},{1,193},{2,194},{3,195},{4,196},{5,197},{6,198},{7,199},{8... | collective-permute-start | bytes 1277960 | tf_op jit(solution)/shard_map/ppermute | solution.py:260
  27.3 17.3 %collective-permute-start.12 = (bf16[128,1664]{1,0:T(8,128)(2,1)S(1)}, bf16[128,1664]{1,0:T(8,128)(2,1)S(1)}, u32[]{:S(2)}, u32[]{:S(2)}) collective-permute-start(bf16[128,1664]{1,0:T(8,128)(2,1)S(1)} %shard_map.77.refs_5_), channel_id=1, source_target_pairs={{0,32},{1,33},{2,34},{3,35},{4,36},{5,37},{6,38},{7,39},{8,40},{9,... | collective-permute-start | bytes 1277960 | tf_op jit(solution)/shard_map/ppermute | solution.py:260
  32.8 35.2 %copy-start.8 = (bf16[2,128,1664]{2,1,0:T(8,128)(2,1)}, bf16[2,128,1664]{2,1,0:T(8,128)(2,1)S(1)}, u32[]{:S(2)}) copy-start(bf16[2,128,1664]{2,1,0:T(8,128)(2,1)S(1)} %pad_maximum_fusion.2.refs_9_) | copy-start | bytes 2555908
  32.8 27.8 %collective-permute-start.11 = (bf16[2,128,1664]{2,1,0:T(8,128)(2,1)S(1)}, bf16[2,128,1664]{2,1,0:T(8,128)(2,1)S(1)}, u32[]{:S(2)}, u32[]{:S(2)}) collective-permute-start(bf16[2,128,1664]{2,1,0:T(8,128)(2,1)S(1)} %pad_maximum_fusion.2.refs_9_), channel_id=1, source_target_pairs={{0,4},{1,5},{2,6},{3,7},{4,8},{5,9},{6,10},{7,11},{8,12},{9,13},{1... | collective-permute-start | bytes 2555912 | tf_op jit(solution)/shard_map/ppermute | solution.py:260
  35.4 25.3 %collective-permute-start.10 = (bf16[2,128,1664]{2,1,0:T(8,128)(2,1)S(1)}, bf16[2,128,1664]{2,1,0:T(8,128)(2,1)S(1)}, u32[]{:S(2)}, u32[]{:S(2)}) collective-permute-start(bf16[2,128,1664]{2,1,0:T(8,128)(2,1)S(1)} %pad_maximum_fusion.2.refs_9_), channel_id=1, source_target_pairs={{0,12},{1,13},{2,14},{3,15},{4,0},{5,1},{6,2},{7,3},{8,4},{9,5},{1... | collective-permute-start | bytes 2555912 | tf_op jit(solution)/shard_map/ppermute | solution.py:260
  35.4 9.9 %collective-permute-start.6 = (bf16[128,1664]{1,0:T(8,128)(2,1)S(1)}, bf16[128,1664]{1,0:T(8,128)(2,1)S(1)}, u32[]{:S(2)}, u32[]{:S(2)}) collective-permute-start(bf16[128,1664]{1,0:T(8,128)(2,1)S(1)} %collective-permute-done.1), channel_id=1, source_target_pairs={{0,64},{1,65},{2,66},{3,67},{4,68},{5,69},{6,70},{7,71},{8,72},{9,... | collective-permute-start | bytes 1277960 | tf_op jit(solution)/shard_map/ppermute | solution.py:260
  38.5 22.2 %collective-permute-start.8 = (bf16[128,1664]{1,0:T(8,128)(2,1)S(1)}, bf16[128,1664]{1,0:T(8,128)(2,1)S(1)}, u32[]{:S(2)}, u32[]{:S(2)}) collective-permute-start(bf16[128,1664]{1,0:T(8,128)(2,1)S(1)} %collective-permute-done.5), channel_id=1, source_target_pairs={{1,0},{2,3},{5,4},{6,7},{9,8},{10,11},{13,12},{14,15},{17,16},{18,... | collective-permute-start | bytes 1277960 | tf_op jit(solution)/shard_map/ppermute | solution.py:269
  44.6 41.0 %copy-start.10 = (bf16[128,1664]{1,0:T(8,128)(2,1)}, bf16[128,1664]{1,0:T(8,128)(2,1)S(1)}, u32[]{:S(2)}) copy-start(bf16[128,1664]{1,0:T(8,128)(2,1)S(1)} %collective-permute-done.12.refs_18_) | copy-start | bytes 1277956
  44.6 16.1 %collective-permute-start.9 = (bf16[128,1664]{1,0:T(8,128)(2,1)S(1)}, bf16[128,1664]{1,0:T(8,128)(2,1)S(1)}, u32[]{:S(2)}, u32[]{:S(2)}) collective-permute-start(bf16[128,1664]{1,0:T(8,128)(2,1)S(1)} %collective-permute-done.4), channel_id=1, source_target_pairs={{1,2},{2,1},{5,6},{6,5},{9,10},{10,9},{13,14},{14,13},{17,18},{18,... | collective-permute-start | bytes 1277960 | tf_op jit(solution)/shard_map/ppermute | solution.py:269
  45.3 13.4 %collective-permute-start.7 = (bf16[128,1664]{1,0:T(8,128)(2,1)S(1)}, bf16[128,1664]{1,0:T(8,128)(2,1)S(1)}, u32[]{:S(2)}, u32[]{:S(2)}) collective-permute-start(bf16[128,1664]{1,0:T(8,128)(2,1)S(1)} %collective-permute-done.3.refs_6_), channel_id=1, source_target_pairs={{0,4},{1,5},{2,6},{3,7},{4,8},{5,9},{6,10},{7,11},{8,12},{9,13},{1... | collective-permute-start | bytes 1277960 | tf_op jit(solution)/shard_map/ppermute | solution.py:260
  60.7 21.4 %collective-permute-start.17 = (bf16[2,128,1664]{2,1,0:T(8,128)(2,1)S(1)}, bf16[2,128,1664]{2,1,0:T(8,128)(2,1)S(1)}, u32[]{:S(2)}, u32[]{:S(2)}) collective-permute-start(bf16[2,128,1664]{2,1,0:T(8,128)(2,1)S(1)} %collective-permute-done.11.refs_10_), channel_id=1, source_target_pairs={{0,4},{1,5},{2,6},{3,7},{4,8},{5,9},{6,10},{7,11},{8,12},{9,13},{1... | collective-permute-start | bytes 2555912 | tf_op jit(solution)/shard_map/ppermute | solution.py:260
  63.3 18.7 %collective-permute-start.16 = (bf16[128,1664]{1,0:T(8,128)(2,1)S(1)}, bf16[128,1664]{1,0:T(8,128)(2,1)S(1)}, u32[]{:S(2)}, u32[]{:S(2)}) collective-permute-start(bf16[128,1664]{1,0:T(8,128)(2,1)S(1)} %broadcast_select_fusion.refs_13_), channel_id=1, source_target_pairs={{0,4},{1,5},{2,6},{3,7},{4,8},{5,9},{6,10},{7,11},{8,12},{9,13},{1... | collective-permute-start | bytes 1277960 | tf_op jit(solution)/shard_map/ppermute | solution.py:260
  63.9 18.1 %collective-permute-start.15 = (bf16[128,1664]{1,0:T(8,128)(2,1)S(1)}, bf16[128,1664]{1,0:T(8,128)(2,1)S(1)}, u32[]{:S(2)}, u32[]{:S(2)}) collective-permute-start(bf16[128,1664]{1,0:T(8,128)(2,1)S(1)} %broadcast_select_fusion.refs_13_), channel_id=1, source_target_pairs={{0,12},{1,13},{2,14},{3,15},{4,0},{5,1},{6,2},{7,3},{8,4},{9,5},{1... | collective-permute-start | bytes 1277960 | tf_op jit(solution)/shard_map/ppermute | solution.py:260
  64.9 17.2 %collective-permute-start.14 = (bf16[128,1664]{1,0:T(8,128)(2,1)S(1)}, bf16[128,1664]{1,0:T(8,128)(2,1)S(1)}, u32[]{:S(2)}, u32[]{:S(2)}) collective-permute-start(bf16[128,1664]{1,0:T(8,128)(2,1)S(1)} %collective-permute-done.12.refs_18_), channel_id=1, source_target_pairs={{0,64},{1,65},{2,66},{3,67},{4,68},{5,69},{6,70},{7,71},{8,72},{9,... | collective-permute-start | bytes 1277960 | tf_op jit(solution)/shard_map/ppermute | solution.py:260
  66.9 15.1 %collective-permute-start.13 = (bf16[128,1664]{1,0:T(8,128)(2,1)S(1)}, bf16[128,1664]{1,0:T(8,128)(2,1)S(1)}, u32[]{:S(2)}, u32[]{:S(2)}) collective-permute-start(bf16[128,1664]{1,0:T(8,128)(2,1)S(1)} %collective-permute-done.12.refs_18_), channel_id=1, source_target_pairs={{0,192},{1,193},{2,194},{3,195},{4,196},{5,197},{6,198},{7,199},{8... | collective-permute-start | bytes 1277960 | tf_op jit(solution)/shard_map/ppermute | solution.py:260
  82.1 11.6 %collective-permute-start.19 = (bf16[4,128,1664]{2,1,0:T(8,128)(2,1)S(1)}, bf16[4,128,1664]{2,1,0:T(8,128)(2,1)S(1)}, u32[]{:S(2)}, u32[]{:S(2)}) collective-permute-start(bf16[4,128,1664]{2,1,0:T(8,128)(2,1)S(1)} %pad_maximum_fusion.refs_17_), channel_id=1, source_target_pairs={{0,16},{1,17},{2,18},{3,19},{4,20},{5,21},{6,22},{7,23},{8,24},{9,... | collective-permute-start | bytes 5111816 | tf_op jit(solution)/shard_map/ppermute | solution.py:260
  85.7 7.9 %collective-permute-start.18 = (bf16[3,128,1664]{2,1,0:T(8,128)(2,1)S(1)}, bf16[3,128,1664]{2,1,0:T(8,128)(2,1)S(1)}, u32[]{:S(2)}, u32[]{:S(2)}) collective-permute-start(bf16[3,128,1664]{2,1,0:T(8,128)(2,1)S(1)} %pad_maximum_fusion.1), channel_id=1, source_target_pairs={{0,16},{1,17},{2,18},{3,19},{4,20},{5,21},{6,22},{7,23},{8,24},{9,... | collective-permute-start | bytes 3833864 | tf_op jit(solution)/shard_map/ppermute | solution.py:260
  85.8 7.4 %collective-permute-start.20 = (bf16[128,1664]{1,0:T(8,128)(2,1)S(1)}, bf16[128,1664]{1,0:T(8,128)(2,1)S(1)}, u32[]{:S(2)}, u32[]{:S(2)}) collective-permute-start(bf16[128,1664]{1,0:T(8,128)(2,1)S(1)} %collective-permute-done.16.refs_14_), channel_id=1, source_target_pairs={{0,4},{1,5},{2,6},{3,7},{4,8},{5,9},{6,10},{7,11},{8,12},{9,13},{1... | collective-permute-start | bytes 1277960 | tf_op jit(solution)/shard_map/ppermute | solution.py:260
  86.1 7.6 %collective-permute-start.21 = (bf16[128,1664]{1,0:T(8,128)(2,1)S(1)}, bf16[128,1664]{1,0:T(8,128)(2,1)}, u32[]{:S(2)}, u32[]{:S(2)}) collective-permute-start(bf16[128,1664]{1,0:T(8,128)(2,1)S(1)} %collective-permute-done.14.refs_19_), channel_id=1, source_target_pairs={{0,64},{1,65},{2,66},{3,67},{4,68},{5,69},{6,70},{7,71},{8,72},{9,... | collective-permute-start | bytes 1277960 | tf_op jit(solution)/shard_map/ppermute | solution.py:260
  95.0 4.1 %collective-permute-start.22 = (bf16[128,1664]{1,0:T(8,128)(2,1)}, bf16[128,1664]{1,0:T(8,128)(2,1)}, u32[]{:S(2)}, u32[]{:S(2)}) collective-permute-start(bf16[128,1664]{1,0:T(8,128)(2,1)} %collective-permute-done.21.refs_20_), channel_id=1, source_target_pairs={{0,16},{1,17},{2,18},{3,19},{4,20},{5,21},{6,22},{7,23},{8,24},{9,... | collective-permute-start | bytes 1277960 | tf_op jit(solution)/shard_map/ppermute | solution.py:260
  98.1 38.0 %copy-start.5 = (f32[128]{0:T(128)S(1)}, f32[128]{0:T(128)}, u32[]{:S(2)}) copy-start(f32[128]{0:T(128)} %param.7) | copy-start | bytes 1540
  110.7 47.2 %copy-start.1 = (f32[32,128,128]{2,1,0:T(8,128)S(1)}, f32[32,128,128]{2,1,0:T(8,128)}, u32[]{:S(2)}) copy-start(f32[32,128,128]{2,1,0:T(8,128)} %get-tuple-element.64.refs_2_) | copy-start | bytes 6291460
  110.7 47.2 %copy-start.3 = (s32[32,3]{1,0:T(8,128)S(1)}, s32[32,3]{1,0:T(8,128)}, u32[]{:S(2)}) copy-start(s32[32,3]{1,0:T(8,128)} %copy.16.refs_1_) | copy-start | bytes 1156
  110.7 47.2 %copy-start.6 = (s32[2]{0:T(128)S(1)}, s32[2]{0:T(128)}, u32[]{:S(2)}) copy-start(s32[2]{0:T(128)} %pad_add_fusion.1.refs_0_) | copy-start | bytes 28
  (17 other events, 194.7 us)

commit v6 on v5

--- a/solution.py
+++ b/solution.py
@@ -7,7 +7,7 @@
 from jax.sharding import PartitionSpec as P
 
 RIDGE = 1.0
-GROUP = 4
+GROUP = 8
 STAGES = 4
 AXES = ("row", "col")
 LANES = 128

time: 183 us -> 184 us (level)
  no operation moved by 1% of the time
where the time goes in v6:
time: 184 us; the launch traced here: 183 us
  blocking collectives  69.4 us (38%)
  waiting for transfers between devices  46.1 us (25%)
  starting transfers between devices  42.8 us (23%)
  Pallas kernels  14.2 us (8%)
  local copies, waits for them, and re-layouts  5.73 us (3%)
  other arithmetic  3.19 us (2%)
    all_to_all x3, blocking collectives, swap(): return lax.all_to_all(slots, AXES, 0, 0, tiled=True)  69.4 us
    ppermute x19, starting transfers between devices, send(): return lax.ppermute(array, AXES, pairs)  35.6 us
    ppermute x19, waiting for transfers between devices, send(): return lax.ppermute(array, AXES, pairs)  35.2 us
    ppermute x4, waiting for transfers between devices, along_z(): return lax.ppermute(array, AXES, pairs)  10.9 us
    pallas_call x1, Pallas kernels, body(): pl.pallas_call(lambda *refs: first_sweep_kernel(row_plan, col_plan, width...  10.5 us
    ppermute x4, starting transfers between devices, along_z(): return lax.ppermute(array, AXES, pairs)  7.23 us
  transfers between devices with their start and end apart: 23, of which 9 were waited for; matrix products, arithmetic and copies ran while one was open for 3% of the time, Pallas kernels for 0%

profile of v6, /device:TPU:1, one launch (start us, length us, event | category | flops | bytes accessed | tf_op | source)
XLA Modules:
  0.0 183.2 jit_solution(16806373101825013528)
XLA Ops:
  0.6 1.0 copy-done.2
  2.5 5.3 %collective-permute-start.5 = (bf16[128,1664]{1,0:T(8,128)(2,1)S(1)}, bf16[128,1664]{1,0:T(8,128)(2,1)S(1)}, u32[]{:S(2)}, u32[]{:S(2)}) collective-permute-start(bf16[128,1664]{1,0:T(8,128)(2,1)S(1)} %shard_map.77.refs_5_), channel_id=1, source_target_pairs={{0,3},{1,2},{2,1},{3,0},{4,7},{5,6},{6,5},{7,4},{8,11},{9,10},{10,... | collective-permute-start | bytes 1277960 | tf_op jit(solution)/shard_map/ppermute | solution.py:269
  7.8 2.5 %collective-permute-start.3 = (bf16[128,1664]{1,0:T(8,128)(2,1)S(1)}, bf16[128,1664]{1,0:T(8,128)(2,1)S(1)}, u32[]{:S(2)}, u32[]{:S(2)}) collective-permute-start(bf16[128,1664]{1,0:T(8,128)(2,1)S(1)} %shard_map.77.refs_5_), channel_id=1, source_target_pairs={{0,4},{1,5},{2,6},{3,7},{4,8},{5,9},{6,10},{7,11},{8,12},{9,13},{1... | collective-permute-start | bytes 1277960 | tf_op jit(solution)/shard_map/ppermute | solution.py:260
  10.3 2.7 %collective-permute-start.1 = (bf16[128,1664]{1,0:T(8,128)(2,1)S(1)}, bf16[128,1664]{1,0:T(8,128)(2,1)S(1)}, u32[]{:S(2)}, u32[]{:S(2)}) collective-permute-start(bf16[128,1664]{1,0:T(8,128)(2,1)S(1)} %shard_map.77.refs_5_), channel_id=1, source_target_pairs={{0,64},{1,65},{2,66},{3,67},{4,68},{5,69},{6,70},{7,71},{8,72},{9,... | collective-permute-start | bytes 1277960 | tf_op jit(solution)/shard_map/ppermute | solution.py:260
  13.7 0.7 dynamic-slice_bitcast_fusion
  15.1 1.3 collective-permute-done.5
  16.4 2.3 %collective-permute-start = (bf16[128,1664]{1,0:T(8,128)(2,1)S(1)}, bf16[128,1664]{1,0:T(8,128)(2,1)S(1)}, u32[]{:S(2)}, u32[]{:S(2)}) collective-permute-start(bf16[128,1664]{1,0:T(8,128)(2,1)S(1)} %shard_map.77.refs_5_), channel_id=1, source_target_pairs={{0,192},{1,193},{2,194},{3,195},{4,196},{5,197},{6,198},{7,199},{8... | collective-permute-start | bytes 1277960 | tf_op jit(solution)/shard_map/ppermute | solution.py:260
  18.7 0.8 slice_bitcast_fusion
  19.7 7.6 %collective-permute-done.4 = bf16[128,1664]{1,0:T(8,128)(2,1)S(1)} collective-permute-done((bf16[128,1664]{1,0:T(8,128)(2,1)S(1)}, bf16[128,1664]{1,0:T(8,128)(2,1)S(1)}, u32[]{:S(2)}, u32[]{:S(2)}) %collective-permute-start.4) | collective-permute-done | bytes 426016 | tf_op jit(solution)/shard_map/ppermute | solution.py:269
  27.3 5.4 %collective-permute-start.12 = (bf16[128,1664]{1,0:T(8,128)(2,1)S(1)}, bf16[128,1664]{1,0:T(8,128)(2,1)S(1)}, u32[]{:S(2)}, u32[]{:S(2)}) collective-permute-start(bf16[128,1664]{1,0:T(8,128)(2,1)S(1)} %shard_map.77.refs_5_), channel_id=1, source_target_pairs={{0,32},{1,33},{2,34},{3,35},{4,36},{5,37},{6,38},{7,39},{8,40},{9,... | collective-permute-start | bytes 1277960 | tf_op jit(solution)/shard_map/ppermute | solution.py:260
  32.8 2.6 %collective-permute-start.11 = (bf16[2,128,1664]{2,1,0:T(8,128)(2,1)S(1)}, bf16[2,128,1664]{2,1,0:T(8,128)(2,1)S(1)}, u32[]{:S(2)}, u32[]{:S(2)}) collective-permute-start(bf16[2,128,1664]{2,1,0:T(8,128)(2,1)S(1)} %pad_maximum_fusion.2.refs_9_), channel_id=1, source_target_pairs={{0,4},{1,5},{2,6},{3,7},{4,8},{5,9},{6,10},{7,11},{8,12},{9,13},{1... | collective-permute-start | bytes 2555912 | tf_op jit(solution)/shard_map/ppermute | solution.py:260
  35.4 2.7 %collective-permute-start.6 = (bf16[128,1664]{1,0:T(8,128)(2,1)S(1)}, bf16[128,1664]{1,0:T(8,128)(2,1)S(1)}, u32[]{:S(2)}, u32[]{:S(2)}) collective-permute-start(bf16[128,1664]{1,0:T(8,128)(2,1)S(1)} %collective-permute-done.1), channel_id=1, source_target_pairs={{0,64},{1,65},{2,66},{3,67},{4,68},{5,69},{6,70},{7,71},{8,72},{9,... | collective-permute-start | bytes 1277960 | tf_op jit(solution)/shard_map/ppermute | solution.py:260
  38.5 1.3 collective-permute-start.8
  39.8 4.8 %collective-permute-done.12.refs_18_ = bf16[128,1664]{1,0:T(8,128)(2,1)S(1)} collective-permute-done((bf16[128,1664]{1,0:T(8,128)(2,1)S(1)}, bf16[128,1664]{1,0:T(8,128)(2,1)S(1)}, u32[]{:S(2)}, u32[]{:S(2)}) %collective-permute-start.12) | collective-permute-done | bytes 426016 | tf_op jit(solution)/shard_map/ppermute | solution.py:260
  45.3 2.6 %collective-permute-start.7 = (bf16[128,1664]{1,0:T(8,128)(2,1)S(1)}, bf16[128,1664]{1,0:T(8,128)(2,1)S(1)}, u32[]{:S(2)}, u32[]{:S(2)}) collective-permute-start(bf16[128,1664]{1,0:T(8,128)(2,1)S(1)} %collective-permute-done.3.refs_6_), channel_id=1, source_target_pairs={{0,4},{1,5},{2,6},{3,7},{4,8},{5,9},{6,10},{7,11},{8,12},{9,13},{1... | collective-permute-start | bytes 1277960 | tf_op jit(solution)/shard_map/ppermute | solution.py:260
  48.4 10.3 %collective-permute-done.7.refs_7_ = bf16[128,1664]{1,0:T(8,128)(2,1)S(1)} collective-permute-done((bf16[128,1664]{1,0:T(8,128)(2,1)S(1)}, bf16[128,1664]{1,0:T(8,128)(2,1)S(1)}, u32[]{:S(2)}, u32[]{:S(2)}) %collective-permute-start.7) | collective-permute-done | bytes 426016 | tf_op jit(solution)/shard_map/ppermute | solution.py:260
  58.7 1.9 %collective-permute-done.8 = bf16[128,1664]{1,0:T(8,128)(2,1)S(1)} collective-permute-done((bf16[128,1664]{1,0:T(8,128)(2,1)S(1)}, bf16[128,1664]{1,0:T(8,128)(2,1)S(1)}, u32[]{:S(2)}, u32[]{:S(2)}) %collective-permute-start.8) | collective-permute-done | bytes 426016 | tf_op jit(solution)/shard_map/ppermute | solution.py:269
  60.7 2.6 %collective-permute-start.17 = (bf16[2,128,1664]{2,1,0:T(8,128)(2,1)S(1)}, bf16[2,128,1664]{2,1,0:T(8,128)(2,1)S(1)}, u32[]{:S(2)}, u32[]{:S(2)}) collective-permute-start(bf16[2,128,1664]{2,1,0:T(8,128)(2,1)S(1)} %collective-permute-done.11.refs_10_), channel_id=1, source_target_pairs={{0,4},{1,5},{2,6},{3,7},{4,8},{5,9},{6,10},{7,11},{8,12},{9,13},{1... | collective-permute-start | bytes 2555912 | tf_op jit(solution)/shard_map/ppermute | solution.py:260
  63.9 0.9 collective-permute-start.15
  64.9 2.1 %collective-permute-start.14 = (bf16[128,1664]{1,0:T(8,128)(2,1)S(1)}, bf16[128,1664]{1,0:T(8,128)(2,1)S(1)}, u32[]{:S(2)}, u32[]{:S(2)}) collective-permute-start(bf16[128,1664]{1,0:T(8,128)(2,1)S(1)} %collective-permute-done.12.refs_18_), channel_id=1, source_target_pairs={{0,64},{1,65},{2,66},{3,67},{4,68},{5,69},{6,70},{7,71},{8,72},{9,... | collective-permute-start | bytes 1277960 | tf_op jit(solution)/shard_map/ppermute | solution.py:260
  68.1 14.0 %collective-permute-done.16.refs_14_ = bf16[128,1664]{1,0:T(8,128)(2,1)S(1)} collective-permute-done((bf16[128,1664]{1,0:T(8,128)(2,1)S(1)}, bf16[128,1664]{1,0:T(8,128)(2,1)S(1)}, u32[]{:S(2)}, u32[]{:S(2)}) %collective-permute-start.16) | collective-permute-done | bytes 426016 | tf_op jit(solution)/shard_map/ppermute | solution.py:260
  82.1 3.5 %collective-permute-start.19 = (bf16[4,128,1664]{2,1,0:T(8,128)(2,1)S(1)}, bf16[4,128,1664]{2,1,0:T(8,128)(2,1)S(1)}, u32[]{:S(2)}, u32[]{:S(2)}) collective-permute-start(bf16[4,128,1664]{2,1,0:T(8,128)(2,1)S(1)} %pad_maximum_fusion.refs_17_), channel_id=1, source_target_pairs={{0,16},{1,17},{2,18},{3,19},{4,20},{5,21},{6,22},{7,23},{8,24},{9,... | collective-permute-start | bytes 5111816 | tf_op jit(solution)/shard_map/ppermute | solution.py:260
  86.1 2.5 %collective-permute-start.21 = (bf16[128,1664]{1,0:T(8,128)(2,1)S(1)}, bf16[128,1664]{1,0:T(8,128)(2,1)}, u32[]{:S(2)}, u32[]{:S(2)}) collective-permute-start(bf16[128,1664]{1,0:T(8,128)(2,1)S(1)} %collective-permute-done.14.refs_19_), channel_id=1, source_target_pairs={{0,64},{1,65},{2,66},{3,67},{4,68},{5,69},{6,70},{7,71},{8,72},{9,... | collective-permute-start | bytes 1277960 | tf_op jit(solution)/shard_map/ppermute | solution.py:260
  88.6 4.7 %collective-permute-done.20.refs_15_ = bf16[128,1664]{1,0:T(8,128)(2,1)S(1)} collective-permute-done((bf16[128,1664]{1,0:T(8,128)(2,1)S(1)}, bf16[128,1664]{1,0:T(8,128)(2,1)S(1)}, u32[]{:S(2)}, u32[]{:S(2)}) %collective-permute-start.20) | collective-permute-done | bytes 426016 | tf_op jit(solution)/shard_map/ppermute | solution.py:260
  93.7 1.3 copy-done.9
  95.0 2.4 %collective-permute-start.22 = (bf16[128,1664]{1,0:T(8,128)(2,1)}, bf16[128,1664]{1,0:T(8,128)(2,1)}, u32[]{:S(2)}, u32[]{:S(2)}) collective-permute-start(bf16[128,1664]{1,0:T(8,128)(2,1)} %collective-permute-done.21.refs_20_), channel_id=1, source_target_pairs={{0,16},{1,17},{2,18},{3,19},{4,20},{5,21},{6,22},{7,23},{8,24},{9,... | collective-permute-start | bytes 1277960 | tf_op jit(solution)/shard_map/ppermute | solution.py:260
  98.1 1.1 collective-permute-done.22.refs_24_
  99.1 10.5 %shard_map.78 = (f32[32,128,128]{2,1,0:T(8,128)}, f32[256,128]{1,0:T(8,128)}) custom-call(s32[2]{0:T(128)} %pad_add_fusion.1.refs_0_, s32[32,3]{1,0:T(8,128)} %copy.16.refs_1_, s32[4]{0:T(128)} %and_select_fusion.refs_2_, s32[16]{0:T(128)} %copy-done.24, s32[16]{0:T(128)} %copy-done.25, bf16[128,1664]{1,0:T(8,128)(2,1)} %copy-done, ...), custom_call_target="tpu_custom_call" | custom-call | tf_op jit(solution)/shard_map/pallas_call | solution.py:383
  109.7 26.7 %all_to_all.33 = f32[256,1,128]{2,1,0:T(1,128)S(1)} all-to-all(f32[256,1,128]{2,1,0:T(1,128)} %bitcast.53), channel_id=1, replica_groups=mesh['row'=16,'col'=16] {'row','col'}, dimensions={0} | all-to-all | bytes 262144 | tf_op jit(solution)/shard_map/all_to_all | solution.py:239
  136.7 21.5 %all_to_all.34 = f32[256,1,256]{2,1,0:T(1,128)S(1)} all-to-all(f32[256,1,256]{2,1,0:T(1,128)S(1)} %copy.15), channel_id=1, replica_groups=mesh['row'=16,'col'=16] {'row','col'}, dimensions={0} | all-to-all | bytes 524288 | tf_op jit(solution)/shard_map/all_to_all | solution.py:239
  158.2 2.8 %shard_map.80 = (f32[256,256]{1,0:T(8,128)S(1)}, f32[8,128]{1,0:T(8,128)S(1)}) custom-call(s32[2]{0:T(128)S(1)} %copy-done.6, s32[32,3]{1,0:T(8,128)S(1)} %copy-done.3, f32[32,128,128]{2,1,0:T(8,128)S(1)} %copy-done.1, f32[256,256]{1,0:T(8,128)S(1)} %bitcast.40), custom_call_target="tpu_custom_call" | custom-call | tf_op jit(solution)/shard_map/pallas_call | solution.py:412
  161.3 21.3 %all_to_all.35 = f32[256,1,256]{2,1,0:T(1,128)S(1)} all-to-all(f32[256,1,256]{2,1,0:T(1,128)S(1)} %copy.17), channel_id=1, replica_groups=mesh['row'=16,'col'=16] {'row','col'}, dimensions={0} | all-to-all | bytes 524288 | tf_op jit(solution)/shard_map/all_to_all | solution.py:239
  (97 shorter events, 8.1 us)
Async XLA Ops:
  2.5 65.5 %copy-start = (bf16[128,1664]{1,0:T(8,128)(2,1)}, bf16[128,1664]{1,0:T(8,128)(2,1)S(1)}, u32[]{:S(2)}) copy-start(bf16[128,1664]{1,0:T(8,128)(2,1)S(1)} %shard_map.77.refs_5_) | copy-start | bytes 1277956
  2.5 13.9 %collective-permute-start.5 = (bf16[128,1664]{1,0:T(8,128)(2,1)S(1)}, bf16[128,1664]{1,0:T(8,128)(2,1)S(1)}, u32[]{:S(2)}, u32[]{:S(2)}) collective-permute-start(bf16[128,1664]{1,0:T(8,128)(2,1)S(1)} %shard_map.77.refs_5_), channel_id=1, source_target_pairs={{0,3},{1,2},{2,1},{3,0},{4,7},{5,6},{6,5},{7,4},{8,11},{9,10},{10,... | collective-permute-start | bytes 1277960 | tf_op jit(solution)/shard_map/ppermute | solution.py:269
  7.8 19.5 %collective-permute-start.4 = (bf16[128,1664]{1,0:T(8,128)(2,1)S(1)}, bf16[128,1664]{1,0:T(8,128)(2,1)S(1)}, u32[]{:S(2)}, u32[]{:S(2)}) collective-permute-start(bf16[128,1664]{1,0:T(8,128)(2,1)S(1)} %shard_map.77.refs_5_), channel_id=1, source_target_pairs={{0,1},{1,0},{2,3},{3,2},{4,5},{5,4},{6,7},{7,6},{8,9},{9,8},{10,11... | collective-permute-start | bytes 1277960 | tf_op jit(solution)/shard_map/ppermute | solution.py:269
  7.8 24.9 %collective-permute-start.3 = (bf16[128,1664]{1,0:T(8,128)(2,1)S(1)}, bf16[128,1664]{1,0:T(8,128)(2,1)S(1)}, u32[]{:S(2)}, u32[]{:S(2)}) collective-permute-start(bf16[128,1664]{1,0:T(8,128)(2,1)S(1)} %shard_map.77.refs_5_), channel_id=1, source_target_pairs={{0,4},{1,5},{2,6},{3,7},{4,8},{5,9},{6,10},{7,11},{8,12},{9,13},{1... | collective-permute-start | bytes 1277960 | tf_op jit(solution)/shard_map/ppermute | solution.py:260
  10.3 22.4 %collective-permute-start.2 = (bf16[128,1664]{1,0:T(8,128)(2,1)S(1)}, bf16[128,1664]{1,0:T(8,128)(2,1)S(1)}, u32[]{:S(2)}, u32[]{:S(2)}) collective-permute-start(bf16[128,1664]{1,0:T(8,128)(2,1)S(1)} %shard_map.77.refs_5_), channel_id=1, source_target_pairs={{0,12},{1,13},{2,14},{3,15},{4,0},{5,1},{6,2},{7,3},{8,4},{9,5},{1... | collective-permute-start | bytes 1277960 | tf_op jit(solution)/shard_map/ppermute | solution.py:260
  10.3 22.4 %collective-permute-start.1 = (bf16[128,1664]{1,0:T(8,128)(2,1)S(1)}, bf16[128,1664]{1,0:T(8,128)(2,1)S(1)}, u32[]{:S(2)}, u32[]{:S(2)}) collective-permute-start(bf16[128,1664]{1,0:T(8,128)(2,1)S(1)} %shard_map.77.refs_5_), channel_id=1, source_target_pairs={{0,64},{1,65},{2,66},{3,67},{4,68},{5,69},{6,70},{7,71},{8,72},{9,... | collective-permute-start | bytes 1277960 | tf_op jit(solution)/shard_map/ppermute | solution.py:260
  14.4 53.6 %copy-start.24 = (s32[16]{0:T(128)}, s32[16]{0:T(128)S(1)}, u32[]{:S(2)}) copy-start(s32[16]{0:T(128)S(1)} %get-tuple-element.49.refs_3_) | copy-start | bytes 196
  14.4 53.6 %copy-start.25 = (s32[16]{0:T(128)}, s32[16]{0:T(128)S(1)}, u32[]{:S(2)}) copy-start(s32[16]{0:T(128)S(1)} %get-tuple-element.50.refs_4_) | copy-start | bytes 196
  16.4 16.3 %collective-permute-start = (bf16[128,1664]{1,0:T(8,128)(2,1)S(1)}, bf16[128,1664]{1,0:T(8,128)(2,1)S(1)}, u32[]{:S(2)}, u32[]{:S(2)}) collective-permute-start(bf16[128,1664]{1,0:T(8,128)(2,1)S(1)} %shard_map.77.refs_5_), channel_id=1, source_target_pairs={{0,192},{1,193},{2,194},{3,195},{4,196},{5,197},{6,198},{7,199},{8... | collective-permute-start | bytes 1277960 | tf_op jit(solution)/shard_map/ppermute | solution.py:260
  27.3 17.3 %collective-permute-start.12 = (bf16[128,1664]{1,0:T(8,128)(2,1)S(1)}, bf16[128,1664]{1,0:T(8,128)(2,1)S(1)}, u32[]{:S(2)}, u32[]{:S(2)}) collective-permute-start(bf16[128,1664]{1,0:T(8,128)(2,1)S(1)} %shard_map.77.refs_5_), channel_id=1, source_target_pairs={{0,32},{1,33},{2,34},{3,35},{4,36},{5,37},{6,38},{7,39},{8,40},{9,... | collective-permute-start | bytes 1277960 | tf_op jit(solution)/shard_map/ppermute | solution.py:260
  32.8 35.2 %copy-start.8 = (bf16[2,128,1664]{2,1,0:T(8,128)(2,1)}, bf16[2,128,1664]{2,1,0:T(8,128)(2,1)S(1)}, u32[]{:S(2)}) copy-start(bf16[2,128,1664]{2,1,0:T(8,128)(2,1)S(1)} %pad_maximum_fusion.2.refs_9_) | copy-start | bytes 2555908
  32.8 27.8 %collective-permute-start.11 = (bf16[2,128,1664]{2,1,0:T(8,128)(2,1)S(1)}, bf16[2,128,1664]{2,1,0:T(8,128)(2,1)S(1)}, u32[]{:S(2)}, u32[]{:S(2)}) collective-permute-start(bf16[2,128,1664]{2,1,0:T(8,128)(2,1)S(1)} %pad_maximum_fusion.2.refs_9_), channel_id=1, source_target_pairs={{0,4},{1,5},{2,6},{3,7},{4,8},{5,9},{6,10},{7,11},{8,12},{9,13},{1... | collective-permute-start | bytes 2555912 | tf_op jit(solution)/shard_map/ppermute | solution.py:260
  35.4 25.3 %collective-permute-start.10 = (bf16[2,128,1664]{2,1,0:T(8,128)(2,1)S(1)}, bf16[2,128,1664]{2,1,0:T(8,128)(2,1)S(1)}, u32[]{:S(2)}, u32[]{:S(2)}) collective-permute-start(bf16[2,128,1664]{2,1,0:T(8,128)(2,1)S(1)} %pad_maximum_fusion.2.refs_9_), channel_id=1, source_target_pairs={{0,12},{1,13},{2,14},{3,15},{4,0},{5,1},{6,2},{7,3},{8,4},{9,5},{1... | collective-permute-start | bytes 2555912 | tf_op jit(solution)/shard_map/ppermute | solution.py:260
  35.4 9.9 %collective-permute-start.6 = (bf16[128,1664]{1,0:T(8,128)(2,1)S(1)}, bf16[128,1664]{1,0:T(8,128)(2,1)S(1)}, u32[]{:S(2)}, u32[]{:S(2)}) collective-permute-start(bf16[128,1664]{1,0:T(8,128)(2,1)S(1)} %collective-permute-done.1), channel_id=1, source_target_pairs={{0,64},{1,65},{2,66},{3,67},{4,68},{5,69},{6,70},{7,71},{8,72},{9,... | collective-permute-start | bytes 1277960 | tf_op jit(solution)/shard_map/ppermute | solution.py:260
  38.5 22.2 %collective-permute-start.8 = (bf16[128,1664]{1,0:T(8,128)(2,1)S(1)}, bf16[128,1664]{1,0:T(8,128)(2,1)S(1)}, u32[]{:S(2)}, u32[]{:S(2)}) collective-permute-start(bf16[128,1664]{1,0:T(8,128)(2,1)S(1)} %collective-permute-done.5), channel_id=1, source_target_pairs={{1,0},{2,3},{5,4},{6,7},{9,8},{10,11},{13,12},{14,15},{17,16},{18,... | collective-permute-start | bytes 1277960 | tf_op jit(solution)/shard_map/ppermute | solution.py:269
  44.6 41.0 %copy-start.10 = (bf16[128,1664]{1,0:T(8,128)(2,1)}, bf16[128,1664]{1,0:T(8,128)(2,1)S(1)}, u32[]{:S(2)}) copy-start(bf16[128,1664]{1,0:T(8,128)(2,1)S(1)} %collective-permute-done.12.refs_18_) | copy-start | bytes 1277956
  44.6 16.1 %collective-permute-start.9 = (bf16[128,1664]{1,0:T(8,128)(2,1)S(1)}, bf16[128,1664]{1,0:T(8,128)(2,1)S(1)}, u32[]{:S(2)}, u32[]{:S(2)}) collective-permute-start(bf16[128,1664]{1,0:T(8,128)(2,1)S(1)} %collective-permute-done.4), channel_id=1, source_target_pairs={{1,2},{2,1},{5,6},{6,5},{9,10},{10,9},{13,14},{14,13},{17,18},{18,... | collective-permute-start | bytes 1277960 | tf_op jit(solution)/shard_map/ppermute | solution.py:269
  45.3 13.4 %collective-permute-start.7 = (bf16[128,1664]{1,0:T(8,128)(2,1)S(1)}, bf16[128,1664]{1,0:T(8,128)(2,1)S(1)}, u32[]{:S(2)}, u32[]{:S(2)}) collective-permute-start(bf16[128,1664]{1,0:T(8,128)(2,1)S(1)} %collective-permute-done.3.refs_6_), channel_id=1, source_target_pairs={{0,4},{1,5},{2,6},{3,7},{4,8},{5,9},{6,10},{7,11},{8,12},{9,13},{1... | collective-permute-start | bytes 1277960 | tf_op jit(solution)/shard_map/ppermute | solution.py:260
  60.7 21.4 %collective-permute-start.17 = (bf16[2,128,1664]{2,1,0:T(8,128)(2,1)S(1)}, bf16[2,128,1664]{2,1,0:T(8,128)(2,1)S(1)}, u32[]{:S(2)}, u32[]{:S(2)}) collective-permute-start(bf16[2,128,1664]{2,1,0:T(8,128)(2,1)S(1)} %collective-permute-done.11.refs_10_), channel_id=1, source_target_pairs={{0,4},{1,5},{2,6},{3,7},{4,8},{5,9},{6,10},{7,11},{8,12},{9,13},{1... | collective-permute-start | bytes 2555912 | tf_op jit(solution)/shard_map/ppermute | solution.py:260
  63.3 18.7 %collective-permute-start.16 = (bf16[128,1664]{1,0:T(8,128)(2,1)S(1)}, bf16[128,1664]{1,0:T(8,128)(2,1)S(1)}, u32[]{:S(2)}, u32[]{:S(2)}) collective-permute-start(bf16[128,1664]{1,0:T(8,128)(2,1)S(1)} %broadcast_select_fusion.refs_13_), channel_id=1, source_target_pairs={{0,4},{1,5},{2,6},{3,7},{4,8},{5,9},{6,10},{7,11},{8,12},{9,13},{1... | collective-permute-start | bytes 1277960 | tf_op jit(solution)/shard_map/ppermute | solution.py:260
  63.9 18.1 %collective-permute-start.15 = (bf16[128,1664]{1,0:T(8,128)(2,1)S(1)}, bf16[128,1664]{1,0:T(8,128)(2,1)S(1)}, u32[]{:S(2)}, u32[]{:S(2)}) collective-permute-start(bf16[128,1664]{1,0:T(8,128)(2,1)S(1)} %broadcast_select_fusion.refs_13_), channel_id=1, source_target_pairs={{0,12},{1,13},{2,14},{3,15},{4,0},{5,1},{6,2},{7,3},{8,4},{9,5},{1... | collective-permute-start | bytes 1277960 | tf_op jit(solution)/shard_map/ppermute | solution.py:260
  64.9 17.2 %collective-permute-start.14 = (bf16[128,1664]{1,0:T(8,128)(2,1)S(1)}, bf16[128,1664]{1,0:T(8,128)(2,1)S(1)}, u32[]{:S(2)}, u32[]{:S(2)}) collective-permute-start(bf16[128,1664]{1,0:T(8,128)(2,1)S(1)} %collective-permute-done.12.refs_18_), channel_id=1, source_target_pairs={{0,64},{1,65},{2,66},{3,67},{4,68},{5,69},{6,70},{7,71},{8,72},{9,... | collective-permute-start | bytes 1277960 | tf_op jit(solution)/shard_map/ppermute | solution.py:260
  66.9 15.1 %collective-permute-start.13 = (bf16[128,1664]{1,0:T(8,128)(2,1)S(1)}, bf16[128,1664]{1,0:T(8,128)(2,1)S(1)}, u32[]{:S(2)}, u32[]{:S(2)}) collective-permute-start(bf16[128,1664]{1,0:T(8,128)(2,1)S(1)} %collective-permute-done.12.refs_18_), channel_id=1, source_target_pairs={{0,192},{1,193},{2,194},{3,195},{4,196},{5,197},{6,198},{7,199},{8... | collective-permute-start | bytes 1277960 | tf_op jit(solution)/shard_map/ppermute | solution.py:260
  82.1 11.6 %collective-permute-start.19 = (bf16[4,128,1664]{2,1,0:T(8,128)(2,1)S(1)}, bf16[4,128,1664]{2,1,0:T(8,128)(2,1)S(1)}, u32[]{:S(2)}, u32[]{:S(2)}) collective-permute-start(bf16[4,128,1664]{2,1,0:T(8,128)(2,1)S(1)} %pad_maximum_fusion.refs_17_), channel_id=1, source_target_pairs={{0,16},{1,17},{2,18},{3,19},{4,20},{5,21},{6,22},{7,23},{8,24},{9,... | collective-permute-start | bytes 5111816 | tf_op jit(solution)/shard_map/ppermute | solution.py:260
  85.7 7.9 %collective-permute-start.18 = (bf16[3,128,1664]{2,1,0:T(8,128)(2,1)S(1)}, bf16[3,128,1664]{2,1,0:T(8,128)(2,1)S(1)}, u32[]{:S(2)}, u32[]{:S(2)}) collective-permute-start(bf16[3,128,1664]{2,1,0:T(8,128)(2,1)S(1)} %pad_maximum_fusion.1), channel_id=1, source_target_pairs={{0,16},{1,17},{2,18},{3,19},{4,20},{5,21},{6,22},{7,23},{8,24},{9,... | collective-permute-start | bytes 3833864 | tf_op jit(solution)/shard_map/ppermute | solution.py:260
  85.8 7.4 %collective-permute-start.20 = (bf16[128,1664]{1,0:T(8,128)(2,1)S(1)}, bf16[128,1664]{1,0:T(8,128)(2,1)S(1)}, u32[]{:S(2)}, u32[]{:S(2)}) collective-permute-start(bf16[128,1664]{1,0:T(8,128)(2,1)S(1)} %collective-permute-done.16.refs_14_), channel_id=1, source_target_pairs={{0,4},{1,5},{2,6},{3,7},{4,8},{5,9},{6,10},{7,11},{8,12},{9,13},{1... | collective-permute-start | bytes 1277960 | tf_op jit(solution)/shard_map/ppermute | solution.py:260
  86.1 7.6 %collective-permute-start.21 = (bf16[128,1664]{1,0:T(8,128)(2,1)S(1)}, bf16[128,1664]{1,0:T(8,128)(2,1)}, u32[]{:S(2)}, u32[]{:S(2)}) collective-permute-start(bf16[128,1664]{1,0:T(8,128)(2,1)S(1)} %collective-permute-done.14.refs_19_), channel_id=1, source_target_pairs={{0,64},{1,65},{2,66},{3,67},{4,68},{5,69},{6,70},{7,71},{8,72},{9,... | collective-permute-start | bytes 1277960 | tf_op jit(solution)/shard_map/ppermute | solution.py:260
  95.0 4.1 %collective-permute-start.22 = (bf16[128,1664]{1,0:T(8,128)(2,1)}, bf16[128,1664]{1,0:T(8,128)(2,1)}, u32[]{:S(2)}, u32[]{:S(2)}) collective-permute-start(bf16[128,1664]{1,0:T(8,128)(2,1)} %collective-permute-done.21.refs_20_), channel_id=1, source_target_pairs={{0,16},{1,17},{2,18},{3,19},{4,20},{5,21},{6,22},{7,23},{8,24},{9,... | collective-permute-start | bytes 1277960 | tf_op jit(solution)/shard_map/ppermute | solution.py:260
  98.1 38.3 %copy-start.5 = (f32[128]{0:T(128)S(1)}, f32[128]{0:T(128)}, u32[]{:S(2)}) copy-start(f32[128]{0:T(128)} %param.7) | copy-start | bytes 1540
  109.6 48.5 %copy-start.1 = (f32[32,128,128]{2,1,0:T(8,128)S(1)}, f32[32,128,128]{2,1,0:T(8,128)}, u32[]{:S(2)}) copy-start(f32[32,128,128]{2,1,0:T(8,128)} %get-tuple-element.64.refs_2_) | copy-start | bytes 6291460
  109.6 48.5 %copy-start.3 = (s32[32,3]{1,0:T(8,128)S(1)}, s32[32,3]{1,0:T(8,128)}, u32[]{:S(2)}) copy-start(s32[32,3]{1,0:T(8,128)} %copy.16.refs_1_) | copy-start | bytes 1156
  109.6 48.5 %copy-start.6 = (s32[2]{0:T(128)S(1)}, s32[2]{0:T(128)}, u32[]{:S(2)}) copy-start(s32[2]{0:T(128)} %pad_add_fusion.1.refs_0_) | copy-start | bytes 28
  (17 other events, 194.7 us)
